TPU v7x, 32 devices: a whole 2x2x4 slice. The times are simulated.
32 devices in a mesh: basin: 8 (over y, x, core), tm: 4 (over z).
Axes of the slice: x: 2, y: 2, z: 4, core: 2. Of those that a mesh axis runs over, the one named last changes fastest.
Arguments:
- inflow: float32 [128, 32768], P('tm', 'basin'), may hold values from 0.01 to 0.1
- cotangent: float32 [128, 16384], P('tm', 'basin'), may hold values from -6 to 6
- gauge_reach: int32 [16384], P('basin'), may hold values from 0 to 4095
- shape_param: float32 [32768], P('basin'), may hold values from 1.5 to 4
- scale_param: float32 [32768], P('basin'), may hold values from 1.5 to 10
- block_level: int32 [128], P('basin'), may hold values from 0 to 7, as said below
- down_local: int32 [32768], P('basin'), may hold values from -1 to 4095, as said below
- in_slot: int32 [32768], P('basin'), may hold values from -1 to 31, as said below
- send_reach: int32 [8, 7, 32], P('basin'), may hold values from -1 to 4095, as said below
Outputs:
- lateral_grad: float32 [128, 32768], P('tm', 'basin')
- param_grad: float32 [2, 32768], P(None, 'basin')
Inputs may be any that keep to these rules, and one draw needn't show every extreme that they name: `block_level`: every partition holds between one and 4 blocks of each level, and exactly 4 blocks of some level. `down_local`: for a reach in a block of level h >= 1 whose in_slot is -1: a reach of the same partition in a block of level h - 1. -1 for reaches of level 0 and for reaches with in_slot >= 0. `in_slot`: A value s * 4 + c (s a partition other than the reach's own, c < 4) marks a reach of level h >= 1 fed by slot c that partition s fills for it at level h - 1; within one partition no value repeats among the reaches of one level. Exactly the slots that send_reach fills are received. send_reach[s, h, t * 4 + c] is a reach of partition s in a block of level h, or -1 for an empty slot; slots with t = s are empty. At some level some partition t receives all 4 slots from every other partition.
All inputs are finite; a program needn't handle non-finite values.
Results may differ from a plain program's by a relative error of at most 0.0003.
Values sent between devices are 32-bit elements; how exact they have to be, the bound alone decides.
No kernel may reach another device: no remote copies, remote signals or barrier semaphores. Data moves between devices by JAX's collectives and lax.ppermute only.
A program may use at most 128 MiB of HBM per device.

v0:
```python
import functools

import jax
import jax.numpy as jnp
from jax import lax
from jax.experimental import pallas as pl
from jax.experimental.pallas import tpu as pltpu
from jax.sharding import PartitionSpec as P

BLK = 256
LAGS = 30
LEVELS = 8
MAXB = 4
LANES = 128
KROWS = 32
SENDS = LEVELS - 1
F32 = jnp.float32
BF16 = jnp.bfloat16
VMEM_LIMIT = 56 * 1024 * 1024


def iota(shape, axis):
    return lax.broadcasted_iota(jnp.int32, shape, axis)


def split_terms(values):
    high = values.astype(BF16)
    return high, (values - high.astype(F32)).astype(BF16)


def one_hot(hits):
    return jnp.where(hits, 1.0, 0.0).astype(BF16)


def product(left, right):
    return jnp.dot(left, right, preferred_element_type=F32)


def list_blocks(level_ref, order_ref, count_ref):
    for height in range(LEVELS):
        count_ref[height] = 0

    @pl.loop(0, level_ref.shape[0])
    def _(block):
        height = level_ref[block]
        rank = count_ref[height]
        order_ref[height * MAXB + rank] = block
        count_ref[height] = rank + 1


def lag_weights(shape_row, scale_row):
    rows = iota((KROWS, shape_row.shape[1]), 0)
    offsets = rows.astype(F32) + 0.5
    logs = jnp.log(offsets)
    weights = jnp.exp((shape_row - 1.0) * logs - offsets / scale_row)
    weights = jnp.where(rows < LAGS, weights, 0.0)
    return weights / jnp.sum(weights, axis=0, keepdims=True), offsets, logs


def lag_sum(buf, chunk, weight_of, days, lags=LAGS):
    total = jnp.zeros((days, LANES), F32)
    for shift in range(8):
        steps = [k for k in range(shift, lags, 8)]
        shifted = buf[chunk, pl.ds(shift, days + 8 * (len(steps) - 1)), :]
        for step, lag in enumerate(steps):
            total = total + weight_of(lag) * shifted[8 * step : 8 * step + days]
    return total


def lag_sum_forward(buf, chunk, weights_of, days):
    totals = [jnp.zeros((days, LANES), F32) for _ in weights_of]
    for shift in range(8):
        shifted = buf[chunk, pl.ds(8 - shift, days + 24), :]
        for step in range(4):
            lag = 8 * step + shift
            if lag < LAGS:
                part = shifted[24 - 8 * step : 24 - 8 * step + days]
                totals = [t + w(lag) * part for t, w in zip(totals, weights_of)]
    return totals


def path_kernel(
    days, level_ref, part_ref, table_ref, want_ref, want_level_ref, node_ref, weight_ref, comp_ref,
    order_ref, count_ref, term_ref, buf_ref,
):
    list_blocks(level_ref, order_ref, count_ref)
    me = part_ref[0]
    width = want_ref.shape[1]
    want = want_ref[...]
    want_level = want_level_ref[...]
    below = jnp.full((1, width), -1, jnp.int32)
    parent = jnp.full((1, width), -1, jnp.int32)
    rows = iota((BLK, width), 0)
    krows = iota((KROWS, width), 0)
    node_ref[...] = jnp.full(node_ref.shape, -1, jnp.int32)
    for height in range(SENDS - 1, -1, -1):
        node = jnp.where((want_level == height) & (want >= 0), want, below)

        def gather(index, total, node=node, height=height):
            block = order_ref[height * MAXB + index]
            hits = jnp.where(rows == node - block * BLK, 1.0, 0.0)
            return total + jnp.dot(
                table_ref[block], hits, precision=lax.Precision.HIGHEST, preferred_element_type=F32
            )

        found = lax.fori_loop(0, count_ref[height], gather, jnp.zeros((8, width), F32))
        active = node >= 0
        down = jnp.round(found[0:1]).astype(jnp.int32)
        slot = jnp.round(found[1:2]).astype(jnp.int32)
        shape_row = jnp.where(active, found[2:3], 2.0)
        scale_row = jnp.where(active, found[3:4], 2.0)
        ends = active & (slot >= 0)
        below = jnp.where(active & (down >= 0), down, -1)
        sender = slot >> 2
        lane = (sender >> 2) * LANES + ((sender + (height - 1)) & 3) * KROWS + me * 4 + (slot & 3)
        parent = jnp.where(ends, (height - 1) * width + lane, parent)
        weights = lag_weights(shape_row, scale_row)[0]
        weights = jnp.where(active, weights, jnp.where(krows == 0, 1.0, 0.0))
        node_ref[height : height + 1, :] = node
        term_ref[height : height + 1, :] = jnp.where(ends, 1.0, 0.0)
        for chunk in range(width // LANES):
            weight_ref[height, chunk] = weights[:, chunk * LANES : (chunk + 1) * LANES]
    buf_ref[...] = jnp.zeros(buf_ref.shape, F32)
    first = iota((8, LANES), 0) == 0
    for height in range(1, SENDS):
        for chunk in range(width // LANES):
            ends = term_ref[height : height + 1, chunk * LANES : (chunk + 1) * LANES] > 0.5
            start = buf_ref[chunk, KROWS : KROWS + 8, :]
            buf_ref[chunk, KROWS : KROWS + 8, :] = jnp.where(first & ends, 1.0, start)

        @pl.loop(0, width // LANES)
        def _(chunk, height=height):
            row = lambda lag: weight_ref[height, chunk, pl.ds(lag, 1), :]
            (total,) = lag_sum_forward(buf_ref, chunk, [row], days)
            buf_ref[chunk, KROWS : KROWS + days, :] = total

    for chunk in range(width // LANES):
        lanes = slice(chunk * LANES, (chunk + 1) * LANES)
        comp_ref[0:days, lanes] = buf_ref[chunk, KROWS : KROWS + days, :]
    comp_ref[days : days + 8, :] = jnp.broadcast_to(parent.astype(F32), (8, width))


def weights_kernel(
    shape_ref, scale_ref, inflow_ref, earlier_ref, weight_ref, grad_ref, buf_ref, two_ref
):
    days = inflow_ref.shape[0]

    @pl.loop(0, shape_ref.shape[0])
    def _(block):
        scale_row = scale_ref[block]
        weights, offsets, logs = lag_weights(shape_ref[block], scale_row)
        by_shape = weights * (logs - jnp.sum(weights * logs, axis=0, keepdims=True))
        by_scale = weights * (offsets - jnp.sum(weights * offsets, axis=0, keepdims=True))
        by_scale = by_scale / (scale_row * scale_row)
        start = pl.multiple_of(block * BLK, BLK)
        for chunk in range(2):
            lanes = slice(chunk * LANES, (chunk + 1) * LANES)
            weight_ref[block, chunk] = weights[:, lanes]
            two_ref[chunk, 0] = by_shape[:, lanes]
            two_ref[chunk, 1] = by_scale[:, lanes]
            at = pl.ds(pl.multiple_of(start + chunk * LANES, LANES), LANES)
            buf_ref[chunk, 0:days, :] = earlier_ref[:, at]
            buf_ref[chunk, days : 2 * days, :] = inflow_ref[:, at]
        for chunk in range(2):
            rows = [
                lambda lag, chunk=chunk, which=which: two_ref[chunk, which, pl.ds(lag, 1), :]
                for which in range(2)
            ]
            first, second = lag_sum_forward(buf_ref, chunk, rows, days)
            lanes = slice(chunk * LANES, (chunk + 1) * LANES)
            grad_ref[block, 0, :, lanes] = first
            grad_ref[block, 1, :, lanes] = second


def gather_terms(pieces, terms_ref):
    shard_days = pieces[0].shape[0]
    days = shard_days * len(pieces)
    for number, piece in enumerate(pieces):
        high, low = split_terms(piece[...])
        terms_ref[number * shard_days : (number + 1) * shard_days, :] = high
        terms_ref[days + number * shard_days : days + (number + 1) * shard_days, :] = low


def gauge_product(terms_ref, gauge_ref, targets):
    gauges = gauge_ref.shape[0]
    total = jnp.zeros((terms_ref.shape[0], BLK), F32)
    for start in range(0, gauges, BLK):
        ids = gauge_ref[start : start + BLK, :]
        hits = jnp.concatenate(
            [one_hot(ids == targets[:, c * LANES : (c + 1) * LANES]) for c in range(2)], axis=1
        )
        total = total + product(terms_ref[:, start : start + BLK], hits)
    days = terms_ref.shape[0] // 2
    return total[:days] + total[days:]


def path_adjoint_kernel(shards, *refs):
    pieces = refs[:shards]
    gauge_ref, node_ref, weight_ref, out_ref, terms_ref, seed_ref, buf_ref = refs[shards:]
    days = out_ref.shape[0]
    gather_terms(pieces, terms_ref)

    @pl.loop(0, SENDS)
    def _(height):
        seeds = gauge_product(terms_ref, gauge_ref, node_ref[pl.ds(height, 1), :])
        for chunk in range(2):
            seed_ref[height, chunk] = seeds[:, chunk * LANES : (chunk + 1) * LANES]

    for chunk in range(2):
        buf_ref[chunk] = jnp.zeros(buf_ref.shape[1:], F32)

        @pl.loop(0, SENDS)
        def _(height, chunk=chunk):
            buf_ref[chunk, 0:days, :] = buf_ref[chunk, 0:days, :] + seed_ref[height, chunk]
            row = lambda lag: weight_ref[height, chunk, pl.ds(lag, 1), :]
            buf_ref[chunk, 0:days, :] = lag_sum(buf_ref, chunk, row, days)

        out_ref[:, chunk * LANES : (chunk + 1) * LANES] = buf_ref[chunk, 0:days, :]


def seed_kernel(shards, *refs):
    pieces = refs[:shards]
    gauge_ref, out_ref, terms_ref = refs[shards:]
    gather_terms(pieces, terms_ref)

    @pl.loop(0, out_ref.shape[0])
    def _(block):
        targets = iota((1, BLK), 1) + block * BLK
        out_ref[block] = gauge_product(terms_ref, gauge_ref, targets)


def full_kernel(
    own_days, level_ref, part_ref, a_own_ref, a_mate_ref, c_own_ref, c_mate_ref, seed_ref, weight_ref,
    grad_ref, down_ref, slot_ref, out_ref, param_ref,
    order_ref, count_ref, recv_ref, comp_ref, parent_buf, adj_ref, lat_ref,
):
    list_blocks(level_ref, order_ref, count_ref)
    me = part_ref[0]
    flip = (me >> 2) * LANES
    days = seed_ref.shape[1]
    width = 2 * LANES
    groups = iota((1, LANES), 1) >> 5
    rows = iota((BLK, width), 0)

    def merged(own_ref, mate_ref, height, half, at):
        lanes = slice((height // 4) * LANES, (height // 4 + 1) * LANES)
        total = None
        for ref, core in ((own_ref, 0), (mate_ref, 1)):
            for index in (2 * half, 2 * half + 1):
                sender = me ^ (core + 2 * index)
                part = ref[index, at, lanes]
                mine = groups == ((height + sender) & 3)
                total = part if total is None else jnp.where(mine, part, total)
        return total

    parent_buf[...] = jnp.zeros(parent_buf.shape, F32)
    for height in range(SENDS):
        if height:
            parents = jnp.concatenate(
                [
                    merged(c_own_ref, c_mate_ref, height, half, slice(days, days + 8))[0:1]
                    for half in range(2)
                ],
                axis=1,
            )
            parents = jnp.round(parents).astype(jnp.int32)
            parents = jnp.where(parents >= 0, parents ^ flip, -1)
            total = jnp.zeros((2 * days, width), F32)
            for lower in range(height):
                hits = one_hot(rows == parents - lower * width)
                total = total + product(recv_ref[lower], hits)
            total = total[:days] + total[days:]
            for half in range(2):
                parent_buf[half, 0:days, :] = total[:, half * LANES : (half + 1) * LANES]
                comp_ref[half] = merged(c_own_ref, c_mate_ref, height, half, slice(0, days))
        lags = min(days, (LAGS - 1) * height + 1)
        for half in range(2):
            result = merged(a_own_ref, a_mate_ref, height, half, slice(0, days))
            if height:
                tiles = [result[8 * i : 8 * i + 8] for i in range(days // 8)]
                for shift in range(8):
                    steps = [k for k in range(shift, lags, 8)]
                    for step, lag in enumerate(steps):
                        weight = comp_ref[half, lag : lag + 1, :]
                        for i in range(days // 8 - step):
                            at = 8 * (i + step) + shift
                            tiles[i] = tiles[i] + weight * parent_buf[half, at : at + 8, :]
                result = jnp.concatenate(tiles, axis=0)
            high, low = split_terms(result)
            lanes = slice(half * LANES, (half + 1) * LANES)
            recv_ref[height, 0:days, lanes] = high
            recv_ref[height, days : 2 * days, lanes] = low

    def days_of(height):
        return min(days, -(-(own_days + (LAGS - 1) * (LEVELS - 1 - height)) // 16) * 16)

    adj_ref[...] = jnp.zeros(adj_ref.shape, F32)
    for height in range(LEVELS):
        need = days_of(height)
        have = days_of(height - 1) if height else days

        @pl.loop(0, count_ref[height])
        def _(rank, height=height, need=need, have=have):
            block = order_ref[height * MAXB + rank]
            adjoint = seed_ref[block, 0:have, :]
            if height:
                slot = slot_ref[block]
                sender = slot >> 2
                lane = ((sender >> 2) * LANES ^ flip) + ((sender + (height - 1)) & 3) * KROWS
                lane = jnp.where(slot >= 0, lane + me * 4 + (slot & 3), -1)
                hits = one_hot(rows == lane)
                if have == days:
                    total = product(recv_ref[height - 1], hits)
                else:
                    total = jnp.concatenate(
                        [
                            product(recv_ref[height - 1, 0:have, :], hits),
                            product(recv_ref[height - 1, days : days + have, :], hits),
                        ],
                        axis=0,
                    )
                down = down_ref[block]

                def gather(index, total):
                    source = order_ref[(height - 1) * MAXB + index]
                    hits = one_hot(rows == down - source * BLK)
                    return total + product(lat_ref[source, 0 : 2 * have, :], hits)

                total = lax.fori_loop(0, count_ref[height - 1], gather, total)
                adjoint = adjoint + total[:have] + total[have:]
            at = pl.ds(pl.multiple_of(block * BLK, BLK), BLK)
            param_ref[0:1, at] = jnp.sum(adjoint[:own_days] * grad_ref[block, 0], axis=0, keepdims=True)
            param_ref[1:2, at] = jnp.sum(adjoint[:own_days] * grad_ref[block, 1], axis=0, keepdims=True)
            for chunk in range(2):
                adj_ref[chunk, 0:have, :] = adjoint[:, chunk * LANES : (chunk + 1) * LANES]

            for chunk in range(2):
                row = lambda lag, chunk=chunk: weight_ref[block, chunk, pl.ds(lag, 1), :]
                result = lag_sum(adj_ref, chunk, row, need)
                at = pl.ds(pl.multiple_of(block * BLK + chunk * LANES, LANES), LANES)
                out_ref[:, at] = result[:own_days]
                if height + 1 < LEVELS:
                    high, low = split_terms(result)
                    lanes = slice(chunk * LANES, (chunk + 1) * LANES)
                    lat_ref[block, 0:need, lanes] = high
                    lat_ref[block, need : 2 * need, lanes] = low


def call(kernel, out_shape, in_smem, in_vmem, scratch, flops):
    vmem = pl.BlockSpec(memory_space=pltpu.VMEM)
    smem = pl.BlockSpec(memory_space=pltpu.SMEM)
    size = lambda leaves: sum(leaf.size * leaf.dtype.itemsize for leaf in leaves)
    return pl.pallas_call(
        kernel,
        out_shape=out_shape,
        in_specs=[smem] * len(in_smem) + [vmem] * len(in_vmem),
        out_specs=jax.tree.map(lambda _: vmem, out_shape),
        scratch_shapes=scratch,
        compiler_params=pltpu.CompilerParams(vmem_limit_bytes=VMEM_LIMIT),
        cost_estimate=pl.CostEstimate(
            flops=flops,
            bytes_accessed=size(in_vmem) + size(jax.tree.leaves(out_shape)),
            transcendentals=0,
        ),
    )(*in_smem, *in_vmem)


def exchange(values, axis, by):
    return lax.ppermute(values, axis, [(i, i ^ by) for i in range(lax.axis_size(axis))])


def over_basin(values):
    others = [exchange(values, "basin", by) for by in (2, 4, 6)]
    own = jnp.stack([values] + others)
    return own, exchange(own, "basin", 1)


def fast_shards(
    inflow, cotangent, gauge_reach, shape_param, scale_param, block_level, down_local, in_slot, send_reach,
):
    own_days, reaches = inflow.shape
    gauges = cotangent.shape[1]
    blocks = block_level.shape[0]
    shards = lax.axis_size("tm")
    days = shards * own_days
    width = 2 * LANES
    me = lax.axis_index("basin")
    part = me.astype(jnp.int32).reshape(1)
    earlier = lax.ppermute(inflow, "tm", [(i, i + 1) for i in range(shards - 1)])
    pieces = [cotangent] + [
        lax.ppermute(cotangent, "tm", [(i + by, i) for i in range(shards - by)]) for by in range(1, shards)
    ]
    turn = (4 - me % 4) % 4
    padded = jnp.concatenate([send_reach[0], jnp.full((1, send_reach.shape[2]), -1, jnp.int32)], axis=0)
    padded = padded.reshape(2, 4, KROWS)
    padded = jnp.concatenate([padded, padded], axis=1)
    want = lax.dynamic_slice(padded, (0, turn, 0), (2, 4, KROWS)).reshape(1, width)
    lane = jnp.arange(width, dtype=jnp.int32)
    want_level = ((lane // LANES) * 4 + ((lane % LANES) // KROWS + turn) % 4).reshape(1, width)
    zero = jnp.zeros_like(shape_param)
    table = jnp.stack(
        [down_local.astype(F32), in_slot.astype(F32), shape_param, scale_param, zero, zero, zero, zero]
    )
    table = table.reshape(8, blocks, BLK).transpose(1, 0, 2)
    gauge_ids = jnp.broadcast_to(gauge_reach[:, None], (gauges, LANES))
    by_block = lambda values: values.reshape(blocks, 1, BLK)
    shape_of = jax.ShapeDtypeStruct
    tables = [pltpu.SMEM((LEVELS * MAXB,), jnp.int32), pltpu.SMEM((LEVELS,), jnp.int32)]

    nodes, path_weights, composed = call(
        functools.partial(path_kernel, days),
        (
            shape_of((8, width), jnp.int32),
            shape_of((SENDS, 2, KROWS, LANES), F32),
            shape_of((days + 8, width), F32),
        ),
        [block_level, part],
        [table, want, want_level],
        tables + [pltpu.VMEM((8, width), F32), pltpu.VMEM((2, KROWS + days, LANES), F32)],
        8_000_000_000,
    )
    c_own, c_mate = over_basin(composed)
    weights, grads = call(
        weights_kernel,
        (shape_of((blocks, 2, KROWS, LANES), F32), shape_of((blocks, 2, own_days, BLK), F32)),
        [],
        [by_block(shape_param), by_block(scale_param), inflow, earlier],
        [pltpu.VMEM((2, 2 * own_days, LANES), F32), pltpu.VMEM((2, 2, KROWS, LANES), F32)],
        4_000_000_000,
    )
    terms = pltpu.VMEM((2 * days, gauges), BF16)
    path_adjoint = call(
        functools.partial(path_adjoint_kernel, shards),
        shape_of((days, width), F32),
        [],
        pieces + [gauge_ids, nodes, path_weights],
        [terms, pltpu.VMEM((SENDS, 2, days, LANES), F32), pltpu.VMEM((2, days + KROWS, LANES), F32)],
        4_000_000_000,
    )
    a_own, a_mate = over_basin(path_adjoint)
    seeds = call(
        functools.partial(seed_kernel, shards),
        shape_of((blocks, days, BLK), F32),
        [],
        pieces + [gauge_ids],
        [terms],
        6_000_000_000,
    )
    lateral, params = call(
        functools.partial(full_kernel, own_days),
        (shape_of((own_days, reaches), F32), shape_of((2, reaches), F32)),
        [block_level, part],
        [a_own, a_mate, c_own, c_mate, seeds, weights, grads, by_block(down_local), by_block(in_slot)],
        tables
        + [
            pltpu.VMEM((SENDS, 2 * days, width), BF16),
            pltpu.VMEM((2, days, LANES), F32),
            pltpu.VMEM((2, 2 * days, LANES), F32),
            pltpu.VMEM((2, days + KROWS, LANES), F32),
            pltpu.VMEM((blocks, 2 * days, BLK), BF16),
        ],
        10_000_000_000,
    )
    first, second, third = (exchange(params, "tm", by) for by in (1, 2, 3))
    return lateral, (params + first) + (second + third)


def passed_along(shard, axis, by):
    peers = lax.axis_size(axis)
    pairs = [(i, i + by) for i in range(peers) if 0 <= i + by < peers]
    return lax.ppermute(shard, axis, pairs)


def kernel_of(shape_param, scale_param, lag_count):
    offsets = jnp.arange(lag_count, dtype=jnp.float32) + 0.5
    logits = (shape_param[None, :] - 1.0) * jnp.log(offsets)[:, None] - offsets[
        :, None
    ] / scale_param[None, :]
    weights = jnp.exp(logits)
    return (weights / jnp.sum(weights, axis=0, keepdims=True), offsets)


def lag_adjoint(kernel, extended, day_count):
    summed = kernel[0][None, :] * extended[0:day_count]
    for lag_index in range(1, kernel.shape[0]):
        summed = summed + kernel[lag_index][None, :] * extended[lag_index : lag_index + day_count]
    return summed


def lag_gradient(adjoint_in, inflow_ext, lag_count, day_count):
    per_lag = []
    for lag_index in range(lag_count):
        first_day = lag_count - 1 - lag_index
        per_lag.append(jnp.sum(adjoint_in * inflow_ext[first_day : first_day + day_count], axis=0))
    return jnp.stack(per_lag)


def param_terms(kernel, offsets, scale_param, kernel_grad):
    weighted = jnp.sum(kernel * kernel_grad, axis=0, keepdims=True)
    logit_grad = kernel * (kernel_grad - weighted)
    shape_grad = jnp.sum(logit_grad * jnp.log(offsets)[:, None], axis=0)
    scale_grad = jnp.sum(logit_grad * offsets[:, None], axis=0) / (scale_param * scale_param)
    return jnp.stack([shape_grad, scale_grad])


def take_blocks(values, chosen, block_count):
    rows = values.shape[0]
    picked = jnp.take(values.reshape(rows, block_count, BLK), chosen, axis=1)
    return picked.reshape(rows, chosen.shape[0] * BLK)


def inbound(seed_part, adjoint_all, received, below_reach, slot_of):
    local_part = jnp.where(
        below_reach[None, :] >= 0, adjoint_all[:, jnp.maximum(below_reach, 0)], 0.0
    )
    remote_part = jnp.where(slot_of[None, :] >= 0, received[:, jnp.maximum(slot_of, 0)], 0.0)
    return seed_part + local_part + remote_part


def shards(
    inflow,
    cotangent,
    gauge_reach,
    shape_param,
    scale_param,
    block_level,
    down_local,
    in_slot,
    send_reach,
):
    day_count, reach_count = inflow.shape
    lag_count = LAGS
    block_count = block_level.shape[0]
    kernel, offsets = kernel_of(shape_param, scale_param, lag_count)
    gauge_seed = jnp.zeros((day_count, reach_count), jnp.float32).at[:, gauge_reach].add(cotangent)
    earlier = passed_along(inflow[day_count - (lag_count - 1) :], "tm", 1)
    inflow_ext = jnp.concatenate([earlier, inflow], axis=0)
    adjoint_all = jnp.zeros((day_count, reach_count), jnp.float32)
    kernel_grad = jnp.zeros((lag_count, reach_count), jnp.float32)
    received = jnp.zeros((day_count, send_reach.shape[2]), jnp.float32)
    slot_ids = jnp.arange(MAXB, dtype=jnp.int32)
    block_ids = jnp.arange(block_count, dtype=jnp.int32)
    down_rows = down_local.reshape(1, reach_count)
    slot_rows = in_slot.reshape(1, reach_count)
    for height in range(LEVELS):
        at_height = block_level == height
        rank_of = jnp.cumsum(at_height.astype(jnp.int32)) - 1
        slot_hits = at_height[None, :] & (rank_of[None, :] == slot_ids[:, None])
        slot_valid = jnp.any(slot_hits, axis=1)
        chosen = jnp.sum(jnp.where(slot_hits, block_ids[None, :], 0), axis=1)
        below_reach = take_blocks(down_rows, chosen, block_count)[0]
        slot_of = take_blocks(slot_rows, chosen, block_count)[0]
        seed_part = take_blocks(gauge_seed, chosen, block_count)
        adjoint_in = inbound(seed_part, adjoint_all, received, below_reach, slot_of)
        later_head = passed_along(adjoint_in[: lag_count - 1], "tm", -1)
        extended = jnp.concatenate([adjoint_in, later_head], axis=0)
        outflow = lag_adjoint(take_blocks(kernel, chosen, block_count), extended, day_count)
        lag_grads = lag_gradient(
            adjoint_in, take_blocks(inflow_ext, chosen, block_count), lag_count, day_count
        )
        target_blocks = jnp.where(slot_valid, chosen, block_count)
        adjoint_all = (
            adjoint_all.reshape(day_count, block_count, BLK)
            .at[:, target_blocks]
            .set(outflow.reshape(day_count, MAXB, BLK), mode="drop")
            .reshape(day_count, reach_count)
        )
        kernel_grad = (
            kernel_grad.reshape(lag_count, block_count, BLK)
            .at[:, target_blocks]
            .set(lag_grads.reshape(lag_count, MAXB, BLK), mode="drop")
            .reshape(lag_count, reach_count)
        )
        if height + 1 < LEVELS:
            wanted = send_reach[0, height]
            outgoing = jnp.where(wanted[None, :] >= 0, adjoint_all[:, jnp.maximum(wanted, 0)], 0.0)
            received = lax.all_to_all(outgoing, "basin", split_axis=1, concat_axis=1, tiled=True)
    kernel_total = lax.psum(kernel_grad, "tm")
    param_grad = param_terms(kernel, offsets, scale_param, kernel_total)
    return (adjoint_all, param_grad)


def solution(mesh):
    in_specs = (
        P("tm", "basin"),
        P("tm", "basin"),
        P("basin"),
        P("basin"),
        P("basin"),
        P("basin"),
        P("basin"),
        P("basin"),
        P("basin", None, None),
    )
    out_specs = (P("tm", "basin"), P(None, "basin"))
    small = mesh.shape["basin"] == 8 and mesh.shape["tm"] == 4
    body = fast_shards if small else shards
    return jax.shard_map(body, mesh=mesh, in_specs=in_specs, out_specs=out_specs, check_vma=False)
```

profile of v0, /device:TPU:0, one launch (start us, length us, event | category | flops | bytes accessed | tf_op | source)
XLA Modules:
  0.0 97.5 jit_solution(8981049017778568798)
XLA Ops:
  0.6 1.3 %collective-permute-start.2 = (f32[32,2048]{1,0:T(8,128)}, f32[32,2048]{1,0:T(8,128)S(1)}, u32[]{:S(2)}, u32[]{:S(2)}) collective-permute-start(f32[32,2048]{1,0:T(8,128)} %refs_0_.3), channel_id=1, source_target_pairs={{3,0},{7,4},{11,8},{15,12},{19,16},{23,20},{27,24},{31,28}} | collective-permute-start | bytes 786440 | tf_op jit(solution)/shard_map/ppermute | solution.py:391
  1.9 1.3 %collective-permute-start.1 = (f32[32,2048]{1,0:T(8,128)}, f32[32,2048]{1,0:T(8,128)S(1)}, u32[]{:S(2)}, u32[]{:S(2)}) collective-permute-start(f32[32,2048]{1,0:T(8,128)} %refs_0_.3), channel_id=1, source_target_pairs={{2,0},{3,1},{6,4},{7,5},{10,8},{11,9},{14,12},{15,13},{18,16},{19,... | collective-permute-start | bytes 786440 | tf_op jit(solution)/shard_map/ppermute | solution.py:391
  3.2 1.3 %collective-permute-start = (f32[32,2048]{1,0:T(8,128)}, f32[32,2048]{1,0:T(8,128)S(1)}, u32[]{:S(2)}, u32[]{:S(2)}) collective-permute-start(f32[32,2048]{1,0:T(8,128)} %refs_0_.3), channel_id=1, source_target_pairs={{1,0},{2,1},{3,2},{5,4},{6,5},{7,6},{9,8},{10,9},{11,10},{13,12},{... | collective-permute-start | bytes 786440 | tf_op jit(solution)/shard_map/ppermute | solution.py:391
  4.6 0.6 fusion.1.want_level_ref
  5.1 0.7 copy.13
  5.9 0.7 reshape.175.want_ref
  6.5 0.7 convert_element_type.6
  7.3 0.7 convert_element_type.7
  8.0 1.5 %stack.53 = f32[8,16,256]{2,0,1:T(8,128)} concatenate(f32[1,16,256]{2,0,1:T(1,128)S(1)} %bitcast.31, f32[1,16,256]{2,0,1:T(1,128)S(1)} %bitcast.32, f32[1,16,256]{2,0,1:T(1,128)} %bitcast.33, f32[1,16,256]{2,0,1:T(1,128)} %bitcast.35, f32[4,16,256]{2,0,1:T(4,128)S(1)} %stack.52), dimensions={0} | concatenate | bytes 262144 | tf_op jit(solution)/shard_map/stack | solution.py:401
  9.5 0.0 copy-start.3
  9.5 7.8 %shard_map.104 = (s32[8,256]{1,0:T(8,128)}, f32[7,2,32,128]{3,2,1,0:T(8,128)}, f32[136,256]{1,0:T(8,128)}) custom-call(s32[16]{0:T(128)} %level_ref.3, s32[1]{0:T(128)} %bitcast.part_ref, f32[16,8,256]{2,1,0:T(8,128)} %bitcast.26, s32[1,256]{1,0:T(1,128)} %reshape.175.want_ref, s32[1,256]{1,0:T(1,128)} %fusion.1.want_level_ref), custom_call_target="tpu_custom_call" | custom-call | flops 8000000000 | bytes 509952 | tf_op jit(solution)/shard_map/pallas_call | solution.py:353
  17.3 3.9 %collective-permute-start.9 = (f32[136,256]{1,0:T(8,128)}, f32[136,256]{1,0:T(8,128)S(1)}, u32[]{:S(2)}, u32[]{:S(2)}) collective-permute-start(f32[136,256]{1,0:T(8,128)} %get-tuple-element.11), channel_id=1, source_target_pairs={{0,24},{4,28},{8,16},{12,20},{16,8},{20,12},{24,0},{28,4},{1,25},{... | collective-permute-start | bytes 417800 | tf_op jit(solution)/shard_map/ppermute | solution.py:369
  21.1 0.0 collective-permute-start.8
  21.2 0.0 collective-permute-done.2.refs_3_
  21.2 0.0 copy-start.8
  21.2 0.6 collective-permute-start.7
  21.7 3.1 %collective-permute-done.1.refs_2_ = f32[32,2048]{1,0:T(8,128)S(1)} collective-permute-done((f32[32,2048]{1,0:T(8,128)}, f32[32,2048]{1,0:T(8,128)S(1)}, u32[]{:S(2)}, u32[]{:S(2)}) %collective-permute-start.1) | collective-permute-done | bytes 262176 | tf_op jit(solution)/shard_map/ppermute | solution.py:391
  24.8 0.0 copy-start.9
  24.8 0.0 collective-permute-done.refs_1_
  24.8 0.0 copy-start.10
  24.8 0.0 copy-done.3
  24.8 1.3 %broadcast_in_dim.2.refs_4_ = s32[2048,128]{1,0:T(8,128)} broadcast(s32[2048]{0:T(1024)S(1)} %copy-done.3), dimensions={0} | broadcast | bytes 1056768 | tf_op jit(solution)/shard_map/broadcast_in_dim | solution.py:405
  26.1 0.0 copy-done.8
  26.1 0.0 copy-done.9
  26.1 0.0 copy-done.10
  26.1 0.0 copy-start.2
  26.2 7.6 %shard_map.105 = f32[128,256]{1,0:T(8,128)} custom-call(f32[32,2048]{1,0:T(8,128)} %refs_0_.3, f32[32,2048]{1,0:T(8,128)} %copy-done.10, f32[32,2048]{1,0:T(8,128)} %copy-done.9, f32[32,2048]{1,0:T(8,128)} %copy-done.8, s32[2048,128]{1,0:T(8,128)} %broadcast_in_dim.2.refs_4_, s32[8,256]{1,0:T(8,128)} %get-tuple-element.9.refs_5_, ...), custom_call_target="tpu_custom_call" | custom-call | flops 4000000000 | bytes 2465792 | tf_op jit(solution)/shard_map/pallas_call | solution.py:353
  33.7 3.1 %collective-permute-start.5 = (f32[128,256]{1,0:T(8,128)}, f32[128,256]{1,0:T(8,128)S(1)}, u32[]{:S(2)}, u32[]{:S(2)}) collective-permute-start(f32[128,256]{1,0:T(8,128)} %shard_map.105), channel_id=1, source_target_pairs={{0,24},{4,28},{8,16},{12,20},{16,8},{20,12},{24,0},{28,4},{1,25},{... | collective-permute-start | bytes 393224 | tf_op jit(solution)/shard_map/ppermute | solution.py:369
  36.8 0.5 collective-permute-start.4
  37.3 0.0 collective-permute-done.9
  37.3 0.1 collective-permute-start.3
  37.4 0.0 collective-permute-done.8
  37.4 0.0 copy-done.5
  37.4 8.0 %collective-permute-start.11 = (f32[32,4096]{1,0:T(8,128)S(1)}, f32[32,4096]{1,0:T(8,128)S(1)}, u32[]{:S(2)}, u32[]{:S(2)}) collective-permute-start(f32[32,4096]{1,0:T(8,128)S(1)} %copy-done.5), channel_id=1, source_target_pairs={{0,1},{1,2},{2,3},{4,5},{5,6},{6,7},{8,9},{9,10},{10,11},{12,13},{... | collective-permute-start | bytes 1572872 | tf_op jit(solution)/shard_map/ppermute | solution.py:389
  45.4 0.0 collective-permute-done.7
  45.4 0.0 copy-done.2
  45.4 0.0 copy-start
  45.5 0.1 collective-permute-start.10
  45.5 0.0 collective-permute-done.5
  45.5 0.0 collective-permute-done.4
  45.6 0.0 collective-permute-done.3
  45.6 1.0 %pad_maximum_fusion.1.a_own_ref = f32[4,128,256]{2,1,0:T(8,128)S(1)} fusion(f32[1,128,256]{2,1,0:T(8,128)S(1)} %bitcast.28, f32[1,128,256]{2,1,0:T(8,128)S(1)} %bitcast.29, f32[1,128,256]{2,1,0:T(8,128)S(1)} %bitcast.30, f32[1,128,256]{2,1,0:T(8,128)} %bitcast.27), kind=kLoop, calls=%fused_computation.1 | loop fusion | flops 393216 | bytes 1048576 | tf_op jit(solution)/shard_map/stack | solution.py:374
  46.6 0.0 copy-start.1
  46.6 0.5 collective-permute-start.6
  47.1 10.2 %shard_map.106.seed_ref = f32[16,128,256]{2,1,0:T(8,128)} custom-call(f32[32,2048]{1,0:T(8,128)} %refs_0_.3, f32[32,2048]{1,0:T(8,128)} %copy-done.10, f32[32,2048]{1,0:T(8,128)} %copy-done.9, f32[32,2048]{1,0:T(8,128)} %copy-done.8, s32[2048,128]{1,0:T(8,128)} %broadcast_in_dim.2.refs_4_), custom_call_target="tpu_custom_call" | custom-call | flops 6000000000 | bytes 4194304 | tf_op jit(solution)/shard_map/pallas_call | solution.py:353
  57.2 0.0 copy-done
  57.2 0.0 copy-done.1
  57.2 0.0 collective-permute-done.11.earlier_ref
  57.2 0.0 copy-start.6
  57.2 0.8 copy-done.6
  58.0 5.3 %shard_map.107 = (f32[16,2,32,128]{3,2,1,0:T(8,128)}, f32[16,2,32,256]{3,2,1,0:T(8,128)}) custom-call(f32[16,1,256]{2,1,0:T(1,128)} %bitcast.34, f32[16,1,256]{2,1,0:T(1,128)} %bitcast.36, f32[32,4096]{1,0:T(8,128)} %inflow_ref.1, f32[32,4096]{1,0:T(8,128)} %copy-done.6), custom_call_target="tpu_custom_call" | custom-call | flops 4000000000 | bytes 2654208 | tf_op jit(solution)/shard_map/pallas_call | solution.py:353
  63.3 0.0 collective-permute-done.10.c_mate_ref
  63.3 0.0 collective-permute-done.6.a_mate_ref
  63.3 0.0 copy-start.7
  63.3 0.8 copy-done.4
  64.1 0.2 copy-done.7
  64.2 22.3 %shard_map.108 = (f32[32,4096]{1,0:T(8,128)}, f32[2,4096]{1,0:T(2,128)}) custom-call(s32[16]{0:T(128)} %level_ref.3, s32[1]{0:T(128)} %bitcast.part_ref, f32[4,128,256]{2,1,0:T(8,128)} %copy-done.1, f32[4,128,256]{2,1,0:T(8,128)} %copy-done.7, f32[4,136,256]{2,1,0:T(8,128)} %copy-done, f32[4,136,256]{2,1,0:T(8,128)} %copy-done.4, ...), custom_call_target="tpu_custom_call" | custom-call | flops 10000000000 | bytes 6422528 | tf_op jit(solution)/shard_map/pallas_call | solution.py:353
  86.6 0.2 collective-permute-start.14
  86.8 5.2 %collective-permute-start.13 = (f32[2,4096]{1,0:T(2,128)}, f32[2,4096]{1,0:T(2,128)S(1)}, u32[]{:S(2)}, u32[]{:S(2)}) collective-permute-start(f32[2,4096]{1,0:T(2,128)} %get-tuple-element.15), channel_id=1, source_target_pairs={{0,2},{1,3},{2,0},{3,1},{4,6},{5,7},{6,4},{7,5},{8,10},{9,11},{10,... | collective-permute-start | bytes 98312 | tf_op jit(solution)/shard_map/ppermute | solution.py:369
  91.9 0.0 collective-permute-start.12
  91.9 0.9 collective-permute-done.14
  92.8 1.5 %collective-permute-done.13 = f32[2,4096]{1,0:T(2,128)S(1)} collective-permute-done((f32[2,4096]{1,0:T(2,128)}, f32[2,4096]{1,0:T(2,128)S(1)}, u32[]{:S(2)}, u32[]{:S(2)}) %collective-permute-start.13) | collective-permute-done | bytes 32800 | tf_op jit(solution)/shard_map/ppermute | solution.py:369
  94.4 1.7 %collective-permute-done.12 = f32[2,4096]{1,0:T(2,128)S(1)} collective-permute-done((f32[2,4096]{1,0:T(2,128)}, f32[2,4096]{1,0:T(2,128)S(1)}, u32[]{:S(2)}, u32[]{:S(2)}) %collective-permute-start.12) | collective-permute-done | bytes 32800 | tf_op jit(solution)/shard_map/ppermute | solution.py:369
  96.1 1.4 %add_add_fusion = f32[2,4096]{1,0:T(2,128)} fusion(f32[2,4096]{1,0:T(2,128)S(1)} %collective-permute-done.13, f32[2,4096]{1,0:T(2,128)S(1)} %collective-permute-done.14, f32[2,4096]{1,0:T(2,128)} %get-tuple-element.15, f32[2,4096]{1,0:T(2,128)S(1)} %collective-permute-done.12), kind=kLoop, calls=%fused_computation.2 | loop fusion | flops 24576 | bytes 163840 | tf_op jit(solution)/shard_map/add | solution.py:465
  (6 shorter events, 0.1 us)
Async XLA Ops:
  0.6 20.5 %collective-permute-start.2 = (f32[32,2048]{1,0:T(8,128)}, f32[32,2048]{1,0:T(8,128)S(1)}, u32[]{:S(2)}, u32[]{:S(2)}) collective-permute-start(f32[32,2048]{1,0:T(8,128)} %refs_0_.3), channel_id=1, source_target_pairs={{3,0},{7,4},{11,8},{15,12},{19,16},{23,20},{27,24},{31,28}} | collective-permute-start | bytes 786440 | tf_op jit(solution)/shard_map/ppermute | solution.py:391
  1.9 22.9 %collective-permute-start.1 = (f32[32,2048]{1,0:T(8,128)}, f32[32,2048]{1,0:T(8,128)S(1)}, u32[]{:S(2)}, u32[]{:S(2)}) collective-permute-start(f32[32,2048]{1,0:T(8,128)} %refs_0_.3), channel_id=1, source_target_pairs={{2,0},{3,1},{6,4},{7,5},{10,8},{11,9},{14,12},{15,13},{18,16},{19,... | collective-permute-start | bytes 786440 | tf_op jit(solution)/shard_map/ppermute | solution.py:391
  3.2 21.6 %collective-permute-start = (f32[32,2048]{1,0:T(8,128)}, f32[32,2048]{1,0:T(8,128)S(1)}, u32[]{:S(2)}, u32[]{:S(2)}) collective-permute-start(f32[32,2048]{1,0:T(8,128)} %refs_0_.3), channel_id=1, source_target_pairs={{1,0},{2,1},{3,2},{5,4},{6,5},{7,6},{9,8},{10,9},{11,10},{13,12},{... | collective-permute-start | bytes 786440 | tf_op jit(solution)/shard_map/ppermute | solution.py:391
  9.5 15.3 %copy-start.3 = (s32[2048]{0:T(1024)S(1)}, s32[2048]{0:T(1024)}, u32[]{:S(2)}) copy-start(s32[2048]{0:T(1024)} %param.11) | copy-start | bytes 24580
  17.3 20.0 %collective-permute-start.9 = (f32[136,256]{1,0:T(8,128)}, f32[136,256]{1,0:T(8,128)S(1)}, u32[]{:S(2)}, u32[]{:S(2)}) collective-permute-start(f32[136,256]{1,0:T(8,128)} %get-tuple-element.11), channel_id=1, source_target_pairs={{0,24},{4,28},{8,16},{12,20},{16,8},{20,12},{24,0},{28,4},{1,25},{... | collective-permute-start | bytes 417800 | tf_op jit(solution)/shard_map/ppermute | solution.py:369
  21.1 16.2 %collective-permute-start.8 = (f32[136,256]{1,0:T(8,128)}, f32[136,256]{1,0:T(8,128)S(1)}, u32[]{:S(2)}, u32[]{:S(2)}) collective-permute-start(f32[136,256]{1,0:T(8,128)} %get-tuple-element.11), channel_id=1, source_target_pairs={{0,16},{4,20},{8,24},{12,28},{16,0},{20,4},{24,8},{28,12},{1,17},{... | collective-permute-start | bytes 417800 | tf_op jit(solution)/shard_map/ppermute | solution.py:369
  21.2 5.0 %copy-start.8 = (f32[32,2048]{1,0:T(8,128)}, f32[32,2048]{1,0:T(8,128)S(1)}, u32[]{:S(2)}) copy-start(f32[32,2048]{1,0:T(8,128)S(1)} %collective-permute-done.2.refs_3_) | copy-start | bytes 786436
  21.2 24.2 %collective-permute-start.7 = (f32[136,256]{1,0:T(8,128)}, f32[136,256]{1,0:T(8,128)S(1)}, u32[]{:S(2)}, u32[]{:S(2)}) collective-permute-start(f32[136,256]{1,0:T(8,128)} %get-tuple-element.11), channel_id=1, source_target_pairs={{0,8},{4,12},{8,0},{12,4},{16,24},{20,28},{24,16},{28,20},{1,9},{5... | collective-permute-start | bytes 417800 | tf_op jit(solution)/shard_map/ppermute | solution.py:369
  24.8 1.3 %copy-start.9 = (f32[32,2048]{1,0:T(8,128)}, f32[32,2048]{1,0:T(8,128)S(1)}, u32[]{:S(2)}) copy-start(f32[32,2048]{1,0:T(8,128)S(1)} %collective-permute-done.1.refs_2_) | copy-start | bytes 786436
  24.8 1.3 %copy-start.10 = (f32[32,2048]{1,0:T(8,128)}, f32[32,2048]{1,0:T(8,128)S(1)}, u32[]{:S(2)}) copy-start(f32[32,2048]{1,0:T(8,128)S(1)} %collective-permute-done.refs_1_) | copy-start | bytes 786436
  26.1 11.2 %copy-start.5 = (f32[32,4096]{1,0:T(8,128)S(1)}, f32[32,4096]{1,0:T(8,128)}, u32[]{:S(2)}) copy-start(f32[32,4096]{1,0:T(8,128)} %inflow_ref.1) | copy-start | bytes 1572868
  26.1 19.2 %copy-start.2 = (f32[136,256]{1,0:T(8,128)S(1)}, f32[136,256]{1,0:T(8,128)}, u32[]{:S(2)}) copy-start(f32[136,256]{1,0:T(8,128)} %get-tuple-element.11) | copy-start | bytes 417796
  33.7 11.8 %collective-permute-start.5 = (f32[128,256]{1,0:T(8,128)}, f32[128,256]{1,0:T(8,128)S(1)}, u32[]{:S(2)}, u32[]{:S(2)}) collective-permute-start(f32[128,256]{1,0:T(8,128)} %shard_map.105), channel_id=1, source_target_pairs={{0,24},{4,28},{8,16},{12,20},{16,8},{20,12},{24,0},{28,4},{1,25},{... | collective-permute-start | bytes 393224 | tf_op jit(solution)/shard_map/ppermute | solution.py:369
  36.8 8.8 %collective-permute-start.4 = (f32[128,256]{1,0:T(8,128)}, f32[128,256]{1,0:T(8,128)S(1)}, u32[]{:S(2)}, u32[]{:S(2)}) collective-permute-start(f32[128,256]{1,0:T(8,128)} %shard_map.105), channel_id=1, source_target_pairs={{0,16},{4,20},{8,24},{12,28},{16,0},{20,4},{24,8},{28,12},{1,17},{... | collective-permute-start | bytes 393224 | tf_op jit(solution)/shard_map/ppermute | solution.py:369
  37.3 8.3 %collective-permute-start.3 = (f32[128,256]{1,0:T(8,128)}, f32[128,256]{1,0:T(8,128)S(1)}, u32[]{:S(2)}, u32[]{:S(2)}) collective-permute-start(f32[128,256]{1,0:T(8,128)} %shard_map.105), channel_id=1, source_target_pairs={{0,8},{4,12},{8,0},{12,4},{16,24},{20,28},{24,16},{28,20},{1,9},{5... | collective-permute-start | bytes 393224 | tf_op jit(solution)/shard_map/ppermute | solution.py:369
  37.4 19.9 %collective-permute-start.11 = (f32[32,4096]{1,0:T(8,128)S(1)}, f32[32,4096]{1,0:T(8,128)S(1)}, u32[]{:S(2)}, u32[]{:S(2)}) collective-permute-start(f32[32,4096]{1,0:T(8,128)S(1)} %copy-done.5), channel_id=1, source_target_pairs={{0,1},{1,2},{2,3},{4,5},{5,6},{6,7},{8,9},{9,10},{10,11},{12,13},{... | collective-permute-start | bytes 1572872 | tf_op jit(solution)/shard_map/ppermute | solution.py:389
  45.4 11.8 %copy-start = (f32[4,136,256]{2,1,0:T(8,128)}, f32[4,136,256]{2,1,0:T(8,128)S(1)}, u32[]{:S(2)}) copy-start(f32[4,136,256]{2,1,0:T(8,128)S(1)} %pad_maximum_fusion.c_own_ref) | copy-start | bytes 1671172
  45.5 17.8 %collective-permute-start.10 = (f32[4,136,256]{2,1,0:T(8,128)S(1)}, f32[4,136,256]{2,1,0:T(8,128)S(1)}, u32[]{:S(2)}, u32[]{:S(2)}) collective-permute-start(f32[4,136,256]{2,1,0:T(8,128)S(1)} %pad_maximum_fusion.c_own_ref), channel_id=1, source_target_pairs={{0,4},{4,0},{8,12},{12,8},{16,20},{20,16},{24,28},{28,24},{1,5},{5... | collective-permute-start | bytes 1671176 | tf_op jit(solution)/shard_map/ppermute | solution.py:369
  46.6 10.6 %copy-start.1 = (f32[4,128,256]{2,1,0:T(8,128)}, f32[4,128,256]{2,1,0:T(8,128)S(1)}, u32[]{:S(2)}) copy-start(f32[4,128,256]{2,1,0:T(8,128)S(1)} %pad_maximum_fusion.1.a_own_ref) | copy-start | bytes 1572868
  46.6 16.7 %collective-permute-start.6 = (f32[4,128,256]{2,1,0:T(8,128)S(1)}, f32[4,128,256]{2,1,0:T(8,128)S(1)}, u32[]{:S(2)}, u32[]{:S(2)}) collective-permute-start(f32[4,128,256]{2,1,0:T(8,128)S(1)} %pad_maximum_fusion.1.a_own_ref), channel_id=1, source_target_pairs={{0,4},{4,0},{8,12},{12,8},{16,20},{20,16},{24,28},{28,24},{1,5},{5... | collective-permute-start | bytes 1572872 | tf_op jit(solution)/shard_map/ppermute | solution.py:369
  57.2 0.8 copy-start.6
  63.3 0.8 copy-start.4
  63.3 1.0 copy-start.7
  86.6 6.3 %collective-permute-start.14 = (f32[2,4096]{1,0:T(2,128)}, f32[2,4096]{1,0:T(2,128)S(1)}, u32[]{:S(2)}, u32[]{:S(2)}) collective-permute-start(f32[2,4096]{1,0:T(2,128)} %get-tuple-element.15), channel_id=1, source_target_pairs={{0,3},{1,2},{2,1},{3,0},{4,7},{5,6},{6,5},{7,4},{8,11},{9,10},{10,... | collective-permute-start | bytes 98312 | tf_op jit(solution)/shard_map/ppermute | solution.py:369
  86.8 7.6 %collective-permute-start.13 = (f32[2,4096]{1,0:T(2,128)}, f32[2,4096]{1,0:T(2,128)S(1)}, u32[]{:S(2)}, u32[]{:S(2)}) collective-permute-start(f32[2,4096]{1,0:T(2,128)} %get-tuple-element.15), channel_id=1, source_target_pairs={{0,2},{1,3},{2,0},{3,1},{4,6},{5,7},{6,4},{7,5},{8,10},{9,11},{10,... | collective-permute-start | bytes 98312 | tf_op jit(solution)/shard_map/ppermute | solution.py:369
  91.9 4.1 %collective-permute-start.12 = (f32[2,4096]{1,0:T(2,128)}, f32[2,4096]{1,0:T(2,128)S(1)}, u32[]{:S(2)}, u32[]{:S(2)}) collective-permute-start(f32[2,4096]{1,0:T(2,128)} %get-tuple-element.15), channel_id=1, source_target_pairs={{0,1},{1,0},{2,3},{3,2},{4,5},{5,4},{6,7},{7,6},{8,9},{9,8},{10,11... | collective-permute-start | bytes 98312 | tf_op jit(solution)/shard_map/ppermute | solution.py:369
where the time goes:
time: 97.4 us; the launch traced here: 97.5 us
  Pallas kernels  53.1 us (55%)
  starting transfers between devices  25.8 us (26%)
  waiting for transfers between devices  7.22 us (7%)
  local copies, waits for them, and re-layouts  5.98 us (6%)
  other arithmetic  4.52 us (5%)
    pallas_call x5, Pallas kernels, call(): pl.pallas_call(kernel, out_shape=out_shape, in_specs=[smem] * len(in_smem...  53.1 us
    ppermute x11, starting transfers between devices, exchange(): lax.ppermute(values, axis, [(i, i ^ by) for i in range(lax.axis_size(axis...  14 us
    ppermute x1, starting transfers between devices, fast_shards(): lax.ppermute(inflow, 'tm', [(i, i + 1) for i in range(shards - 1)])  8 us
    ppermute x11, waiting for transfers between devices, exchange(): lax.ppermute(values, axis, [(i, i ^ by) for i in range(lax.axis_size(axis...  4.14 us
    ppermute x3, starting transfers between devices, fast_shards(): lax.ppermute(cotangent, 'tm', [(i + by, i) for i in range(shards - by)])  3.88 us
    ppermute x3, waiting for transfers between devices, fast_shards(): lax.ppermute(cotangent, 'tm', [(i + by, i) for i in range(shards - by)])  3.08 us
    unnamed x23, local copies, waits for them, and re-layouts  2.46 us
  transfers between devices with their start and end apart: 15, of which 4 were waited for; matrix products, arithmetic and copies ran while one was open for 8% of the time, Pallas kernels for 32%

commit v1 on v0

--- a/solution.py
+++ b/solution.py
@@ -14,9 +14,10 @@
 LANES = 128
 KROWS = 32
 SENDS = LEVELS - 1
+WIDTH = 2 * LANES
 F32 = jnp.float32
 BF16 = jnp.bfloat16
-VMEM_LIMIT = 56 * 1024 * 1024
+VMEM_LIMIT = 20 * 1024 * 1024
 
 
 def iota(shape, axis):
@@ -65,6 +66,21 @@
         for step, lag in enumerate(steps):
             total = total + weight_of(lag) * shifted[8 * step : 8 * step + days]
     return total
+
+
+def lag_sums(buf, chunk, weight_ref, inflow, days):
+    own_days = inflow.shape[0]
+    total = jnp.zeros((days, LANES), F32)
+    parts = [jnp.zeros((8, LANES), F32) for _ in range(2)]
+    for shift in range(8):
+        steps = [k for k in range(shift, LAGS, 8)]
+        shifted = buf[chunk, pl.ds(shift, days + 8 * (len(steps) - 1)), :]
+        for step, lag in enumerate(steps):
+            total = total + weight_ref[0, lag : lag + 1, :] * shifted[8 * step : 8 * step + days]
+            grad = inflow * shifted[8 * step : 8 * step + own_days]
+            grad = sum(grad[i : i + 8] for i in range(0, own_days, 8))
+            parts = [p + weight_ref[1 + w, lag : lag + 1, :] * grad for w, p in enumerate(parts)]
+    return total, jnp.concatenate([jnp.sum(p, axis=0, keepdims=True) for p in parts], axis=0)
 
 
 def lag_sum_forward(buf, chunk, weights_of, days):
@@ -79,15 +95,41 @@
     return totals
 
 
+def fill_weights(shape_ref, scale_ref, weight_ref):
+    @pl.loop(0, shape_ref.shape[0])
+    def _(block):
+        scale_row = scale_ref[block]
+        weights, offsets, logs = lag_weights(shape_ref[block], scale_row)
+        by_shape = weights * (logs - jnp.sum(weights * logs, axis=0, keepdims=True))
+        by_scale = weights * (offsets - jnp.sum(weights * offsets, axis=0, keepdims=True))
+        by_scale = by_scale / (scale_row * scale_row)
+        for chunk in range(2):
+            lanes = slice(chunk * LANES, (chunk + 1) * LANES)
+            for which, rows in enumerate((weights, by_shape, by_scale)):
+                weight_ref[block, chunk, which] = rows[:, lanes]
+
+
 def path_kernel(
-    days, level_ref, part_ref, table_ref, want_ref, want_level_ref, node_ref, weight_ref, comp_ref,
-    order_ref, count_ref, term_ref, buf_ref,
+    days, level_ref, part_ref, down_ref, slot_ref, shape_ref, scale_ref, send_ref, node_ref, weight_ref,
+    comp_ref, reach_weight_ref, order_ref, count_ref, term_ref, buf_ref,
 ):
+    fill_weights(shape_ref, scale_ref, reach_weight_ref)
     list_blocks(level_ref, order_ref, count_ref)
     me = part_ref[0]
-    width = want_ref.shape[1]
-    want = want_ref[...]
-    want_level = want_level_ref[...]
+    width = WIDTH
+    turn = me & 3
+    halves = []
+    for half in range(2):
+        listed = [
+            send_ref[h] if h < SENDS else jnp.full((1, KROWS), -1, jnp.int32)
+            for h in range(4 * half, 4 * half + 4)
+        ]
+        listed = jnp.broadcast_to(jnp.concatenate(listed, axis=1), (8, LANES))
+        halves.append(pltpu.roll(listed, turn * KROWS, 1)[0:1])
+    want = jnp.concatenate(halves, axis=1)
+    lane_id = iota((1, width), 1)
+    want_level = (lane_id >> 7) * 4 + ((((lane_id & (LANES - 1)) >> 5) - turn) & 3)
+    blank = jnp.zeros((4, BLK), F32)
     below = jnp.full((1, width), -1, jnp.int32)
     parent = jnp.full((1, width), -1, jnp.int32)
     rows = iota((BLK, width), 0)
@@ -98,12 +140,25 @@
 
         def gather(index, total, node=node, height=height):
             block = order_ref[height * MAXB + index]
-            hits = jnp.where(rows == node - block * BLK, 1.0, 0.0)
-            return total + jnp.dot(
-                table_ref[block], hits, precision=lax.Precision.HIGHEST, preferred_element_type=F32
+            hits = one_hot(rows == node - block * BLK)
+            table = jnp.concatenate(
+                [
+                    down_ref[block].astype(F32),
+                    slot_ref[block].astype(F32),
+                    shape_ref[block],
+                    scale_ref[block],
+                    blank,
+                ],
+                axis=0,
             )
-
-        found = lax.fori_loop(0, count_ref[height], gather, jnp.zeros((8, width), F32))
+            high = table.astype(BF16)
+            rest = table - high.astype(F32)
+            middle = rest.astype(BF16)
+            low = (rest - middle.astype(F32)).astype(BF16)
+            return total + product(jnp.concatenate([high, middle, low, high * 0], axis=0), hits)
+
+        found = lax.fori_loop(0, count_ref[height], gather, jnp.zeros((32, width), F32))
+        found = (found[0:8] + found[8:16]) + found[16:24]
         active = node >= 0
         down = jnp.round(found[0:1]).astype(jnp.int32)
         slot = jnp.round(found[1:2]).astype(jnp.int32)
@@ -123,12 +178,12 @@
     buf_ref[...] = jnp.zeros(buf_ref.shape, F32)
     first = iota((8, LANES), 0) == 0
     for height in range(1, SENDS):
-        for chunk in range(width // LANES):
+        for chunk in range(height // 4, width // LANES):
             ends = term_ref[height : height + 1, chunk * LANES : (chunk + 1) * LANES] > 0.5
             start = buf_ref[chunk, KROWS : KROWS + 8, :]
             buf_ref[chunk, KROWS : KROWS + 8, :] = jnp.where(first & ends, 1.0, start)
 
-        @pl.loop(0, width // LANES)
+        @pl.loop(height // 4, width // LANES)
         def _(chunk, height=height):
             row = lambda lag: weight_ref[height, chunk, pl.ds(lag, 1), :]
             (total,) = lag_sum_forward(buf_ref, chunk, [row], days)
@@ -138,38 +193,6 @@
         lanes = slice(chunk * LANES, (chunk + 1) * LANES)
         comp_ref[0:days, lanes] = buf_ref[chunk, KROWS : KROWS + days, :]
     comp_ref[days : days + 8, :] = jnp.broadcast_to(parent.astype(F32), (8, width))
-
-
-def weights_kernel(
-    shape_ref, scale_ref, inflow_ref, earlier_ref, weight_ref, grad_ref, buf_ref, two_ref
-):
-    days = inflow_ref.shape[0]
-
-    @pl.loop(0, shape_ref.shape[0])
-    def _(block):
-        scale_row = scale_ref[block]
-        weights, offsets, logs = lag_weights(shape_ref[block], scale_row)
-        by_shape = weights * (logs - jnp.sum(weights * logs, axis=0, keepdims=True))
-        by_scale = weights * (offsets - jnp.sum(weights * offsets, axis=0, keepdims=True))
-        by_scale = by_scale / (scale_row * scale_row)
-        start = pl.multiple_of(block * BLK, BLK)
-        for chunk in range(2):
-            lanes = slice(chunk * LANES, (chunk + 1) * LANES)
-            weight_ref[block, chunk] = weights[:, lanes]
-            two_ref[chunk, 0] = by_shape[:, lanes]
-            two_ref[chunk, 1] = by_scale[:, lanes]
-            at = pl.ds(pl.multiple_of(start + chunk * LANES, LANES), LANES)
-            buf_ref[chunk, 0:days, :] = earlier_ref[:, at]
-            buf_ref[chunk, days : 2 * days, :] = inflow_ref[:, at]
-        for chunk in range(2):
-            rows = [
-                lambda lag, chunk=chunk, which=which: two_ref[chunk, which, pl.ds(lag, 1), :]
-                for which in range(2)
-            ]
-            first, second = lag_sum_forward(buf_ref, chunk, rows, days)
-            lanes = slice(chunk * LANES, (chunk + 1) * LANES)
-            grad_ref[block, 0, :, lanes] = first
-            grad_ref[block, 1, :, lanes] = second
 
 
 def gather_terms(pieces, terms_ref):
@@ -209,7 +232,7 @@
     for chunk in range(2):
         buf_ref[chunk] = jnp.zeros(buf_ref.shape[1:], F32)
 
-        @pl.loop(0, SENDS)
+        @pl.loop(0, min(SENDS, 4 * chunk + 4))
         def _(height, chunk=chunk):
             buf_ref[chunk, 0:days, :] = buf_ref[chunk, 0:days, :] + seed_ref[height, chunk]
             row = lambda lag: weight_ref[height, chunk, pl.ds(lag, 1), :]
@@ -218,26 +241,26 @@
         out_ref[:, chunk * LANES : (chunk + 1) * LANES] = buf_ref[chunk, 0:days, :]
 
 
-def seed_kernel(shards, *refs):
+def seed_kernel(shards, first, *refs):
     pieces = refs[:shards]
     gauge_ref, out_ref, terms_ref = refs[shards:]
     gather_terms(pieces, terms_ref)
 
     @pl.loop(0, out_ref.shape[0])
     def _(block):
-        targets = iota((1, BLK), 1) + block * BLK
+        targets = iota((1, BLK), 1) + (first + block) * BLK
         out_ref[block] = gauge_product(terms_ref, gauge_ref, targets)
 
 
 def full_kernel(
-    own_days, level_ref, part_ref, a_own_ref, a_mate_ref, c_own_ref, c_mate_ref, seed_ref, weight_ref,
-    grad_ref, down_ref, slot_ref, out_ref, param_ref,
+    own_days, level_ref, part_ref, a_own_ref, a_mate_ref, c_own_ref, c_mate_ref, first_seed_ref, last_seed_ref,
+    weight_ref, inflow_ref, down_ref, slot_ref, out_ref, param_ref,
     order_ref, count_ref, recv_ref, comp_ref, parent_buf, adj_ref, lat_ref,
 ):
     list_blocks(level_ref, order_ref, count_ref)
     me = part_ref[0]
     flip = (me >> 2) * LANES
-    days = seed_ref.shape[1]
+    first_blocks, days = first_seed_ref.shape[:2]
     width = 2 * LANES
     groups = iota((1, LANES), 1) >> 5
     rows = iota((BLK, width), 0)
@@ -252,6 +275,9 @@
                 mine = groups == ((height + sender) & 3)
                 total = part if total is None else jnp.where(mine, part, total)
         return total
+
+    def days_of(height):
+        return min(days, -(-(own_days + (LAGS - 1) * (LEVELS - 1 - height)) // 16) * 16)
 
     parent_buf[...] = jnp.zeros(parent_buf.shape, F32)
     for height in range(SENDS):
@@ -265,10 +291,10 @@
             )
             parents = jnp.round(parents).astype(jnp.int32)
             parents = jnp.where(parents >= 0, parents ^ flip, -1)
-            total = jnp.zeros((2 * days, width), F32)
-            for lower in range(height):
-                hits = one_hot(rows == parents - lower * width)
-                total = total + product(recv_ref[lower], hits)
+            hits = jnp.concatenate(
+                [one_hot(rows == parents - lower * width) for lower in range(height)], axis=0
+            )
+            total = product(recv_ref[:, 0 : height * width], hits)
             total = total[:days] + total[days:]
             for half in range(2):
                 parent_buf[half, 0:days, :] = total[:, half * LANES : (half + 1) * LANES]
@@ -277,22 +303,20 @@
         for half in range(2):
             result = merged(a_own_ref, a_mate_ref, height, half, slice(0, days))
             if height:
+                count = days_of(height) // 8
                 tiles = [result[8 * i : 8 * i + 8] for i in range(days // 8)]
                 for shift in range(8):
                     steps = [k for k in range(shift, lags, 8)]
                     for step, lag in enumerate(steps):
                         weight = comp_ref[half, lag : lag + 1, :]
-                        for i in range(days // 8 - step):
+                        for i in range(min(count, days // 8 - step)):
                             at = 8 * (i + step) + shift
                             tiles[i] = tiles[i] + weight * parent_buf[half, at : at + 8, :]
                 result = jnp.concatenate(tiles, axis=0)
             high, low = split_terms(result)
-            lanes = slice(half * LANES, (half + 1) * LANES)
-            recv_ref[height, 0:days, lanes] = high
-            recv_ref[height, days : 2 * days, lanes] = low
-
-    def days_of(height):
-        return min(days, -(-(own_days + (LAGS - 1) * (LEVELS - 1 - height)) // 16) * 16)
+            lanes = slice(height * width + half * LANES, height * width + (half + 1) * LANES)
+            recv_ref[0:days, lanes] = high
+            recv_ref[days : 2 * days, lanes] = low
 
     adj_ref[...] = jnp.zeros(adj_ref.shape, F32)
     for height in range(LEVELS):
@@ -302,64 +326,68 @@
         @pl.loop(0, count_ref[height])
         def _(rank, height=height, need=need, have=have):
             block = order_ref[height * MAXB + rank]
-            adjoint = seed_ref[block, 0:have, :]
+
+            def keep(adjoint):
+                for chunk in range(2):
+                    adj_ref[chunk, 0:have, :] = adjoint[:, chunk * LANES : (chunk + 1) * LANES]
+
+            @pl.when(block < first_blocks)
+            def _():
+                keep(first_seed_ref[block, 0:have, :])
+
+            @pl.when(block >= first_blocks)
+            def _():
+                keep(last_seed_ref[block - first_blocks, 0:have, :])
+
             if height:
                 slot = slot_ref[block]
                 sender = slot >> 2
                 lane = ((sender >> 2) * LANES ^ flip) + ((sender + (height - 1)) & 3) * KROWS
                 lane = jnp.where(slot >= 0, lane + me * 4 + (slot & 3), -1)
-                hits = one_hot(rows == lane)
-                if have == days:
-                    total = product(recv_ref[height - 1], hits)
-                else:
-                    total = jnp.concatenate(
-                        [
-                            product(recv_ref[height - 1, 0:have, :], hits),
-                            product(recv_ref[height - 1, days : days + have, :], hits),
-                        ],
-                        axis=0,
-                    )
                 down = down_ref[block]
-
-                def gather(index, total):
-                    source = order_ref[(height - 1) * MAXB + index]
-                    hits = one_hot(rows == down - source * BLK)
-                    return total + product(lat_ref[source, 0 : 2 * have, :], hits)
-
-                total = lax.fori_loop(0, count_ref[height - 1], gather, total)
-                adjoint = adjoint + total[:have] + total[have:]
-            at = pl.ds(pl.multiple_of(block * BLK, BLK), BLK)
-            param_ref[0:1, at] = jnp.sum(adjoint[:own_days] * grad_ref[block, 0], axis=0, keepdims=True)
-            param_ref[1:2, at] = jnp.sum(adjoint[:own_days] * grad_ref[block, 1], axis=0, keepdims=True)
+                at = slice((height - 1) * width, height * width)
+
+                def gather(sources):
+                    hits = [one_hot(rows == lane)]
+                    for index in range(sources):
+                        source = order_ref[(height - 1) * MAXB + index]
+                        hits.append(one_hot(rows == down - source * BLK))
+                    terms = []
+                    for start, first in ((0, 0), (have, days)):
+                        local = lat_ref[(height - 1) % 2, start : start + have, 0 : sources * BLK]
+                        received = recv_ref[first : first + have, at]
+                        terms.append(jnp.concatenate([received, local], axis=1))
+                    total = product(jnp.concatenate(terms, axis=0), jnp.concatenate(hits, axis=0))
+                    seeds = jnp.concatenate([adj_ref[chunk, 0:have, :] for chunk in range(2)], axis=1)
+                    keep(seeds + total[:have] + total[have:])
+
+                for sources in range(1, MAXB + 1):
+                    pl.when(count_ref[height - 1] == sources)(functools.partial(gather, sources))
             for chunk in range(2):
-                adj_ref[chunk, 0:have, :] = adjoint[:, chunk * LANES : (chunk + 1) * LANES]
-
-            for chunk in range(2):
-                row = lambda lag, chunk=chunk: weight_ref[block, chunk, pl.ds(lag, 1), :]
-                result = lag_sum(adj_ref, chunk, row, need)
                 at = pl.ds(pl.multiple_of(block * BLK + chunk * LANES, LANES), LANES)
+                result, params = lag_sums(adj_ref, chunk, weight_ref.at[block, chunk], inflow_ref[:, at], need)
                 out_ref[:, at] = result[:own_days]
+                param_ref[:, at] = params
                 if height + 1 < LEVELS:
                     high, low = split_terms(result)
-                    lanes = slice(chunk * LANES, (chunk + 1) * LANES)
-                    lat_ref[block, 0:need, lanes] = high
-                    lat_ref[block, need : 2 * need, lanes] = low
-
-
-def call(kernel, out_shape, in_smem, in_vmem, scratch, flops):
+                    lanes = pl.ds(pl.multiple_of(rank * BLK + chunk * LANES, LANES), LANES)
+                    lat_ref[height % 2, 0:need, lanes] = high
+                    lat_ref[height % 2, need : 2 * need, lanes] = low
+
+
+def call(kernel, out_shape, in_smem, in_vmem, scratch, flops, limit=VMEM_LIMIT):
     vmem = pl.BlockSpec(memory_space=pltpu.VMEM)
     smem = pl.BlockSpec(memory_space=pltpu.SMEM)
-    size = lambda leaves: sum(leaf.size * leaf.dtype.itemsize for leaf in leaves)
     return pl.pallas_call(
         kernel,
         out_shape=out_shape,
         in_specs=[smem] * len(in_smem) + [vmem] * len(in_vmem),
         out_specs=jax.tree.map(lambda _: vmem, out_shape),
         scratch_shapes=scratch,
-        compiler_params=pltpu.CompilerParams(vmem_limit_bytes=VMEM_LIMIT),
+        compiler_params=pltpu.CompilerParams(vmem_limit_bytes=limit),
         cost_estimate=pl.CostEstimate(
             flops=flops,
-            bytes_accessed=size(in_vmem) + size(jax.tree.leaves(out_shape)),
+            bytes_accessed=flops // 1000,
             transcendentals=0,
         ),
     )(*in_smem, *in_vmem)
@@ -369,97 +397,130 @@
     return lax.ppermute(values, axis, [(i, i ^ by) for i in range(lax.axis_size(axis))])
 
 
-def over_basin(values):
+def over_basin(values, *before):
     others = [exchange(values, "basin", by) for by in (2, 4, 6)]
-    own = jnp.stack([values] + others)
+    own = after(jnp.stack([values] + others), *before)
     return own, exchange(own, "basin", 1)
+
+
+def over_basin_in_turn(values, before):
+    own = values[None]
+    own = after(jnp.concatenate([own, exchange(own, "basin", 2)], axis=0), before)
+    own = jnp.concatenate([own, exchange(own, "basin", 4)], axis=0)
+    return own, exchange(own, "basin", 1)
+
+
+def gauge_columns(gauge_reach):
+    return jnp.broadcast_to(gauge_reach[:, None], (gauge_reach.shape[0], LANES))
+
+
+def kernel_tables():
+    return [pltpu.SMEM((LEVELS * MAXB,), jnp.int32), pltpu.SMEM((LEVELS,), jnp.int32)]
+
+
+def by_block(values):
+    return values.reshape(-1, 1, BLK)
+
+
+def sent_paths(days, block_level, part, shape_param, scale_param, down_local, in_slot, sends):
+    return call(
+        functools.partial(path_kernel, days),
+        (
+            jax.ShapeDtypeStruct((8, WIDTH), jnp.int32),
+            jax.ShapeDtypeStruct((SENDS, 2, KROWS, LANES), F32),
+            jax.ShapeDtypeStruct((days + 8, WIDTH), F32),
+            jax.ShapeDtypeStruct((block_level.shape[0], 2, 3, KROWS, LANES), F32),
+        ),
+        [block_level, part],
+        [by_block(down_local), by_block(in_slot), by_block(shape_param), by_block(scale_param), sends],
+        kernel_tables()
+        + [pltpu.VMEM((8, WIDTH), F32), pltpu.VMEM((2, KROWS + days, LANES), F32)],
+        1_000_000,
+        56 * 1024 * 1024,
+    )
+
+
+def path_adjoints(pieces, gauge_ids, nodes, path_weights):
+    shards = len(pieces)
+    days = shards * pieces[0].shape[0]
+    return call(
+        functools.partial(path_adjoint_kernel, shards),
+        jax.ShapeDtypeStruct((days, WIDTH), F32),
+        [],
+        pieces + [gauge_ids, nodes, path_weights],
+        [
+            pltpu.VMEM((2 * days, pieces[0].shape[1]), BF16),
+            pltpu.VMEM((SENDS, 2, days, LANES), F32),
+            pltpu.VMEM((2, days + KROWS, LANES), F32),
+        ],
+        4_000_000_000,
+    )
+
+
+def reach_seeds(pieces, gauge_ids, first, end):
+    shards = len(pieces)
+    days = sum(piece.shape[0] for piece in pieces)
+    return call(
+        functools.partial(seed_kernel, shards, first),
+        jax.ShapeDtypeStruct((end - first, days, BLK), F32),
+        [],
+        pieces + [gauge_ids],
+        [pltpu.VMEM((2 * days, pieces[0].shape[1]), BF16)],
+        3_000_000_000,
+    )
+
+
+def all_reaches(inflow, block_level, part, adjoints, composed, first_seeds, last_seeds, weights, down_local, in_slot):
+    own_days = inflow.shape[0]
+    blocks, days = block_level.shape[0], first_seeds.shape[1]
+    reaches = blocks * BLK
+    return call(
+        functools.partial(full_kernel, own_days),
+        (jax.ShapeDtypeStruct((own_days, reaches), F32), jax.ShapeDtypeStruct((2, reaches), F32)),
+        [block_level, part],
+        [*adjoints, *composed, first_seeds, last_seeds, weights, inflow, by_block(down_local), by_block(in_slot)],
+        kernel_tables()
+        + [
+            pltpu.VMEM((2 * days, SENDS * WIDTH), BF16),
+            pltpu.VMEM((2, days, LANES), F32),
+            pltpu.VMEM((2, 2 * days, LANES), F32),
+            pltpu.VMEM((2, days + KROWS, LANES), F32),
+            pltpu.VMEM((2, 2 * days, MAXB * BLK), BF16),
+        ],
+        10_000_000_000,
+    )
+
+
+def after(values, *others):
+    return lax.optimization_barrier((values, *others))[0]
 
 
 def fast_shards(
     inflow, cotangent, gauge_reach, shape_param, scale_param, block_level, down_local, in_slot, send_reach,
 ):
-    own_days, reaches = inflow.shape
-    gauges = cotangent.shape[1]
+    own_days = inflow.shape[0]
     blocks = block_level.shape[0]
     shards = lax.axis_size("tm")
     days = shards * own_days
-    width = 2 * LANES
-    me = lax.axis_index("basin")
-    part = me.astype(jnp.int32).reshape(1)
-    earlier = lax.ppermute(inflow, "tm", [(i, i + 1) for i in range(shards - 1)])
-    pieces = [cotangent] + [
-        lax.ppermute(cotangent, "tm", [(i + by, i) for i in range(shards - by)]) for by in range(1, shards)
-    ]
-    turn = (4 - me % 4) % 4
-    padded = jnp.concatenate([send_reach[0], jnp.full((1, send_reach.shape[2]), -1, jnp.int32)], axis=0)
-    padded = padded.reshape(2, 4, KROWS)
-    padded = jnp.concatenate([padded, padded], axis=1)
-    want = lax.dynamic_slice(padded, (0, turn, 0), (2, 4, KROWS)).reshape(1, width)
-    lane = jnp.arange(width, dtype=jnp.int32)
-    want_level = ((lane // LANES) * 4 + ((lane % LANES) // KROWS + turn) % 4).reshape(1, width)
-    zero = jnp.zeros_like(shape_param)
-    table = jnp.stack(
-        [down_local.astype(F32), in_slot.astype(F32), shape_param, scale_param, zero, zero, zero, zero]
-    )
-    table = table.reshape(8, blocks, BLK).transpose(1, 0, 2)
-    gauge_ids = jnp.broadcast_to(gauge_reach[:, None], (gauges, LANES))
-    by_block = lambda values: values.reshape(blocks, 1, BLK)
-    shape_of = jax.ShapeDtypeStruct
-    tables = [pltpu.SMEM((LEVELS * MAXB,), jnp.int32), pltpu.SMEM((LEVELS,), jnp.int32)]
-
-    nodes, path_weights, composed = call(
-        functools.partial(path_kernel, days),
-        (
-            shape_of((8, width), jnp.int32),
-            shape_of((SENDS, 2, KROWS, LANES), F32),
-            shape_of((days + 8, width), F32),
-        ),
-        [block_level, part],
-        [table, want, want_level],
-        tables + [pltpu.VMEM((8, width), F32), pltpu.VMEM((2, KROWS + days, LANES), F32)],
-        8_000_000_000,
-    )
-    c_own, c_mate = over_basin(composed)
-    weights, grads = call(
-        weights_kernel,
-        (shape_of((blocks, 2, KROWS, LANES), F32), shape_of((blocks, 2, own_days, BLK), F32)),
-        [],
-        [by_block(shape_param), by_block(scale_param), inflow, earlier],
-        [pltpu.VMEM((2, 2 * own_days, LANES), F32), pltpu.VMEM((2, 2, KROWS, LANES), F32)],
-        4_000_000_000,
-    )
-    terms = pltpu.VMEM((2 * days, gauges), BF16)
-    path_adjoint = call(
-        functools.partial(path_adjoint_kernel, shards),
-        shape_of((days, width), F32),
-        [],
-        pieces + [gauge_ids, nodes, path_weights],
-        [terms, pltpu.VMEM((SENDS, 2, days, LANES), F32), pltpu.VMEM((2, days + KROWS, LANES), F32)],
-        4_000_000_000,
-    )
-    a_own, a_mate = over_basin(path_adjoint)
-    seeds = call(
-        functools.partial(seed_kernel, shards),
-        shape_of((blocks, days, BLK), F32),
-        [],
-        pieces + [gauge_ids],
-        [terms],
-        6_000_000_000,
-    )
-    lateral, params = call(
-        functools.partial(full_kernel, own_days),
-        (shape_of((own_days, reaches), F32), shape_of((2, reaches), F32)),
-        [block_level, part],
-        [a_own, a_mate, c_own, c_mate, seeds, weights, grads, by_block(down_local), by_block(in_slot)],
-        tables
-        + [
-            pltpu.VMEM((SENDS, 2 * days, width), BF16),
-            pltpu.VMEM((2, days, LANES), F32),
-            pltpu.VMEM((2, 2 * days, LANES), F32),
-            pltpu.VMEM((2, days + KROWS, LANES), F32),
-            pltpu.VMEM((blocks, 2 * days, BLK), BF16),
-        ],
-        10_000_000_000,
+    part = lax.axis_index("basin").astype(jnp.int32).reshape(1)
+    nodes, path_weights, composed, weights = sent_paths(
+        days, block_level, part, shape_param, scale_param, down_local, in_slot, send_reach.reshape(SENDS, 1, KROWS)
+    )
+    back = lambda by, reach: [(i + by, i) for i in range(shards - reach)]
+    following = lax.ppermute(cotangent, "tm", back(1, 1))
+    following, composed = lax.optimization_barrier((following, composed, nodes))[:2]
+    second = lax.ppermute(following, "tm", back(1, 2))
+    third = lax.ppermute(following, "tm", back(2, 3))
+    gauge_ids = gauge_columns(gauge_reach)
+    composed = over_basin_in_turn(composed, after(second, gauge_ids))
+    third, second, nodes, gauge_ids = lax.optimization_barrier((third, second, nodes, gauge_ids))
+    pieces = [cotangent, following, second, third]
+    adjoints = path_adjoints(pieces, gauge_ids, nodes, path_weights)
+    first_seeds = reach_seeds(pieces, gauge_ids, 0, blocks // 2)
+    adjoints = over_basin(adjoints, first_seeds)
+    last_seeds = reach_seeds(after(pieces, adjoints[0]), gauge_ids, blocks // 2, blocks)
+    lateral, params = all_reaches(
+        inflow, block_level, part, adjoints, composed, first_seeds, last_seeds, weights, down_local, in_slot
     )
     first, second, third = (exchange(params, "tm", by) for by in (1, 2, 3))
     return lateral, (params + first) + (second + third)

time: 97.4 us -> 72.2 us (0.74)
  Pallas kernels: 53.1 us -> 35.7 us
  starting transfers between devices: 25.8 us -> 15.5 us
  waiting for transfers between devices: 7.22 us -> 16.5 us
  local copies, waits for them, and re-layouts: 5.98 us -> 1.06 us
  other arithmetic: 4.52 us -> 1.65 us
    pallas_call x5, Pallas kernels: 53.1 us -> 35.7 us  [call(): pl.pallas_call(kernel, out_shape=out_shape, in_specs=[smem] * len(in_smem...]
    ppermute x4 -> x3, starting transfers between devices: 11.9 us -> 4 us  [the longest x1 1.42 us: fast_shards(): following = lax.ppermute(cotangent, 'tm', back(1, 1))]
    ppermute x4 -> x3, waiting for transfers between devices: 3.08 us -> 8.69 us  [the longest x1 3.82 us: fast_shards(): second = lax.ppermute(following, 'tm', back(1, 2))]
    ppermute x11 -> x10, waiting for transfers between devices: 4.14 us -> 7.85 us  [exchange(): lax.ppermute(values, axis, [(i, i ^ by) for i in range(lax.axis_size(axis...]
    ppermute x11 -> x10, starting transfers between devices: 14 us -> 11.5 us  [exchange(): lax.ppermute(values, axis, [(i, i ^ by) for i in range(lax.axis_size(axis...]
    unnamed x23 -> x16, local copies, waits for them, and re-layouts: 2.46 us -> 0.04 us
    another operation x2 -> x0, local copies, waits for them, and re-layouts: 1.51 us -> none  [fast_shards(): jnp.stack([down_local.astype(F32), in_slot.astype(F32), shape_param, scal...]
    convert_element_type x2 -> x0, other arithmetic: 1.44 us -> none  [the longest x1 0.72 us: fast_shards(): down_local.astype(F32)]
  transfers between devices with their start and end apart: 15 -> 13, of which waited for: 4 -> 7; matrix products, arithmetic and copies ran while one was open for 8% -> 3% of each run, Pallas kernels for 32% -> 27%
where the time goes in v1:
time: 72.2 us; the launch traced here: 71.4 us
  Pallas kernels  35.7 us (49%)
  waiting for transfers between devices  16.5 us (23%)
  starting transfers between devices  15.5 us (21%)
  other arithmetic  1.65 us (2%)
  local copies, waits for them, and re-layouts  1.06 us (1%)
  between operations  0.88 us (1%)
    pallas_call x5, Pallas kernels, call(): pl.pallas_call(kernel, out_shape=out_shape, in_specs=[smem] * len(in_smem...  35.7 us
    ppermute x10, starting transfers between devices, exchange(): lax.ppermute(values, axis, [(i, i ^ by) for i in range(lax.axis_size(axis...  11.5 us
    ppermute x10, waiting for transfers between devices, exchange(): lax.ppermute(values, axis, [(i, i ^ by) for i in range(lax.axis_size(axis...  7.85 us
    ppermute x1, waiting for transfers between devices, fast_shards(): second = lax.ppermute(following, 'tm', back(1, 2))  3.82 us
    ppermute x1, waiting for transfers between devices, fast_shards(): following = lax.ppermute(cotangent, 'tm', back(1, 1))  3.39 us
    ppermute x1, waiting for transfers between devices, fast_shards(): third = lax.ppermute(following, 'tm', back(2, 3))  1.48 us
  transfers between devices with their start and end apart: 13, of which 7 were waited for; matrix products, arithmetic and copies ran while one was open for 3% of the time, Pallas kernels for 27%

profile of v1, /device:TPU:0, one launch (start us, length us, event | category | flops | bytes accessed | tf_op | source)
XLA Modules:
  0.0 71.4 jit_solution(11856950072298550308)
XLA Ops:
  0.6 0.0 copy-start.5
  0.6 1.4 %collective-permute-start = (f32[32,2048]{1,0:T(8,128)}, f32[32,2048]{1,0:T(8,128)S(1)}, u32[]{:S(2)}, u32[]{:S(2)}) collective-permute-start(f32[32,2048]{1,0:T(8,128)} %refs_0_.4), channel_id=1, source_target_pairs={{1,0},{2,1},{3,2},{5,4},{6,5},{7,6},{9,8},{10,9},{11,10},{13,12},{... | collective-permute-start | bytes 786440 | tf_op jit(solution)/shard_map/ppermute | solution.py:510
  2.1 6.7 %shard_map.104 = (s32[8,256]{1,0:T(8,128)}, f32[7,2,32,128]{3,2,1,0:T(8,128)}, f32[136,256]{1,0:T(8,128)}, f32[16,2,3,32,128]{4,3,2,1,0:T(8,128)}) custom-call(s32[16]{0:T(128)} %level_ref.3, s32[1]{0:T(128)} %bitcast.part_ref, s32[16,1,256]{2,1,0:T(1,128)} %bitcast.12, s32[16,1,256]{2,1,0:T(1,128)} %bitcast.14, f32[16,1,256]{2,1,0:T(1,128)} %bitcast.21, ...), custom_call_target="tpu_custom_call" | custom-call | flops 1000000 | bytes 1000 | tf_op jit(solution)/shard_map/pallas_call | solution.py:381
  8.8 0.0 copy-start.6
  8.8 0.0 copy-start.7
  8.8 3.4 %collective-permute-done.refs_1_ = f32[32,2048]{1,0:T(8,128)S(1)} collective-permute-done((f32[32,2048]{1,0:T(8,128)}, f32[32,2048]{1,0:T(8,128)S(1)}, u32[]{:S(2)}, u32[]{:S(2)}) %collective-permute-start) | collective-permute-done | bytes 262176 | tf_op jit(solution)/shard_map/ppermute | solution.py:510
  12.2 1.3 %collective-permute-start.1 = (f32[32,2048]{1,0:T(8,128)S(1)}, f32[32,2048]{1,0:T(8,128)S(1)}, u32[]{:S(2)}, u32[]{:S(2)}) collective-permute-start(f32[32,2048]{1,0:T(8,128)S(1)} %collective-permute-done.refs_1_), channel_id=1, source_target_pairs={{2,0},{6,4},{10,8},{14,12},{18,16},{22,20},{26,24},{30,28}} | collective-permute-start | bytes 786440 | tf_op jit(solution)/shard_map/ppermute | solution.py:513
  13.5 1.3 %collective-permute-start.2 = (f32[32,2048]{1,0:T(8,128)S(1)}, f32[32,2048]{1,0:T(8,128)S(1)}, u32[]{:S(2)}, u32[]{:S(2)}) collective-permute-start(f32[32,2048]{1,0:T(8,128)S(1)} %collective-permute-done.refs_1_), channel_id=1, source_target_pairs={{1,0},{2,1},{5,4},{6,5},{9,8},{10,9},{13,12},{14,13},{17,16},{18,1... | collective-permute-start | bytes 786440 | tf_op jit(solution)/shard_map/ppermute | solution.py:512
  14.8 1.7 %collective-permute-start.7 = (f32[1,136,256]{2,1,0:T(8,128)}, f32[1,136,256]{2,1,0:T(8,128)S(1)}, u32[]{:S(2)}, u32[]{:S(2)}) collective-permute-start(f32[1,136,256]{2,1,0:T(8,128)} %bitcast.16), channel_id=1, source_target_pairs={{0,8},{4,12},{8,0},{12,4},{16,24},{20,28},{24,16},{28,20},{1,9},{5... | collective-permute-start | bytes 417800 | tf_op jit(solution)/shard_map/ppermute | solution.py:397
  16.5 3.6 %collective-permute-done.7 = f32[1,136,256]{2,1,0:T(8,128)S(1)} collective-permute-done((f32[1,136,256]{2,1,0:T(8,128)}, f32[1,136,256]{2,1,0:T(8,128)S(1)}, u32[]{:S(2)}, u32[]{:S(2)}) %collective-permute-start.7) | collective-permute-done | bytes 139296 | tf_op jit(solution)/shard_map/ppermute | solution.py:397
  20.1 0.9 %pad_maximum_fusion.2 = f32[2,136,256]{2,1,0:T(8,128)S(1)} fusion(f32[1,136,256]{2,1,0:T(8,128)S(1)} %collective-permute-done.7, f32[1,136,256]{2,1,0:T(8,128)} %bitcast.17), kind=kLoop, calls=%fused_computation.2 | loop fusion | flops 69632 | bytes 557056 | tf_op jit(solution)/shard_map/concatenate | solution.py:408
  21.1 1.7 %collective-permute-start.8 = (f32[2,136,256]{2,1,0:T(8,128)S(1)}, f32[2,136,256]{2,1,0:T(8,128)S(1)}, u32[]{:S(2)}, u32[]{:S(2)}) collective-permute-start(f32[2,136,256]{2,1,0:T(8,128)S(1)} %pad_maximum_fusion.2), channel_id=1, source_target_pairs={{0,16},{4,20},{8,24},{12,28},{16,0},{20,4},{24,8},{28,12},{1,17},{... | collective-permute-start | bytes 835592 | tf_op jit(solution)/shard_map/ppermute | solution.py:397
  22.8 1.5 %collective-permute-done.1.refs_3_ = f32[32,2048]{1,0:T(8,128)S(1)} collective-permute-done((f32[32,2048]{1,0:T(8,128)S(1)}, f32[32,2048]{1,0:T(8,128)S(1)}, u32[]{:S(2)}, u32[]{:S(2)}) %collective-permute-start.1) | collective-permute-done | bytes 262176 | tf_op jit(solution)/shard_map/ppermute | solution.py:513
  24.3 3.8 %collective-permute-done.2.refs_2_ = f32[32,2048]{1,0:T(8,128)S(1)} collective-permute-done((f32[32,2048]{1,0:T(8,128)S(1)}, f32[32,2048]{1,0:T(8,128)S(1)}, u32[]{:S(2)}, u32[]{:S(2)}) %collective-permute-start.2) | collective-permute-done | bytes 262176 | tf_op jit(solution)/shard_map/ppermute | solution.py:512
  28.1 1.0 %broadcast_in_dim.4.refs_4_ = s32[2048,128]{1,0:T(8,128)S(1)} broadcast(s32[2048]{0:T(1024)} %param.11), dimensions={0} | broadcast | bytes 1056768 | tf_op jit(solution)/shard_map/broadcast_in_dim | solution.py:414
  29.1 0.0 copy-done.5
  29.1 0.0 copy-done.6
  29.2 0.0 copy-done.7
  29.2 4.8 %shard_map.105 = f32[128,256]{1,0:T(8,128)S(1)} custom-call(f32[32,2048]{1,0:T(8,128)S(1)} %copy-done.5, f32[32,2048]{1,0:T(8,128)S(1)} %collective-permute-done.refs_1_, f32[32,2048]{1,0:T(8,128)S(1)} %collective-permute-done.2.refs_2_, f32[32,2048]{1,0:T(8,128)S(1)} %collective-permute-done.1.refs_3_, s32[2048,128]{1,0:T(8,128)S(1)} %broadcast_in_dim.4.refs_4_, ...), custom_call_target="tpu_custom_call" | custom-call | flops 4000000000 | bytes 4000000 | tf_op jit(solution)/shard_map/pallas_call | solution.py:381
  34.0 1.4 %collective-permute-start.3 = (f32[128,256]{1,0:T(8,128)S(1)}, f32[128,256]{1,0:T(8,128)S(1)}, u32[]{:S(2)}, u32[]{:S(2)}) collective-permute-start(f32[128,256]{1,0:T(8,128)S(1)} %shard_map.105), channel_id=1, source_target_pairs={{0,8},{4,12},{8,0},{12,4},{16,24},{20,28},{24,16},{28,20},{1,9},{5... | collective-permute-start | bytes 393224 | tf_op jit(solution)/shard_map/ppermute | solution.py:397
  35.4 1.5 %collective-permute-start.4 = (f32[128,256]{1,0:T(8,128)S(1)}, f32[128,256]{1,0:T(8,128)S(1)}, u32[]{:S(2)}, u32[]{:S(2)}) collective-permute-start(f32[128,256]{1,0:T(8,128)S(1)} %shard_map.105), channel_id=1, source_target_pairs={{0,16},{4,20},{8,24},{12,28},{16,0},{20,4},{24,8},{28,12},{1,17},{... | collective-permute-start | bytes 393224 | tf_op jit(solution)/shard_map/ppermute | solution.py:397
  36.9 0.6 collective-permute-start.5
  37.6 3.7 %shard_map.106.first_seed_ref = f32[8,128,256]{2,1,0:T(8,128)S(1)} custom-call(f32[32,2048]{1,0:T(8,128)S(1)} %copy-done.5, f32[32,2048]{1,0:T(8,128)S(1)} %collective-permute-done.refs_1_, f32[32,2048]{1,0:T(8,128)S(1)} %collective-permute-done.2.refs_2_, f32[32,2048]{1,0:T(8,128)S(1)} %collective-permute-done.1.refs_3_, ...), custom_call_target="tpu_custom_call" | custom-call | flops 3000000000 | bytes 3000000 | tf_op jit(solution)/shard_map/pallas_call | solution.py:381
  41.3 0.0 collective-permute-done.8
  41.3 0.1 collective-permute-start.9
  41.4 0.0 collective-permute-done.3
  41.4 1.9 %collective-permute-done.4 = f32[128,256]{1,0:T(8,128)S(1)} collective-permute-done((f32[128,256]{1,0:T(8,128)S(1)}, f32[128,256]{1,0:T(8,128)S(1)}, u32[]{:S(2)}, u32[]{:S(2)}) %collective-permute-start.4) | collective-permute-done | bytes 131104 | tf_op jit(solution)/shard_map/ppermute | solution.py:397
  43.3 0.0 collective-permute-done.5
  43.4 0.0 copy-start
  43.4 0.0 copy-start.1
  43.4 0.0 copy-start.2
  43.4 0.0 copy-start.3
  43.4 0.0 copy-start.4
  43.5 0.1 collective-permute-start.6
  43.5 3.7 %shard_map.107.last_seed_ref = f32[8,128,256]{2,1,0:T(8,128)S(1)} custom-call(f32[32,2048]{1,0:T(8,128)S(1)} %copy-done.5, f32[32,2048]{1,0:T(8,128)S(1)} %collective-permute-done.refs_1_, f32[32,2048]{1,0:T(8,128)S(1)} %collective-permute-done.2.refs_2_, f32[32,2048]{1,0:T(8,128)S(1)} %collective-permute-done.1.refs_3_, s32[2048,128]{1,0:T(8,128)S(1)} %broadcast_in_dim.4.refs_4_), custom_call_target="tpu_custom_call" | custom-call | flops 3000000000 | bytes 3000000 | tf_op jit(solution)/shard_map/pallas_call | solution.py:381
  47.2 0.0 collective-permute-done.6.a_mate_ref
  47.3 0.0 collective-permute-done.9.c_mate_ref
  47.3 0.0 copy-done
  47.3 0.0 copy-done.1
  47.3 0.0 copy-done.2
  47.3 0.0 copy-done.3
  47.3 0.0 copy-done.4
  47.3 16.7 %shard_map.108 = (f32[32,4096]{1,0:T(8,128)}, f32[2,4096]{1,0:T(2,128)S(1)}) custom-call(s32[16]{0:T(128)S(1)} %copy-done.2, s32[1]{0:T(128)} %bitcast.part_ref, f32[4,128,256]{2,1,0:T(8,128)S(1)} %pad_maximum_fusion.1.a_own_ref, f32[4,128,256]{2,1,0:T(8,128)S(1)} %collective-permute-done.6.a_mate_ref, f32[4,136,256]{2,1,0:T(8,128)S(1)} %pad_maximum_fusion.c_own_ref, ...), custom_call_target="tpu_custom_call" | custom-call | flops 10000000000 | bytes 10000000 | tf_op jit(solution)/shard_map/pallas_call | solution.py:381
  64.0 0.3 collective-permute-start.10
  64.3 0.0 collective-permute-start.11
  64.4 4.1 %collective-permute-start.12 = (f32[2,4096]{1,0:T(2,128)S(1)}, f32[2,4096]{1,0:T(2,128)S(1)}, u32[]{:S(2)}, u32[]{:S(2)}) collective-permute-start(f32[2,4096]{1,0:T(2,128)S(1)} %get-tuple-element.35), channel_id=1, source_target_pairs={{0,3},{1,2},{2,1},{3,0},{4,7},{5,6},{6,5},{7,4},{8,11},{9,10},{10,... | collective-permute-start | bytes 98312 | tf_op jit(solution)/shard_map/ppermute | solution.py:397
  68.4 0.0 collective-permute-done.10
  68.4 0.7 %collective-permute-done.11 = f32[2,4096]{1,0:T(2,128)S(1)} collective-permute-done((f32[2,4096]{1,0:T(2,128)S(1)}, f32[2,4096]{1,0:T(2,128)S(1)}, u32[]{:S(2)}, u32[]{:S(2)}) %collective-permute-start.11) | collective-permute-done | bytes 32800 | tf_op jit(solution)/shard_map/ppermute | solution.py:397
  69.2 1.6 %collective-permute-done.12 = f32[2,4096]{1,0:T(2,128)S(1)} collective-permute-done((f32[2,4096]{1,0:T(2,128)S(1)}, f32[2,4096]{1,0:T(2,128)S(1)}, u32[]{:S(2)}, u32[]{:S(2)}) %collective-permute-start.12) | collective-permute-done | bytes 32800 | tf_op jit(solution)/shard_map/ppermute | solution.py:397
  70.7 0.6 add_add_fusion
  (2 shorter events, 0.1 us)
Async XLA Ops:
  0.6 28.5 %copy-start.5 = (f32[32,2048]{1,0:T(8,128)S(1)}, f32[32,2048]{1,0:T(8,128)}, u32[]{:S(2)}) copy-start(f32[32,2048]{1,0:T(8,128)} %refs_0_.4) | copy-start | bytes 786436
  0.6 11.6 %collective-permute-start = (f32[32,2048]{1,0:T(8,128)}, f32[32,2048]{1,0:T(8,128)S(1)}, u32[]{:S(2)}, u32[]{:S(2)}) collective-permute-start(f32[32,2048]{1,0:T(8,128)} %refs_0_.4), channel_id=1, source_target_pairs={{1,0},{2,1},{3,2},{5,4},{6,5},{7,6},{9,8},{10,9},{11,10},{13,12},{... | collective-permute-start | bytes 786440 | tf_op jit(solution)/shard_map/ppermute | solution.py:510
  8.8 20.3 %copy-start.6 = (f32[7,2,32,128]{3,2,1,0:T(8,128)S(1)}, f32[7,2,32,128]{3,2,1,0:T(8,128)}, u32[]{:S(2)}) copy-start(f32[7,2,32,128]{3,2,1,0:T(8,128)} %get-tuple-element.26.refs_6_) | copy-start | bytes 688132
  8.8 20.3 %copy-start.7 = (s32[8,256]{1,0:T(8,128)S(1)}, s32[8,256]{1,0:T(8,128)}, u32[]{:S(2)}) copy-start(s32[8,256]{1,0:T(8,128)} %get-tuple-element.25.refs_5_) | copy-start | bytes 24580
  12.2 12.1 %collective-permute-start.1 = (f32[32,2048]{1,0:T(8,128)S(1)}, f32[32,2048]{1,0:T(8,128)S(1)}, u32[]{:S(2)}, u32[]{:S(2)}) collective-permute-start(f32[32,2048]{1,0:T(8,128)S(1)} %collective-permute-done.refs_1_), channel_id=1, source_target_pairs={{2,0},{6,4},{10,8},{14,12},{18,16},{22,20},{26,24},{30,28}} | collective-permute-start | bytes 786440 | tf_op jit(solution)/shard_map/ppermute | solution.py:513
  13.5 14.6 %collective-permute-start.2 = (f32[32,2048]{1,0:T(8,128)S(1)}, f32[32,2048]{1,0:T(8,128)S(1)}, u32[]{:S(2)}, u32[]{:S(2)}) collective-permute-start(f32[32,2048]{1,0:T(8,128)S(1)} %collective-permute-done.refs_1_), channel_id=1, source_target_pairs={{1,0},{2,1},{5,4},{6,5},{9,8},{10,9},{13,12},{14,13},{17,16},{18,1... | collective-permute-start | bytes 786440 | tf_op jit(solution)/shard_map/ppermute | solution.py:512
  14.8 5.3 %collective-permute-start.7 = (f32[1,136,256]{2,1,0:T(8,128)}, f32[1,136,256]{2,1,0:T(8,128)S(1)}, u32[]{:S(2)}, u32[]{:S(2)}) collective-permute-start(f32[1,136,256]{2,1,0:T(8,128)} %bitcast.16), channel_id=1, source_target_pairs={{0,8},{4,12},{8,0},{12,4},{16,24},{20,28},{24,16},{28,20},{1,9},{5... | collective-permute-start | bytes 417800 | tf_op jit(solution)/shard_map/ppermute | solution.py:397
  21.1 20.2 %collective-permute-start.8 = (f32[2,136,256]{2,1,0:T(8,128)S(1)}, f32[2,136,256]{2,1,0:T(8,128)S(1)}, u32[]{:S(2)}, u32[]{:S(2)}) collective-permute-start(f32[2,136,256]{2,1,0:T(8,128)S(1)} %pad_maximum_fusion.2), channel_id=1, source_target_pairs={{0,16},{4,20},{8,24},{12,28},{16,0},{20,4},{24,8},{28,12},{1,17},{... | collective-permute-start | bytes 835592 | tf_op jit(solution)/shard_map/ppermute | solution.py:397
  34.0 7.4 %collective-permute-start.3 = (f32[128,256]{1,0:T(8,128)S(1)}, f32[128,256]{1,0:T(8,128)S(1)}, u32[]{:S(2)}, u32[]{:S(2)}) collective-permute-start(f32[128,256]{1,0:T(8,128)S(1)} %shard_map.105), channel_id=1, source_target_pairs={{0,8},{4,12},{8,0},{12,4},{16,24},{20,28},{24,16},{28,20},{1,9},{5... | collective-permute-start | bytes 393224 | tf_op jit(solution)/shard_map/ppermute | solution.py:397
  35.4 7.9 %collective-permute-start.4 = (f32[128,256]{1,0:T(8,128)S(1)}, f32[128,256]{1,0:T(8,128)S(1)}, u32[]{:S(2)}, u32[]{:S(2)}) collective-permute-start(f32[128,256]{1,0:T(8,128)S(1)} %shard_map.105), channel_id=1, source_target_pairs={{0,16},{4,20},{8,24},{12,28},{16,0},{20,4},{24,8},{28,12},{1,17},{... | collective-permute-start | bytes 393224 | tf_op jit(solution)/shard_map/ppermute | solution.py:397
  36.9 6.4 %collective-permute-start.5 = (f32[128,256]{1,0:T(8,128)S(1)}, f32[128,256]{1,0:T(8,128)S(1)}, u32[]{:S(2)}, u32[]{:S(2)}) collective-permute-start(f32[128,256]{1,0:T(8,128)S(1)} %shard_map.105), channel_id=1, source_target_pairs={{0,24},{4,28},{8,16},{12,20},{16,8},{20,12},{24,0},{28,4},{1,25},{... | collective-permute-start | bytes 393224 | tf_op jit(solution)/shard_map/ppermute | solution.py:397
  41.3 5.9 %collective-permute-start.9 = (f32[4,136,256]{2,1,0:T(8,128)S(1)}, f32[4,136,256]{2,1,0:T(8,128)S(1)}, u32[]{:S(2)}, u32[]{:S(2)}) collective-permute-start(f32[4,136,256]{2,1,0:T(8,128)S(1)} %pad_maximum_fusion.c_own_ref), channel_id=1, source_target_pairs={{0,4},{4,0},{8,12},{12,8},{16,20},{20,16},{24,28},{28,24},{1,5},{5... | collective-permute-start | bytes 1671176 | tf_op jit(solution)/shard_map/ppermute | solution.py:397
  43.4 3.9 %copy-start = (s32[4096]{0:T(1024)S(1)}, s32[4096]{0:T(1024)}, u32[]{:S(2)}) copy-start(s32[4096]{0:T(1024)} %param.15) | copy-start | bytes 49156
  43.4 3.9 %copy-start.1 = (s32[4096]{0:T(1024)S(1)}, s32[4096]{0:T(1024)}, u32[]{:S(2)}) copy-start(s32[4096]{0:T(1024)} %param.16) | copy-start | bytes 49156
  43.4 3.9 %copy-start.2 = (s32[16]{0:T(128)S(1)}, s32[16]{0:T(128)}, u32[]{:S(2)}) copy-start(s32[16]{0:T(128)} %level_ref.3) | copy-start | bytes 196
  43.4 3.9 %copy-start.3 = (f32[16,2,3,32,128]{4,3,2,1,0:T(8,128)S(1)}, f32[16,2,3,32,128]{4,3,2,1,0:T(8,128)}, u32[]{:S(2)}) copy-start(f32[16,2,3,32,128]{4,3,2,1,0:T(8,128)} %get-tuple-element.33.weight_ref) | copy-start | bytes 4718596
  43.4 3.9 %copy-start.4 = (f32[32,4096]{1,0:T(8,128)S(1)}, f32[32,4096]{1,0:T(8,128)}, u32[]{:S(2)}) copy-start(f32[32,4096]{1,0:T(8,128)} %inflow_ref.1) | copy-start | bytes 1572868
  43.5 3.8 %collective-permute-start.6 = (f32[4,128,256]{2,1,0:T(8,128)S(1)}, f32[4,128,256]{2,1,0:T(8,128)S(1)}, u32[]{:S(2)}, u32[]{:S(2)}) collective-permute-start(f32[4,128,256]{2,1,0:T(8,128)S(1)} %pad_maximum_fusion.1.a_own_ref), channel_id=1, source_target_pairs={{0,4},{4,0},{8,12},{12,8},{16,20},{20,16},{24,28},{28,24},{1,5},{5... | collective-permute-start | bytes 1572872 | tf_op jit(solution)/shard_map/ppermute | solution.py:397
  64.0 4.4 %collective-permute-start.10 = (f32[2,4096]{1,0:T(2,128)S(1)}, f32[2,4096]{1,0:T(2,128)S(1)}, u32[]{:S(2)}, u32[]{:S(2)}) collective-permute-start(f32[2,4096]{1,0:T(2,128)S(1)} %get-tuple-element.35), channel_id=1, source_target_pairs={{0,1},{1,0},{2,3},{3,2},{4,5},{5,4},{6,7},{7,6},{8,9},{9,8},{10,11... | collective-permute-start | bytes 98312 | tf_op jit(solution)/shard_map/ppermute | solution.py:397
  64.3 4.8 %collective-permute-start.11 = (f32[2,4096]{1,0:T(2,128)S(1)}, f32[2,4096]{1,0:T(2,128)S(1)}, u32[]{:S(2)}, u32[]{:S(2)}) collective-permute-start(f32[2,4096]{1,0:T(2,128)S(1)} %get-tuple-element.35), channel_id=1, source_target_pairs={{0,2},{1,3},{2,0},{3,1},{4,6},{5,7},{6,4},{7,5},{8,10},{9,11},{10,... | collective-permute-start | bytes 98312 | tf_op jit(solution)/shard_map/ppermute | solution.py:397
  64.4 6.4 %collective-permute-start.12 = (f32[2,4096]{1,0:T(2,128)S(1)}, f32[2,4096]{1,0:T(2,128)S(1)}, u32[]{:S(2)}, u32[]{:S(2)}) collective-permute-start(f32[2,4096]{1,0:T(2,128)S(1)} %get-tuple-element.35), channel_id=1, source_target_pairs={{0,3},{1,2},{2,1},{3,0},{4,7},{5,6},{6,5},{7,4},{8,11},{9,10},{10,... | collective-permute-start | bytes 98312 | tf_op jit(solution)/shard_map/ppermute | solution.py:397

commit v2 on v1

--- a/solution.py
+++ b/solution.py
@@ -18,6 +18,7 @@
 F32 = jnp.float32
 BF16 = jnp.bfloat16
 VMEM_LIMIT = 20 * 1024 * 1024
+JOINT = 4
 
 
 def iota(shape, axis):
@@ -66,21 +67,6 @@
         for step, lag in enumerate(steps):
             total = total + weight_of(lag) * shifted[8 * step : 8 * step + days]
     return total
-
-
-def lag_sums(buf, chunk, weight_ref, inflow, days):
-    own_days = inflow.shape[0]
-    total = jnp.zeros((days, LANES), F32)
-    parts = [jnp.zeros((8, LANES), F32) for _ in range(2)]
-    for shift in range(8):
-        steps = [k for k in range(shift, LAGS, 8)]
-        shifted = buf[chunk, pl.ds(shift, days + 8 * (len(steps) - 1)), :]
-        for step, lag in enumerate(steps):
-            total = total + weight_ref[0, lag : lag + 1, :] * shifted[8 * step : 8 * step + days]
-            grad = inflow * shifted[8 * step : 8 * step + own_days]
-            grad = sum(grad[i : i + 8] for i in range(0, own_days, 8))
-            parts = [p + weight_ref[1 + w, lag : lag + 1, :] * grad for w, p in enumerate(parts)]
-    return total, jnp.concatenate([jnp.sum(p, axis=0, keepdims=True) for p in parts], axis=0)
 
 
 def lag_sum_forward(buf, chunk, weights_of, days):
@@ -110,7 +96,7 @@
 
 
 def path_kernel(
-    days, level_ref, part_ref, down_ref, slot_ref, shape_ref, scale_ref, send_ref, node_ref, weight_ref,
+    days, level_ref, part_ref, down_ref, slot_ref, shape_ref, scale_ref, send_ref, weight_ref,
     comp_ref, reach_weight_ref, order_ref, count_ref, term_ref, buf_ref,
 ):
     fill_weights(shape_ref, scale_ref, reach_weight_ref)
@@ -134,7 +120,6 @@
     parent = jnp.full((1, width), -1, jnp.int32)
     rows = iota((BLK, width), 0)
     krows = iota((KROWS, width), 0)
-    node_ref[...] = jnp.full(node_ref.shape, -1, jnp.int32)
     for height in range(SENDS - 1, -1, -1):
         node = jnp.where((want_level == height) & (want >= 0), want, below)
 
@@ -171,7 +156,7 @@
         parent = jnp.where(ends, (height - 1) * width + lane, parent)
         weights = lag_weights(shape_row, scale_row)[0]
         weights = jnp.where(active, weights, jnp.where(krows == 0, 1.0, 0.0))
-        node_ref[height : height + 1, :] = node
+        weights = jnp.where(krows == KROWS - 1, node.astype(F32), weights)
         term_ref[height : height + 1, :] = jnp.where(ends, 1.0, 0.0)
         for chunk in range(width // LANES):
             weight_ref[height, chunk] = weights[:, chunk * LANES : (chunk + 1) * LANES]
@@ -195,37 +180,57 @@
     comp_ref[days : days + 8, :] = jnp.broadcast_to(parent.astype(F32), (8, width))
 
 
+def grad_kernel(inflow_ref, weight_ref, grad_ref, buf_ref):
+    days = inflow_ref.shape[0]
+    buf_ref[...] = jnp.zeros(buf_ref.shape, F32)
+
+    @pl.loop(0, weight_ref.shape[0])
+    def _(block):
+        for chunk in range(2):
+            lanes = slice(chunk * LANES, (chunk + 1) * LANES)
+            at = pl.ds(pl.multiple_of(block * BLK + chunk * LANES, LANES), LANES)
+            buf_ref[chunk, KROWS : KROWS + days, :] = inflow_ref[:, at]
+            rows = [
+                lambda lag, chunk=chunk, which=which: weight_ref[block, chunk, which, lag : lag + 1, :]
+                for which in (1, 2)
+            ]
+            for which, total in enumerate(lag_sum_forward(buf_ref, chunk, rows, 2 * days)):
+                grad_ref[block, which, :, lanes] = total
+
+
 def gather_terms(pieces, terms_ref):
-    shard_days = pieces[0].shape[0]
-    days = shard_days * len(pieces)
-    for number, piece in enumerate(pieces):
+    days = terms_ref.shape[0] // 2
+    start = 0
+    for piece in pieces:
         high, low = split_terms(piece[...])
-        terms_ref[number * shard_days : (number + 1) * shard_days, :] = high
-        terms_ref[days + number * shard_days : days + (number + 1) * shard_days, :] = low
-
-
-def gauge_product(terms_ref, gauge_ref, targets):
-    gauges = gauge_ref.shape[0]
-    total = jnp.zeros((terms_ref.shape[0], BLK), F32)
-    for start in range(0, gauges, BLK):
-        ids = gauge_ref[start : start + BLK, :]
-        hits = jnp.concatenate(
-            [one_hot(ids == targets[:, c * LANES : (c + 1) * LANES]) for c in range(2)], axis=1
-        )
-        total = total + product(terms_ref[:, start : start + BLK], hits)
-    days = terms_ref.shape[0] // 2
+        end = start + piece.shape[0]
+        terms_ref[start:end, :] = high
+        terms_ref[days + start : days + end, :] = low
+        start = end
+
+
+def gauge_hits(gauge_ref, targets):
+    return jnp.concatenate(
+        [one_hot(gauge_ref[...] == targets[:, c * LANES : (c + 1) * LANES]) for c in range(2)], axis=1
+    )
+
+
+def folded(total):
+    days = total.shape[0] // 2
     return total[:days] + total[days:]
 
 
 def path_adjoint_kernel(shards, *refs):
     pieces = refs[:shards]
-    gauge_ref, node_ref, weight_ref, out_ref, terms_ref, seed_ref, buf_ref = refs[shards:]
+    gauge_ref, weight_ref, out_ref, terms_ref, seed_ref, buf_ref = refs[shards:]
     days = out_ref.shape[0]
     gather_terms(pieces, terms_ref)
 
     @pl.loop(0, SENDS)
     def _(height):
-        seeds = gauge_product(terms_ref, gauge_ref, node_ref[pl.ds(height, 1), :])
+        nodes = [weight_ref[height, chunk, KROWS - 1 : KROWS, :] for chunk in range(2)]
+        nodes = jnp.round(jnp.concatenate(nodes, axis=1)).astype(jnp.int32)
+        seeds = folded(product(terms_ref[...], gauge_hits(gauge_ref, nodes)))
         for chunk in range(2):
             seed_ref[height, chunk] = seeds[:, chunk * LANES : (chunk + 1) * LANES]
 
@@ -241,26 +246,35 @@
         out_ref[:, chunk * LANES : (chunk + 1) * LANES] = buf_ref[chunk, 0:days, :]
 
 
-def seed_kernel(shards, first, *refs):
+def seed_kernel(shards, *refs):
     pieces = refs[:shards]
-    gauge_ref, out_ref, terms_ref = refs[shards:]
+    row_ref, gauge_ref, out_ref, terms_ref, hits_ref = refs[shards:]
     gather_terms(pieces, terms_ref)
-
-    @pl.loop(0, out_ref.shape[0])
-    def _(block):
-        targets = iota((1, BLK), 1) + (first + block) * BLK
-        out_ref[block] = gauge_product(terms_ref, gauge_ref, targets)
+    places = gauge_ref[...] & (BLK - 1)
+    for chunk in range(2):
+        lanes = iota((1, LANES), 1) + chunk * LANES
+        hits_ref[:, chunk * LANES : (chunk + 1) * LANES] = one_hot(places == lanes)
+    blocks = row_ref[...] // BLK
+
+    rows = terms_ref.shape[0]
+
+    @pl.loop(0, out_ref.shape[0] // JOINT)
+    def _(group):
+        masked = [terms_ref[...] * one_hot(blocks == group * JOINT + i) for i in range(JOINT)]
+        total = product(jnp.concatenate(masked, axis=0), hits_ref[...])
+        for i in range(JOINT):
+            out_ref[group * JOINT + i] = folded(total[i * rows : (i + 1) * rows])
 
 
 def full_kernel(
-    own_days, level_ref, part_ref, a_own_ref, a_mate_ref, c_own_ref, c_mate_ref, first_seed_ref, last_seed_ref,
-    weight_ref, inflow_ref, down_ref, slot_ref, out_ref, param_ref,
+    own_days, level_ref, part_ref, a_own_ref, a_mate_ref, c_own_ref, c_mate_ref, seed_ref, weight_ref,
+    grad_ref, down_ref, slot_ref, out_ref, param_ref,
     order_ref, count_ref, recv_ref, comp_ref, parent_buf, adj_ref, lat_ref,
 ):
     list_blocks(level_ref, order_ref, count_ref)
     me = part_ref[0]
     flip = (me >> 2) * LANES
-    first_blocks, days = first_seed_ref.shape[:2]
+    days = seed_ref.shape[1]
     width = 2 * LANES
     groups = iota((1, LANES), 1) >> 5
     rows = iota((BLK, width), 0)
@@ -319,60 +333,62 @@
             recv_ref[days : 2 * days, lanes] = low
 
     adj_ref[...] = jnp.zeros(adj_ref.shape, F32)
-    for height in range(LEVELS):
+    lat_ref[...] = jnp.zeros(lat_ref.shape, BF16)
+
+    def level(height, sources):
         need = days_of(height)
         have = days_of(height - 1) if height else days
-
-        @pl.loop(0, count_ref[height])
-        def _(rank, height=height, need=need, have=have):
+        count = count_ref[height]
+
+        def gather(rank):
             block = order_ref[height * MAXB + rank]
-
-            def keep(adjoint):
-                for chunk in range(2):
-                    adj_ref[chunk, 0:have, :] = adjoint[:, chunk * LANES : (chunk + 1) * LANES]
-
-            @pl.when(block < first_blocks)
-            def _():
-                keep(first_seed_ref[block, 0:have, :])
-
-            @pl.when(block >= first_blocks)
-            def _():
-                keep(last_seed_ref[block - first_blocks, 0:have, :])
-
-            if height:
-                slot = slot_ref[block]
-                sender = slot >> 2
-                lane = ((sender >> 2) * LANES ^ flip) + ((sender + (height - 1)) & 3) * KROWS
-                lane = jnp.where(slot >= 0, lane + me * 4 + (slot & 3), -1)
-                down = down_ref[block]
-                at = slice((height - 1) * width, height * width)
-
-                def gather(sources):
-                    hits = [one_hot(rows == lane)]
-                    for index in range(sources):
-                        source = order_ref[(height - 1) * MAXB + index]
-                        hits.append(one_hot(rows == down - source * BLK))
-                    terms = []
-                    for start, first in ((0, 0), (have, days)):
-                        local = lat_ref[(height - 1) % 2, start : start + have, 0 : sources * BLK]
-                        received = recv_ref[first : first + have, at]
-                        terms.append(jnp.concatenate([received, local], axis=1))
-                    total = product(jnp.concatenate(terms, axis=0), jnp.concatenate(hits, axis=0))
-                    seeds = jnp.concatenate([adj_ref[chunk, 0:have, :] for chunk in range(2)], axis=1)
-                    keep(seeds + total[:have] + total[have:])
-
-                for sources in range(1, MAXB + 1):
-                    pl.when(count_ref[height - 1] == sources)(functools.partial(gather, sources))
+            seeds = seed_ref[block, 0:have, :]
+            if not height:
+                return seeds
+            slot = slot_ref[block]
+            sender = slot >> 2
+            lane = ((sender >> 2) * LANES ^ flip) + ((sender + (height - 1)) & 3) * KROWS
+            lane = jnp.where(slot >= 0, lane + me * 4 + (slot & 3), -1)
+            down = down_ref[block]
+            hits = [one_hot(rows == lane)]
+            for index in range(sources):
+                source = jnp.where(
+                    index < count_ref[height - 1], order_ref[(height - 1) * MAXB + index], -2
+                )
+                hits.append(one_hot((rows == down - source * BLK) & (down >= 0)))
+            terms = []
+            for start, first in ((0, 0), (have, days)):
+                local = lat_ref[(height - 1) % 2, start : start + have, 0 : sources * BLK]
+                received = recv_ref[first : first + have, (height - 1) * width : height * width]
+                terms.append(jnp.concatenate([received, local], axis=1))
+            total = product(jnp.concatenate(terms, axis=0), jnp.concatenate(hits, axis=0))
+            return seeds + total[:have] + total[have:]
+
+        @pl.loop(0, count)
+        def _(rank):
+            adjoint = gather(rank)
+            block = order_ref[height * MAXB + rank]
             for chunk in range(2):
+                lanes = slice(chunk * LANES, (chunk + 1) * LANES)
+                adj_ref[chunk, 0:have, :] = adjoint[:, lanes]
                 at = pl.ds(pl.multiple_of(block * BLK + chunk * LANES, LANES), LANES)
-                result, params = lag_sums(adj_ref, chunk, weight_ref.at[block, chunk], inflow_ref[:, at], need)
+                for which in range(2):
+                    grads = adjoint[: 2 * own_days, lanes] * grad_ref[block, which, :, lanes]
+                    param_ref[which : which + 1, at] = jnp.sum(grads, axis=0, keepdims=True)
+                row = lambda lag, chunk=chunk: weight_ref[block, chunk, 0, lag : lag + 1, :]
+                result = lag_sum(adj_ref, chunk, row, need)
                 out_ref[:, at] = result[:own_days]
-                param_ref[:, at] = params
                 if height + 1 < LEVELS:
                     high, low = split_terms(result)
                     lanes = pl.ds(pl.multiple_of(rank * BLK + chunk * LANES, LANES), LANES)
                     lat_ref[height % 2, 0:need, lanes] = high
                     lat_ref[height % 2, need : 2 * need, lanes] = low
+
+    level(0, 0)
+    for height in range(1, LEVELS):
+        few = count_ref[height - 1] <= MAXB // 2
+        pl.when(few)(functools.partial(level, height, MAXB // 2))
+        pl.when(jnp.logical_not(few))(functools.partial(level, height, MAXB))
 
 
 def call(kernel, out_shape, in_smem, in_vmem, scratch, flops, limit=VMEM_LIMIT):
@@ -403,13 +419,6 @@
     return own, exchange(own, "basin", 1)
 
 
-def over_basin_in_turn(values, before):
-    own = values[None]
-    own = after(jnp.concatenate([own, exchange(own, "basin", 2)], axis=0), before)
-    own = jnp.concatenate([own, exchange(own, "basin", 4)], axis=0)
-    return own, exchange(own, "basin", 1)
-
-
 def gauge_columns(gauge_reach):
     return jnp.broadcast_to(gauge_reach[:, None], (gauge_reach.shape[0], LANES))
 
@@ -426,7 +435,6 @@
     return call(
         functools.partial(path_kernel, days),
         (
-            jax.ShapeDtypeStruct((8, WIDTH), jnp.int32),
             jax.ShapeDtypeStruct((SENDS, 2, KROWS, LANES), F32),
             jax.ShapeDtypeStruct((days + 8, WIDTH), F32),
             jax.ShapeDtypeStruct((block_level.shape[0], 2, 3, KROWS, LANES), F32),
@@ -440,14 +448,14 @@
     )
 
 
-def path_adjoints(pieces, gauge_ids, nodes, path_weights):
+def path_adjoints(pieces, gauge_ids, path_weights):
     shards = len(pieces)
-    days = shards * pieces[0].shape[0]
+    days = sum(piece.shape[0] for piece in pieces)
     return call(
         functools.partial(path_adjoint_kernel, shards),
         jax.ShapeDtypeStruct((days, WIDTH), F32),
         [],
-        pieces + [gauge_ids, nodes, path_weights],
+        pieces + [gauge_ids, path_weights],
         [
             pltpu.VMEM((2 * days, pieces[0].shape[1]), BF16),
             pltpu.VMEM((SENDS, 2, days, LANES), F32),
@@ -457,28 +465,41 @@
     )
 
 
-def reach_seeds(pieces, gauge_ids, first, end):
+def reach_seeds(pieces, gauge_reach, gauge_ids, blocks):
     shards = len(pieces)
     days = sum(piece.shape[0] for piece in pieces)
+    gauges = gauge_reach.shape[0]
     return call(
-        functools.partial(seed_kernel, shards, first),
-        jax.ShapeDtypeStruct((end - first, days, BLK), F32),
+        functools.partial(seed_kernel, shards),
+        jax.ShapeDtypeStruct((blocks, days, BLK), F32),
         [],
-        pieces + [gauge_ids],
-        [pltpu.VMEM((2 * days, pieces[0].shape[1]), BF16)],
+        pieces + [gauge_reach.reshape(1, gauges), gauge_ids],
+        [pltpu.VMEM((2 * days, gauges), BF16), pltpu.VMEM((gauges, BLK), BF16)],
         3_000_000_000,
     )
 
 
-def all_reaches(inflow, block_level, part, adjoints, composed, first_seeds, last_seeds, weights, down_local, in_slot):
+def day_grads(inflow, weights):
     own_days = inflow.shape[0]
-    blocks, days = block_level.shape[0], first_seeds.shape[1]
+    return call(
+        grad_kernel,
+        jax.ShapeDtypeStruct((weights.shape[0], 2, 2 * own_days, BLK), F32),
+        [],
+        [inflow, weights],
+        [pltpu.VMEM((2, KROWS + 2 * own_days, LANES), F32)],
+        1_000_000,
+    )
+
+
+def all_reaches(block_level, part, adjoints, composed, seeds, weights, grads, down_local, in_slot):
+    own_days = grads.shape[2] // 2
+    blocks, days = block_level.shape[0], seeds.shape[1]
     reaches = blocks * BLK
     return call(
         functools.partial(full_kernel, own_days),
         (jax.ShapeDtypeStruct((own_days, reaches), F32), jax.ShapeDtypeStruct((2, reaches), F32)),
         [block_level, part],
-        [*adjoints, *composed, first_seeds, last_seeds, weights, inflow, by_block(down_local), by_block(in_slot)],
+        [*adjoints, *composed, seeds, weights, grads, by_block(down_local), by_block(in_slot)],
         kernel_tables()
         + [
             pltpu.VMEM((2 * days, SENDS * WIDTH), BF16),
@@ -502,25 +523,32 @@
     blocks = block_level.shape[0]
     shards = lax.axis_size("tm")
     days = shards * own_days
-    part = lax.axis_index("basin").astype(jnp.int32).reshape(1)
-    nodes, path_weights, composed, weights = sent_paths(
+    gauge_ids = gauge_columns(gauge_reach)
+    part = after(lax.axis_index("basin").astype(jnp.int32).reshape(1), gauge_ids)
+    path_weights, composed, weights = sent_paths(
         days, block_level, part, shape_param, scale_param, down_local, in_slot, send_reach.reshape(SENDS, 1, KROWS)
     )
     back = lambda by, reach: [(i + by, i) for i in range(shards - reach)]
     following = lax.ppermute(cotangent, "tm", back(1, 1))
-    following, composed = lax.optimization_barrier((following, composed, nodes))[:2]
+    following, composed, path_weights = lax.optimization_barrier((following, composed, path_weights))
     second = lax.ppermute(following, "tm", back(1, 2))
     third = lax.ppermute(following, "tm", back(2, 3))
-    gauge_ids = gauge_columns(gauge_reach)
-    composed = over_basin_in_turn(composed, after(second, gauge_ids))
-    third, second, nodes, gauge_ids = lax.optimization_barrier((third, second, nodes, gauge_ids))
-    pieces = [cotangent, following, second, third]
-    adjoints = path_adjoints(pieces, gauge_ids, nodes, path_weights)
-    first_seeds = reach_seeds(pieces, gauge_ids, 0, blocks // 2)
-    adjoints = over_basin(adjoints, first_seeds)
-    last_seeds = reach_seeds(after(pieces, adjoints[0]), gauge_ids, blocks // 2, blocks)
+    early = jnp.concatenate([cotangent, following], axis=0)
+    path_weights = jnp.pad(path_weights, ((0, 1), (0, 0), (0, 0), (0, 0)))
+    composed = jnp.concatenate([composed[None], exchange(composed[None], "basin", 2)], axis=0)
+    composed, early, path_weights, weights = lax.optimization_barrier(
+        (composed, early, path_weights, weights)
+    )
+    grads = day_grads(inflow, weights)
+    composed = jnp.concatenate([composed, exchange(composed, "basin", 4)], axis=0)
+    composed = (composed, exchange(composed, "basin", 1))
+    third, second, grads = lax.optimization_barrier((third, second, grads))
+    pieces = [early, second, third]
+    adjoints = path_adjoints(pieces, gauge_ids, path_weights)
+    seeds = reach_seeds(pieces, gauge_reach, gauge_ids, blocks)
+    adjoints = over_basin(adjoints, seeds)
     lateral, params = all_reaches(
-        inflow, block_level, part, adjoints, composed, first_seeds, last_seeds, weights, down_local, in_slot
+        block_level, part, adjoints, composed, seeds, weights, grads, down_local, in_slot
     )
     first, second, third = (exchange(params, "tm", by) for by in (1, 2, 3))
     return lateral, (params + first) + (second + third)

time: 72.2 us -> 69.6 us (0.964)
  waiting for transfers between devices: 16.5 us -> 11.3 us
  Pallas kernels: 35.7 us -> 37 us
  local copies, waits for them, and re-layouts: 1.06 us -> 2.05 us
  other arithmetic: 1.65 us -> 2.59 us
    ppermute x1, waiting for transfers between devices: 3.82 us -> 0.99 us  [fast_shards(): second = lax.ppermute(following, 'tm', back(1, 2))]
    ppermute x1, waiting for transfers between devices: 3.39 us -> 1.87 us  [fast_shards(): following = lax.ppermute(cotangent, 'tm', back(1, 1))]
    ppermute x1, waiting for transfers between devices: 1.48 us -> 0.01 us  [fast_shards(): third = lax.ppermute(following, 'tm', back(2, 3))]
    pallas_call x5, Pallas kernels: 35.7 us -> 37 us  [call(): pl.pallas_call(kernel, out_shape=out_shape, in_specs=[smem] * len(in_smem...]
    pad x0 -> x1, local copies, waits for them, and re-layouts: none -> 0.96 us  [fast_shards(): path_weights = jnp.pad(path_weights, ((0, 1), (0, 0), (0, 0), (0, 0)))]
    concatenate x2, other arithmetic: 0.96 us -> 1.91 us  [the longest x1 0.98 us: fast_shards(): early = jnp.concatenate([cotangent, following], axis=0)]
  transfers between devices with their start and end apart: 13 -> 13, of which waited for: 7 -> 7; matrix products, arithmetic and copies ran while one was open for 3% -> 6% of each run, Pallas kernels for 27% -> 31%
where the time goes in v2:
time: 69.6 us; the launch traced here: 69.2 us
  Pallas kernels  37 us (53%)
  starting transfers between devices  15.6 us (22%)
  waiting for transfers between devices  11.3 us (16%)
  other arithmetic  2.59 us (4%)
  local copies, waits for them, and re-layouts  2.05 us (3%)
  between operations  0.8 us (1%)
    pallas_call x5, Pallas kernels, call(): pl.pallas_call(kernel, out_shape=out_shape, in_specs=[smem] * len(in_smem...  37 us
    ppermute x10, starting transfers between devices, exchange(): lax.ppermute(values, axis, [(i, i ^ by) for i in range(lax.axis_size(axis...  11.6 us
    ppermute x10, waiting for transfers between devices, exchange(): lax.ppermute(values, axis, [(i, i ^ by) for i in range(lax.axis_size(axis...  8.4 us
    ppermute x1, waiting for transfers between devices, fast_shards(): following = lax.ppermute(cotangent, 'tm', back(1, 1))  1.87 us
    ppermute x1, starting transfers between devices, fast_shards(): following = lax.ppermute(cotangent, 'tm', back(1, 1))  1.42 us
  transfers between devices with their start and end apart: 13, of which 7 were waited for; matrix products, arithmetic and copies ran while one was open for 6% of the time, Pallas kernels for 31%

profile of v2, /device:TPU:0, one launch (start us, length us, event | category | flops | bytes accessed | tf_op | source)
XLA Modules:
  0.0 69.2 jit_solution(5890926977090638965)
XLA Ops:
  0.6 0.0 copy-start.1
  0.6 1.4 %collective-permute-start = (f32[32,2048]{1,0:T(8,128)}, f32[32,2048]{1,0:T(8,128)S(1)}, u32[]{:S(2)}, u32[]{:S(2)}) collective-permute-start(f32[32,2048]{1,0:T(8,128)} %param.10), channel_id=1, source_target_pairs={{1,0},{2,1},{3,2},{5,4},{6,5},{7,6},{9,8},{10,9},{11,10},{13,12},{... | collective-permute-start | bytes 786440 | tf_op jit(solution)/shard_map/ppermute | solution.py:532
  2.1 1.0 %broadcast_in_dim.4.refs_3_.refs_4_ = s32[2048,128]{1,0:T(8,128)S(1)} broadcast(s32[2048]{0:T(1024)} %param.11), dimensions={0} | broadcast | bytes 1056768 | tf_op jit(solution)/shard_map/broadcast_in_dim | solution.py:423
  3.1 7.2 %shard_map.104 = (f32[7,2,32,128]{3,2,1,0:T(8,128)}, f32[136,256]{1,0:T(8,128)}, f32[16,2,3,32,128]{4,3,2,1,0:T(8,128)}) custom-call(s32[16]{0:T(128)} %level_ref.3, s32[1]{0:T(128)} %bitcast.part_ref, s32[16,1,256]{2,1,0:T(1,128)} %bitcast.13, s32[16,1,256]{2,1,0:T(1,128)} %bitcast.15, f32[16,1,256]{2,1,0:T(1,128)} %bitcast.23, f32[16,1,256]{2,1,0:T(1,128)} %bitcast.24, ...), custom_call_target="tpu_custom_call" | custom-call | flops 1000000 | bytes 1000 | tf_op jit(solution)/shard_map/pallas_call | solution.py:397
  10.3 0.0 copy-start
  10.3 1.9 %collective-permute-done = f32[32,2048]{1,0:T(8,128)S(1)} collective-permute-done((f32[32,2048]{1,0:T(8,128)}, f32[32,2048]{1,0:T(8,128)S(1)}, u32[]{:S(2)}, u32[]{:S(2)}) %collective-permute-start) | collective-permute-done | bytes 262176 | tf_op jit(solution)/shard_map/ppermute | solution.py:532
  12.2 1.3 %collective-permute-start.2 = (f32[32,2048]{1,0:T(8,128)S(1)}, f32[32,2048]{1,0:T(8,128)S(1)}, u32[]{:S(2)}, u32[]{:S(2)}) collective-permute-start(f32[32,2048]{1,0:T(8,128)S(1)} %collective-permute-done), channel_id=1, source_target_pairs={{2,0},{6,4},{10,8},{14,12},{18,16},{22,20},{26,24},{30,28}} | collective-permute-start | bytes 786440 | tf_op jit(solution)/shard_map/ppermute | solution.py:535
  13.5 1.3 %collective-permute-start.3 = (f32[32,2048]{1,0:T(8,128)S(1)}, f32[32,2048]{1,0:T(8,128)S(1)}, u32[]{:S(2)}, u32[]{:S(2)}) collective-permute-start(f32[32,2048]{1,0:T(8,128)S(1)} %collective-permute-done), channel_id=1, source_target_pairs={{1,0},{2,1},{5,4},{6,5},{9,8},{10,9},{13,12},{14,13},{17,16},{18,1... | collective-permute-start | bytes 786440 | tf_op jit(solution)/shard_map/ppermute | solution.py:534
  14.8 1.7 %collective-permute-start.1 = (f32[1,136,256]{2,1,0:T(8,128)}, f32[1,136,256]{2,1,0:T(8,128)S(1)}, u32[]{:S(2)}, u32[]{:S(2)}) collective-permute-start(f32[1,136,256]{2,1,0:T(8,128)} %bitcast.18), channel_id=1, source_target_pairs={{0,8},{4,12},{8,0},{12,4},{16,24},{20,28},{24,16},{28,20},{1,9},{5... | collective-permute-start | bytes 417800 | tf_op jit(solution)/shard_map/ppermute | solution.py:413
  16.5 1.0 %pad_maximum_fusion.refs_0_ = f32[64,2048]{1,0:T(8,128)S(1)} fusion(f32[32,2048]{1,0:T(8,128)S(1)} %collective-permute-done, f32[32,2048]{1,0:T(8,128)} %param.10), kind=kLoop, calls=%fused_computation | loop fusion | flops 131072 | bytes 1048576 | tf_op jit(solution)/shard_map/concatenate | solution.py:536
  17.5 1.0 %pad.4.refs_4_ = f32[8,2,32,128]{3,2,1,0:T(8,128)S(1)} pad(f32[7,2,32,128]{3,2,1,0:T(8,128)} %get-tuple-element.24, f32[]{:T(128)} %constant.8.clone.1), padding=0_1x0_0x0_0x0_0 | pad | bytes 491524 | tf_op jit(solution)/shard_map/jit(_pad)/pad | solution.py:537
  18.5 1.7 %collective-permute-done.1 = f32[1,136,256]{2,1,0:T(8,128)S(1)} collective-permute-done((f32[1,136,256]{2,1,0:T(8,128)}, f32[1,136,256]{2,1,0:T(8,128)S(1)}, u32[]{:S(2)}, u32[]{:S(2)}) %collective-permute-start.1) | collective-permute-done | bytes 139296 | tf_op jit(solution)/shard_map/ppermute | solution.py:413
  20.1 0.9 %pad_maximum_fusion.2 = f32[2,136,256]{2,1,0:T(8,128)S(1)} fusion(f32[1,136,256]{2,1,0:T(8,128)S(1)} %collective-permute-done.1, f32[1,136,256]{2,1,0:T(8,128)} %bitcast.19), kind=kLoop, calls=%fused_computation.2 | loop fusion | flops 69632 | bytes 557056 | tf_op jit(solution)/shard_map/concatenate | solution.py:538
  21.1 1.9 %collective-permute-start.8 = (f32[2,136,256]{2,1,0:T(8,128)S(1)}, f32[2,136,256]{2,1,0:T(8,128)S(1)}, u32[]{:S(2)}, u32[]{:S(2)}) collective-permute-start(f32[2,136,256]{2,1,0:T(8,128)S(1)} %pad_maximum_fusion.2), channel_id=1, source_target_pairs={{0,16},{4,20},{8,24},{12,28},{16,0},{20,4},{24,8},{28,12},{1,17},{... | collective-permute-start | bytes 835592 | tf_op jit(solution)/shard_map/ppermute | solution.py:413
  22.9 0.0 copy-done.1
  22.9 0.0 copy-done
  22.9 4.2 %shard_map.105.grad_ref = f32[16,2,64,256]{3,2,1,0:T(8,128)S(1)} custom-call(f32[32,4096]{1,0:T(8,128)S(1)} %copy-done.1, f32[16,2,3,32,128]{4,3,2,1,0:T(8,128)S(1)} %copy-done), custom_call_target="tpu_custom_call" | custom-call | flops 1000000 | bytes 1000 | tf_op jit(solution)/shard_map/pallas_call | solution.py:397
  27.2 0.0 copy-start.4
  27.2 0.0 collective-permute-done.2.refs_2_
  27.2 1.0 %collective-permute-done.3.refs_1_ = f32[32,2048]{1,0:T(8,128)S(1)} collective-permute-done((f32[32,2048]{1,0:T(8,128)S(1)}, f32[32,2048]{1,0:T(8,128)S(1)}, u32[]{:S(2)}, u32[]{:S(2)}) %collective-permute-start.3) | collective-permute-done | bytes 262176 | tf_op jit(solution)/shard_map/ppermute | solution.py:534
  28.2 4.8 %shard_map.106 = f32[128,256]{1,0:T(8,128)S(1)} custom-call(f32[64,2048]{1,0:T(8,128)S(1)} %pad_maximum_fusion.refs_0_, f32[32,2048]{1,0:T(8,128)S(1)} %collective-permute-done.3.refs_1_, f32[32,2048]{1,0:T(8,128)S(1)} %collective-permute-done.2.refs_2_, s32[2048,128]{1,0:T(8,128)S(1)} %broadcast_in_dim.4.refs_3_.refs_4_, f32[8,2,32,128]{3,2,1,0:T(8,128)S(1)} %pad.4.refs_4_), custom_call_target="tpu_custom_call" | custom-call | flops 4000000000 | bytes 4000000 | tf_op jit(solution)/shard_map/pallas_call | solution.py:397
  33.0 3.0 %collective-permute-start.6 = (f32[128,256]{1,0:T(8,128)S(1)}, f32[128,256]{1,0:T(8,128)S(1)}, u32[]{:S(2)}, u32[]{:S(2)}) collective-permute-start(f32[128,256]{1,0:T(8,128)S(1)} %shard_map.106), channel_id=1, source_target_pairs={{0,24},{4,28},{8,16},{12,20},{16,8},{20,12},{24,0},{28,4},{1,25},{... | collective-permute-start | bytes 393224 | tf_op jit(solution)/shard_map/ppermute | solution.py:413
  36.0 0.4 collective-permute-start.5
  36.3 0.3 collective-permute-start.4
  36.6 0.0 copy-done.4
  36.6 0.0 copy-start.2
  36.6 0.0 copy-start.3
  36.6 0.0 copy-start.5
  36.6 5.5 %shard_map.107.seed_ref = f32[16,128,256]{2,1,0:T(8,128)S(1)} custom-call(f32[64,2048]{1,0:T(8,128)S(1)} %pad_maximum_fusion.refs_0_, f32[32,2048]{1,0:T(8,128)S(1)} %collective-permute-done.3.refs_1_, f32[32,2048]{1,0:T(8,128)S(1)} %collective-permute-done.2.refs_2_, s32[1,2048]{1,0:T(1,128)S(1)} %bitcast.17, s32[2048,128]{1,0:T(8,128)S(1)} %broadcast_in_dim.4.refs_3_.refs_4_), custom_call_target="tpu_custom_call" | custom-call | flops 3000000000 | bytes 3000000 | tf_op jit(solution)/shard_map/pallas_call | solution.py:397
  42.1 0.0 collective-permute-done.8
  42.1 0.1 collective-permute-start.9
  42.2 0.0 collective-permute-done.6
  42.2 0.2 collective-permute-done.5
  42.5 0.0 collective-permute-done.4
  42.5 0.3 collective-permute-start.7
  42.8 2.1 %collective-permute-done.7.a_mate_ref = f32[4,128,256]{2,1,0:T(8,128)S(1)} collective-permute-done((f32[4,128,256]{2,1,0:T(8,128)S(1)}, f32[4,128,256]{2,1,0:T(8,128)S(1)}, u32[]{:S(2)}, u32[]{:S(2)}) %collective-permute-start.7) | collective-permute-done | bytes 524320 | tf_op jit(solution)/shard_map/ppermute | solution.py:413
  44.9 0.0 collective-permute-done.9.c_mate_ref
  44.9 0.0 copy-done.2
  44.9 0.0 copy-done.3
  44.9 0.0 copy-done.5
  44.9 15.3 %shard_map.108 = (f32[32,4096]{1,0:T(8,128)}, f32[2,4096]{1,0:T(2,128)S(1)}) custom-call(s32[16]{0:T(128)S(1)} %copy-done.5, s32[1]{0:T(128)} %bitcast.part_ref, f32[4,128,256]{2,1,0:T(8,128)S(1)} %pad_maximum_fusion.1.a_own_ref, f32[4,128,256]{2,1,0:T(8,128)S(1)} %collective-permute-done.7.a_mate_ref, ...), custom_call_target="tpu_custom_call" | custom-call | flops 10000000000 | bytes 10000000 | tf_op jit(solution)/shard_map/pallas_call | solution.py:397
  60.2 2.7 %collective-permute-start.11 = (f32[2,4096]{1,0:T(2,128)S(1)}, f32[2,4096]{1,0:T(2,128)S(1)}, u32[]{:S(2)}, u32[]{:S(2)}) collective-permute-start(f32[2,4096]{1,0:T(2,128)S(1)} %get-tuple-element.35), channel_id=1, source_target_pairs={{0,2},{1,3},{2,0},{3,1},{4,6},{5,7},{6,4},{7,5},{8,10},{9,11},{10,... | collective-permute-start | bytes 98312 | tf_op jit(solution)/shard_map/ppermute | solution.py:413
  62.9 1.3 %collective-permute-start.12 = (f32[2,4096]{1,0:T(2,128)S(1)}, f32[2,4096]{1,0:T(2,128)S(1)}, u32[]{:S(2)}, u32[]{:S(2)}) collective-permute-start(f32[2,4096]{1,0:T(2,128)S(1)} %get-tuple-element.35), channel_id=1, source_target_pairs={{0,3},{1,2},{2,1},{3,0},{4,7},{5,6},{6,5},{7,4},{8,11},{9,10},{10,... | collective-permute-start | bytes 98312 | tf_op jit(solution)/shard_map/ppermute | solution.py:413
  64.2 0.0 collective-permute-start.10
  64.2 1.3 %collective-permute-done.11 = f32[2,4096]{1,0:T(2,128)S(1)} collective-permute-done((f32[2,4096]{1,0:T(2,128)S(1)}, f32[2,4096]{1,0:T(2,128)S(1)}, u32[]{:S(2)}, u32[]{:S(2)}) %collective-permute-start.11) | collective-permute-done | bytes 32800 | tf_op jit(solution)/shard_map/ppermute | solution.py:413
  65.5 3.1 %collective-permute-done.12 = f32[2,4096]{1,0:T(2,128)S(1)} collective-permute-done((f32[2,4096]{1,0:T(2,128)S(1)}, f32[2,4096]{1,0:T(2,128)S(1)}, u32[]{:S(2)}, u32[]{:S(2)}) %collective-permute-start.12) | collective-permute-done | bytes 32800 | tf_op jit(solution)/shard_map/ppermute | solution.py:413
  68.6 0.0 collective-permute-done.10
  68.6 0.6 add_add_fusion
  (3 shorter events, 0.1 us)
Async XLA Ops:
  0.6 22.3 %copy-start.1 = (f32[32,4096]{1,0:T(8,128)S(1)}, f32[32,4096]{1,0:T(8,128)}, u32[]{:S(2)}) copy-start(f32[32,4096]{1,0:T(8,128)} %inflow_ref.1) | copy-start | bytes 1572868
  0.6 11.6 %collective-permute-start = (f32[32,2048]{1,0:T(8,128)}, f32[32,2048]{1,0:T(8,128)S(1)}, u32[]{:S(2)}, u32[]{:S(2)}) collective-permute-start(f32[32,2048]{1,0:T(8,128)} %param.10), channel_id=1, source_target_pairs={{1,0},{2,1},{3,2},{5,4},{6,5},{7,6},{9,8},{10,9},{11,10},{13,12},{... | collective-permute-start | bytes 786440 | tf_op jit(solution)/shard_map/ppermute | solution.py:532
  10.3 12.6 %copy-start = (f32[16,2,3,32,128]{4,3,2,1,0:T(8,128)S(1)}, f32[16,2,3,32,128]{4,3,2,1,0:T(8,128)}, u32[]{:S(2)}) copy-start(f32[16,2,3,32,128]{4,3,2,1,0:T(8,128)} %get-tuple-element.27.weight_ref) | copy-start | bytes 4718596
  12.2 15.0 %collective-permute-start.2 = (f32[32,2048]{1,0:T(8,128)S(1)}, f32[32,2048]{1,0:T(8,128)S(1)}, u32[]{:S(2)}, u32[]{:S(2)}) collective-permute-start(f32[32,2048]{1,0:T(8,128)S(1)} %collective-permute-done), channel_id=1, source_target_pairs={{2,0},{6,4},{10,8},{14,12},{18,16},{22,20},{26,24},{30,28}} | collective-permute-start | bytes 786440 | tf_op jit(solution)/shard_map/ppermute | solution.py:535
  13.5 14.7 %collective-permute-start.3 = (f32[32,2048]{1,0:T(8,128)S(1)}, f32[32,2048]{1,0:T(8,128)S(1)}, u32[]{:S(2)}, u32[]{:S(2)}) collective-permute-start(f32[32,2048]{1,0:T(8,128)S(1)} %collective-permute-done), channel_id=1, source_target_pairs={{1,0},{2,1},{5,4},{6,5},{9,8},{10,9},{13,12},{14,13},{17,16},{18,1... | collective-permute-start | bytes 786440 | tf_op jit(solution)/shard_map/ppermute | solution.py:534
  14.8 5.3 %collective-permute-start.1 = (f32[1,136,256]{2,1,0:T(8,128)}, f32[1,136,256]{2,1,0:T(8,128)S(1)}, u32[]{:S(2)}, u32[]{:S(2)}) collective-permute-start(f32[1,136,256]{2,1,0:T(8,128)} %bitcast.18), channel_id=1, source_target_pairs={{0,8},{4,12},{8,0},{12,4},{16,24},{20,28},{24,16},{28,20},{1,9},{5... | collective-permute-start | bytes 417800 | tf_op jit(solution)/shard_map/ppermute | solution.py:413
  21.1 21.0 %collective-permute-start.8 = (f32[2,136,256]{2,1,0:T(8,128)S(1)}, f32[2,136,256]{2,1,0:T(8,128)S(1)}, u32[]{:S(2)}, u32[]{:S(2)}) collective-permute-start(f32[2,136,256]{2,1,0:T(8,128)S(1)} %pad_maximum_fusion.2), channel_id=1, source_target_pairs={{0,16},{4,20},{8,24},{12,28},{16,0},{20,4},{24,8},{28,12},{1,17},{... | collective-permute-start | bytes 835592 | tf_op jit(solution)/shard_map/ppermute | solution.py:413
  27.2 9.4 %copy-start.4 = (s32[2048]{0:T(1024)S(1)}, s32[2048]{0:T(1024)}, u32[]{:S(2)}) copy-start(s32[2048]{0:T(1024)} %param.11) | copy-start | bytes 24580
  33.0 9.2 %collective-permute-start.6 = (f32[128,256]{1,0:T(8,128)S(1)}, f32[128,256]{1,0:T(8,128)S(1)}, u32[]{:S(2)}, u32[]{:S(2)}) collective-permute-start(f32[128,256]{1,0:T(8,128)S(1)} %shard_map.106), channel_id=1, source_target_pairs={{0,24},{4,28},{8,16},{12,20},{16,8},{20,12},{24,0},{28,4},{1,25},{... | collective-permute-start | bytes 393224 | tf_op jit(solution)/shard_map/ppermute | solution.py:413
  36.0 6.5 %collective-permute-start.5 = (f32[128,256]{1,0:T(8,128)S(1)}, f32[128,256]{1,0:T(8,128)S(1)}, u32[]{:S(2)}, u32[]{:S(2)}) collective-permute-start(f32[128,256]{1,0:T(8,128)S(1)} %shard_map.106), channel_id=1, source_target_pairs={{0,16},{4,20},{8,24},{12,28},{16,0},{20,4},{24,8},{28,12},{1,17},{... | collective-permute-start | bytes 393224 | tf_op jit(solution)/shard_map/ppermute | solution.py:413
  36.3 6.1 %collective-permute-start.4 = (f32[128,256]{1,0:T(8,128)S(1)}, f32[128,256]{1,0:T(8,128)S(1)}, u32[]{:S(2)}, u32[]{:S(2)}) collective-permute-start(f32[128,256]{1,0:T(8,128)S(1)} %shard_map.106), channel_id=1, source_target_pairs={{0,8},{4,12},{8,0},{12,4},{16,24},{20,28},{24,16},{28,20},{1,9},{5... | collective-permute-start | bytes 393224 | tf_op jit(solution)/shard_map/ppermute | solution.py:413
  36.6 8.3 %copy-start.2 = (s32[4096]{0:T(1024)S(1)}, s32[4096]{0:T(1024)}, u32[]{:S(2)}) copy-start(s32[4096]{0:T(1024)} %param.15) | copy-start | bytes 49156
  36.6 8.3 %copy-start.3 = (s32[4096]{0:T(1024)S(1)}, s32[4096]{0:T(1024)}, u32[]{:S(2)}) copy-start(s32[4096]{0:T(1024)} %param.16) | copy-start | bytes 49156
  36.6 8.3 %copy-start.5 = (s32[16]{0:T(128)S(1)}, s32[16]{0:T(128)}, u32[]{:S(2)}) copy-start(s32[16]{0:T(128)} %level_ref.3) | copy-start | bytes 196
  42.1 2.8 %collective-permute-start.9 = (f32[4,136,256]{2,1,0:T(8,128)S(1)}, f32[4,136,256]{2,1,0:T(8,128)S(1)}, u32[]{:S(2)}, u32[]{:S(2)}) collective-permute-start(f32[4,136,256]{2,1,0:T(8,128)S(1)} %constant_dynamic-update-slice_fusion.c_own_ref), channel_id=1, source_target_pairs={{0,4},{4,0},{8,12},{12,8},{16,20},{20,16},{24,28},{28,24},{1,5},{5... | collective-permute-start | bytes 1671176 | tf_op jit(solution)/shard_map/ppermute | solution.py:413
  42.5 2.4 %collective-permute-start.7 = (f32[4,128,256]{2,1,0:T(8,128)S(1)}, f32[4,128,256]{2,1,0:T(8,128)S(1)}, u32[]{:S(2)}, u32[]{:S(2)}) collective-permute-start(f32[4,128,256]{2,1,0:T(8,128)S(1)} %pad_maximum_fusion.1.a_own_ref), channel_id=1, source_target_pairs={{0,4},{4,0},{8,12},{12,8},{16,20},{20,16},{24,28},{28,24},{1,5},{5... | collective-permute-start | bytes 1572872 | tf_op jit(solution)/shard_map/ppermute | solution.py:413
  60.2 5.2 %collective-permute-start.11 = (f32[2,4096]{1,0:T(2,128)S(1)}, f32[2,4096]{1,0:T(2,128)S(1)}, u32[]{:S(2)}, u32[]{:S(2)}) collective-permute-start(f32[2,4096]{1,0:T(2,128)S(1)} %get-tuple-element.35), channel_id=1, source_target_pairs={{0,2},{1,3},{2,0},{3,1},{4,6},{5,7},{6,4},{7,5},{8,10},{9,11},{10,... | collective-permute-start | bytes 98312 | tf_op jit(solution)/shard_map/ppermute | solution.py:413
  62.9 5.7 %collective-permute-start.12 = (f32[2,4096]{1,0:T(2,128)S(1)}, f32[2,4096]{1,0:T(2,128)S(1)}, u32[]{:S(2)}, u32[]{:S(2)}) collective-permute-start(f32[2,4096]{1,0:T(2,128)S(1)} %get-tuple-element.35), channel_id=1, source_target_pairs={{0,3},{1,2},{2,1},{3,0},{4,7},{5,6},{6,5},{7,4},{8,11},{9,10},{10,... | collective-permute-start | bytes 98312 | tf_op jit(solution)/shard_map/ppermute | solution.py:413
  64.2 4.4 %collective-permute-start.10 = (f32[2,4096]{1,0:T(2,128)S(1)}, f32[2,4096]{1,0:T(2,128)S(1)}, u32[]{:S(2)}, u32[]{:S(2)}) collective-permute-start(f32[2,4096]{1,0:T(2,128)S(1)} %get-tuple-element.35), channel_id=1, source_target_pairs={{0,1},{1,0},{2,3},{3,2},{4,5},{5,4},{6,7},{7,6},{8,9},{9,8},{10,11... | collective-permute-start | bytes 98312 | tf_op jit(solution)/shard_map/ppermute | solution.py:413

commit v3 on v2

--- a/solution.py
+++ b/solution.py
@@ -81,25 +81,10 @@
     return totals
 
 
-def fill_weights(shape_ref, scale_ref, weight_ref):
-    @pl.loop(0, shape_ref.shape[0])
-    def _(block):
-        scale_row = scale_ref[block]
-        weights, offsets, logs = lag_weights(shape_ref[block], scale_row)
-        by_shape = weights * (logs - jnp.sum(weights * logs, axis=0, keepdims=True))
-        by_scale = weights * (offsets - jnp.sum(weights * offsets, axis=0, keepdims=True))
-        by_scale = by_scale / (scale_row * scale_row)
-        for chunk in range(2):
-            lanes = slice(chunk * LANES, (chunk + 1) * LANES)
-            for which, rows in enumerate((weights, by_shape, by_scale)):
-                weight_ref[block, chunk, which] = rows[:, lanes]
-
-
 def path_kernel(
-    days, level_ref, part_ref, down_ref, slot_ref, shape_ref, scale_ref, send_ref, weight_ref,
-    comp_ref, reach_weight_ref, order_ref, count_ref, term_ref, buf_ref,
+    level_ref, part_ref, down_ref, slot_ref, shape_ref, scale_ref, send_ref, weight_ref,
+    ends_ref, order_ref, count_ref,
 ):
-    fill_weights(shape_ref, scale_ref, reach_weight_ref)
     list_blocks(level_ref, order_ref, count_ref)
     me = part_ref[0]
     width = WIDTH
@@ -157,14 +142,20 @@
         weights = lag_weights(shape_row, scale_row)[0]
         weights = jnp.where(active, weights, jnp.where(krows == 0, 1.0, 0.0))
         weights = jnp.where(krows == KROWS - 1, node.astype(F32), weights)
-        term_ref[height : height + 1, :] = jnp.where(ends, 1.0, 0.0)
+        ends_ref[height : height + 1, :] = jnp.where(ends, 1.0, 0.0)
         for chunk in range(width // LANES):
             weight_ref[height, chunk] = weights[:, chunk * LANES : (chunk + 1) * LANES]
+    ends_ref[SENDS : SENDS + 1, :] = parent.astype(F32)
+
+
+def compose_kernel(ends_ref, weight_ref, comp_ref, buf_ref):
+    width = ends_ref.shape[1]
+    days = buf_ref.shape[1] - KROWS
     buf_ref[...] = jnp.zeros(buf_ref.shape, F32)
     first = iota((8, LANES), 0) == 0
     for height in range(1, SENDS):
         for chunk in range(height // 4, width // LANES):
-            ends = term_ref[height : height + 1, chunk * LANES : (chunk + 1) * LANES] > 0.5
+            ends = ends_ref[height : height + 1, chunk * LANES : (chunk + 1) * LANES] > 0.5
             start = buf_ref[chunk, KROWS : KROWS + 8, :]
             buf_ref[chunk, KROWS : KROWS + 8, :] = jnp.where(first & ends, 1.0, start)
 
@@ -177,25 +168,40 @@
     for chunk in range(width // LANES):
         lanes = slice(chunk * LANES, (chunk + 1) * LANES)
         comp_ref[0:days, lanes] = buf_ref[chunk, KROWS : KROWS + days, :]
-    comp_ref[days : days + 8, :] = jnp.broadcast_to(parent.astype(F32), (8, width))
-
-
-def grad_kernel(inflow_ref, weight_ref, grad_ref, buf_ref):
+    comp_ref[days : days + 8, :] = jnp.broadcast_to(ends_ref[SENDS : SENDS + 1, :], (8, width))
+
+
+def grad_kernel(inflow_ref, shape_ref, scale_ref, weight_ref, grad_ref, buf_ref, row_ref):
     days = inflow_ref.shape[0]
     buf_ref[...] = jnp.zeros(buf_ref.shape, F32)
 
     @pl.loop(0, weight_ref.shape[0])
     def _(block):
+        scale_row = scale_ref[block]
+        weights, offsets, logs = lag_weights(shape_ref[block], scale_row)
+        by_shape = weights * (logs - jnp.sum(weights * logs, axis=0, keepdims=True))
+        by_scale = weights * (offsets - jnp.sum(weights * offsets, axis=0, keepdims=True))
+        by_scale = by_scale / (scale_row * scale_row)
         for chunk in range(2):
             lanes = slice(chunk * LANES, (chunk + 1) * LANES)
+            weight_ref[block, chunk] = weights[:, lanes]
+            row_ref[chunk, 0] = by_shape[:, lanes]
+            row_ref[chunk, 1] = by_scale[:, lanes]
             at = pl.ds(pl.multiple_of(block * BLK + chunk * LANES, LANES), LANES)
-            buf_ref[chunk, KROWS : KROWS + days, :] = inflow_ref[:, at]
-            rows = [
-                lambda lag, chunk=chunk, which=which: weight_ref[block, chunk, which, lag : lag + 1, :]
-                for which in (1, 2)
-            ]
-            for which, total in enumerate(lag_sum_forward(buf_ref, chunk, rows, 2 * days)):
-                grad_ref[block, which, :, lanes] = total
+            buf_ref[chunk, 8 : 8 + days, :] = inflow_ref[:, at]
+        for chunk in range(2):
+            lanes = slice(chunk * LANES, (chunk + 1) * LANES)
+            totals = [[jnp.zeros((8, LANES), F32) for _ in range(days // 4)] for _ in range(2)]
+            for shift in range(8):
+                shifted = buf_ref[chunk, pl.ds(8 - shift, days + 8), :]
+                for lag in range(shift, LAGS, 8):
+                    for which, tiles in enumerate(totals):
+                        weight = row_ref[chunk, which, lag : lag + 1, :]
+                        for tile in range(days // 8 + 1):
+                            at = tile + lag // 8
+                            tiles[at] = tiles[at] + weight * shifted[8 * tile : 8 * tile + 8]
+            for which, tiles in enumerate(totals):
+                grad_ref[block, which, :, lanes] = jnp.concatenate(tiles, axis=0)
 
 
 def gather_terms(pieces, terms_ref):
@@ -375,7 +381,7 @@
                 for which in range(2):
                     grads = adjoint[: 2 * own_days, lanes] * grad_ref[block, which, :, lanes]
                     param_ref[which : which + 1, at] = jnp.sum(grads, axis=0, keepdims=True)
-                row = lambda lag, chunk=chunk: weight_ref[block, chunk, 0, lag : lag + 1, :]
+                row = lambda lag, chunk=chunk: weight_ref[block, chunk, lag : lag + 1, :]
                 result = lag_sum(adj_ref, chunk, row, need)
                 out_ref[:, at] = result[:own_days]
                 if height + 1 < LEVELS:
@@ -431,20 +437,29 @@
     return values.reshape(-1, 1, BLK)
 
 
-def sent_paths(days, block_level, part, shape_param, scale_param, down_local, in_slot, sends):
+def sent_paths(block_level, part, shape_param, scale_param, down_local, in_slot, sends):
     return call(
-        functools.partial(path_kernel, days),
+        path_kernel,
         (
             jax.ShapeDtypeStruct((SENDS, 2, KROWS, LANES), F32),
-            jax.ShapeDtypeStruct((days + 8, WIDTH), F32),
-            jax.ShapeDtypeStruct((block_level.shape[0], 2, 3, KROWS, LANES), F32),
+            jax.ShapeDtypeStruct((SENDS + 1, WIDTH), F32),
         ),
         [block_level, part],
         [by_block(down_local), by_block(in_slot), by_block(shape_param), by_block(scale_param), sends],
-        kernel_tables()
-        + [pltpu.VMEM((8, WIDTH), F32), pltpu.VMEM((2, KROWS + days, LANES), F32)],
+        kernel_tables(),
+        9_000_000_000,
+        56 * 1024 * 1024,
+    )
+
+
+def composed_paths(days, ends, path_weights):
+    return call(
+        compose_kernel,
+        jax.ShapeDtypeStruct((days + 8, WIDTH), F32),
+        [],
+        [ends, path_weights],
+        [pltpu.VMEM((2, KROWS + days, LANES), F32)],
         1_000_000,
-        56 * 1024 * 1024,
     )
 
 
@@ -479,14 +494,18 @@
     )
 
 
-def day_grads(inflow, weights):
+def day_grads(inflow, shape_param, scale_param):
     own_days = inflow.shape[0]
+    blocks = shape_param.shape[0] // BLK
     return call(
         grad_kernel,
-        jax.ShapeDtypeStruct((weights.shape[0], 2, 2 * own_days, BLK), F32),
+        (
+            jax.ShapeDtypeStruct((blocks, 2, KROWS, LANES), F32),
+            jax.ShapeDtypeStruct((blocks, 2, 2 * own_days, BLK), F32),
+        ),
         [],
-        [inflow, weights],
-        [pltpu.VMEM((2, KROWS + 2 * own_days, LANES), F32)],
+        [inflow, by_block(shape_param), by_block(scale_param)],
+        [pltpu.VMEM((2, own_days + 16, LANES), F32), pltpu.VMEM((2, 2, KROWS, LANES), F32)],
         1_000_000,
     )
 
@@ -525,24 +544,24 @@
     days = shards * own_days
     gauge_ids = gauge_columns(gauge_reach)
     part = after(lax.axis_index("basin").astype(jnp.int32).reshape(1), gauge_ids)
-    path_weights, composed, weights = sent_paths(
-        days, block_level, part, shape_param, scale_param, down_local, in_slot, send_reach.reshape(SENDS, 1, KROWS)
+    path_weights, ends = sent_paths(
+        block_level, part, shape_param, scale_param, down_local, in_slot, send_reach.reshape(SENDS, 1, KROWS)
     )
     back = lambda by, reach: [(i + by, i) for i in range(shards - reach)]
     following = lax.ppermute(cotangent, "tm", back(1, 1))
-    following, composed, path_weights = lax.optimization_barrier((following, composed, path_weights))
+    following, ends, path_weights = lax.optimization_barrier((following, ends, path_weights))
     second = lax.ppermute(following, "tm", back(1, 2))
     third = lax.ppermute(following, "tm", back(2, 3))
     early = jnp.concatenate([cotangent, following], axis=0)
     path_weights = jnp.pad(path_weights, ((0, 1), (0, 0), (0, 0), (0, 0)))
-    composed = jnp.concatenate([composed[None], exchange(composed[None], "basin", 2)], axis=0)
-    composed, early, path_weights, weights = lax.optimization_barrier(
-        (composed, early, path_weights, weights)
-    )
-    grads = day_grads(inflow, weights)
+    composed = composed_paths(days, ends, path_weights)[None]
+    composed, own_inflow = lax.optimization_barrier((composed, inflow))
+    weights, grads = day_grads(own_inflow, shape_param, scale_param)
+    composed = jnp.concatenate([composed, exchange(composed, "basin", 2)], axis=0)
+    composed, early, path_weights, grads = lax.optimization_barrier((composed, early, path_weights, grads))
     composed = jnp.concatenate([composed, exchange(composed, "basin", 4)], axis=0)
     composed = (composed, exchange(composed, "basin", 1))
-    third, second, grads = lax.optimization_barrier((third, second, grads))
+    third, second, path_weights = lax.optimization_barrier((third, second, path_weights))
     pieces = [early, second, third]
     adjoints = path_adjoints(pieces, gauge_ids, path_weights)
     seeds = reach_seeds(pieces, gauge_reach, gauge_ids, blocks)

time: 69.6 us -> 67.9 us (0.976)
  other arithmetic: 2.59 us -> 0.74 us
  Pallas kernels: 37 us -> 35.2 us
  waiting for transfers between devices: 11.3 us -> 12.1 us
  local copies, waits for them, and re-layouts: 2.05 us -> 2.75 us
    ppermute x10, waiting for transfers between devices: 8.4 us -> 3.98 us  [exchange(): lax.ppermute(values, axis, [(i, i ^ by) for i in range(lax.axis_size(axis...]
    ppermute x1, waiting for transfers between devices: 0.01 us -> 3.36 us  [fast_shards(): third = lax.ppermute(following, 'tm', back(2, 3))]
    ppermute x1, waiting for transfers between devices: 1.87 us -> 4.71 us  [fast_shards(): following = lax.ppermute(cotangent, 'tm', back(1, 1))]
    pallas_call x5 -> x6, Pallas kernels: 37 us -> 35.2 us  [call(): pl.pallas_call(kernel, out_shape=out_shape, in_specs=[smem] * len(in_smem...]
    ppermute x1, waiting for transfers between devices: 0.99 us -> 0.01 us  [fast_shards(): second = lax.ppermute(following, 'tm', back(1, 2))]
    concatenate x1, other arithmetic: 0.98 us -> 0.03 us  [fast_shards(): early = jnp.concatenate([cotangent, following], axis=0)]
    concatenate x1, other arithmetic: 0.93 us -> 0.02 us  [fast_shards(): jnp.concatenate([composed, exchange(composed, 'basin', 2)], axis=0)]
    unnamed x13 -> x19, local copies, waits for them, and re-layouts: 0.05 us -> 0.75 us
  transfers between devices with their start and end apart: 13 -> 13, of which waited for: 7 -> 5; matrix products, arithmetic and copies ran while one was open for 6% -> 3% of each run, Pallas kernels for 31% -> 29%
where the time goes in v3:
time: 67.9 us; the launch traced here: 67.4 us
  Pallas kernels  35.2 us (52%)
  starting transfers between devices  15.7 us (23%)
  waiting for transfers between devices  12.1 us (18%)
  local copies, waits for them, and re-layouts  2.75 us (4%)
  between operations  0.87 us (1%)
  other arithmetic  0.74 us (1%)
    pallas_call x6, Pallas kernels, call(): pl.pallas_call(kernel, out_shape=out_shape, in_specs=[smem] * len(in_smem...  35.2 us
    ppermute x10, starting transfers between devices, exchange(): lax.ppermute(values, axis, [(i, i ^ by) for i in range(lax.axis_size(axis...  11.9 us
    ppermute x1, waiting for transfers between devices, fast_shards(): following = lax.ppermute(cotangent, 'tm', back(1, 1))  4.71 us
    ppermute x10, waiting for transfers between devices, exchange(): lax.ppermute(values, axis, [(i, i ^ by) for i in range(lax.axis_size(axis...  3.98 us
    ppermute x1, waiting for transfers between devices, fast_shards(): third = lax.ppermute(following, 'tm', back(2, 3))  3.36 us
  transfers between devices with their start and end apart: 13, of which 5 were waited for; matrix products, arithmetic and copies ran while one was open for 3% of the time, Pallas kernels for 29%

profile of v3, /device:TPU:0, one launch (start us, length us, event | category | flops | bytes accessed | tf_op | source)
XLA Modules:
  0.0 67.4 jit_solution(4952897358718048482)
XLA Ops:
  0.6 1.3 %collective-permute-start = (f32[32,2048]{1,0:T(8,128)}, f32[32,2048]{1,0:T(8,128)S(1)}, u32[]{:S(2)}, u32[]{:S(2)}) collective-permute-start(f32[32,2048]{1,0:T(8,128)} %param.10), channel_id=1, source_target_pairs={{1,0},{2,1},{3,2},{5,4},{6,5},{7,6},{9,8},{10,9},{11,10},{13,12},{... | collective-permute-start | bytes 786440 | tf_op jit(solution)/shard_map/ppermute | solution.py:551
  1.9 1.0 %broadcast_in_dim.4.refs_3_.refs_4_ = s32[2048,128]{1,0:T(8,128)S(1)} broadcast(s32[2048]{0:T(1024)} %param.11), dimensions={0} | broadcast | bytes 1056768 | tf_op jit(solution)/shard_map/broadcast_in_dim | solution.py:429
  3.0 0.0 copy-start.8
  3.0 0.0 copy-start.1
  3.0 0.0 copy-start.2
  3.0 4.4 %shard_map.104 = (f32[7,2,32,128]{3,2,1,0:T(8,128)}, f32[8,256]{1,0:T(8,128)}) custom-call(s32[16]{0:T(128)} %level_ref.3, s32[1]{0:T(128)} %bitcast.part_ref, s32[16,1,256]{2,1,0:T(1,128)} %bitcast.20, s32[16,1,256]{2,1,0:T(1,128)} %bitcast.22, f32[16,1,256]{2,1,0:T(1,128)} %bitcast.15, f32[16,1,256]{2,1,0:T(1,128)} %bitcast.17, s32[7,1,32]{2,1,0:T(1,128)} %bitcast.27), custom_call_target="tpu_custom_call" | custom-call | flops 8999999488 | bytes 9000000 | tf_op jit(solution)/shard_map/pallas_call | solution.py:403
  7.4 0.0 copy-start
  7.4 4.7 %collective-permute-done = f32[32,2048]{1,0:T(8,128)S(1)} collective-permute-done((f32[32,2048]{1,0:T(8,128)}, f32[32,2048]{1,0:T(8,128)S(1)}, u32[]{:S(2)}, u32[]{:S(2)}) %collective-permute-start) | collective-permute-done | bytes 262176 | tf_op jit(solution)/shard_map/ppermute | solution.py:551
  12.1 1.3 %collective-permute-start.3 = (f32[32,2048]{1,0:T(8,128)S(1)}, f32[32,2048]{1,0:T(8,128)S(1)}, u32[]{:S(2)}, u32[]{:S(2)}) collective-permute-start(f32[32,2048]{1,0:T(8,128)S(1)} %collective-permute-done), channel_id=1, source_target_pairs={{1,0},{2,1},{5,4},{6,5},{9,8},{10,9},{13,12},{14,13},{17,16},{18,1... | collective-permute-start | bytes 786440 | tf_op jit(solution)/shard_map/ppermute | solution.py:553
  13.4 1.3 %collective-permute-start.2 = (f32[32,2048]{1,0:T(8,128)S(1)}, f32[32,2048]{1,0:T(8,128)S(1)}, u32[]{:S(2)}, u32[]{:S(2)}) collective-permute-start(f32[32,2048]{1,0:T(8,128)S(1)} %collective-permute-done), channel_id=1, source_target_pairs={{2,0},{6,4},{10,8},{14,12},{18,16},{22,20},{26,24},{30,28}} | collective-permute-start | bytes 786440 | tf_op jit(solution)/shard_map/ppermute | solution.py:554
  14.7 1.0 %pad.4.weight_ref.refs_4_ = f32[8,2,32,128]{3,2,1,0:T(8,128)S(1)} pad(f32[7,2,32,128]{3,2,1,0:T(8,128)} %get-tuple-element.26, f32[]{:T(128)} %constant.8.clone.1), padding=0_1x0_0x0_0x0_0 | pad | bytes 491524 | tf_op jit(solution)/shard_map/jit(_pad)/pad | solution.py:556
  15.6 0.0 copy-start.4
  15.6 0.7 %copy-done.4 = f32[8,256]{1,0:T(8,128)S(1)} copy-done((f32[8,256]{1,0:T(8,128)S(1)}, f32[8,256]{1,0:T(8,128)}, u32[]{:S(2)}) %copy-start.4) | copy-done | bytes 8216
  16.3 1.3 %shard_map.105 = f32[136,256]{1,0:T(8,128)S(1)} custom-call(f32[8,256]{1,0:T(8,128)S(1)} %copy-done.4, f32[8,2,32,128]{3,2,1,0:T(8,128)S(1)} %pad.4.weight_ref.refs_4_), custom_call_target="tpu_custom_call" | custom-call | flops 1000000 | bytes 1000 | tf_op jit(solution)/shard_map/pallas_call | solution.py:403
  17.6 1.7 %collective-permute-start.1 = (f32[1,136,256]{2,1,0:T(8,128)S(1)}, f32[1,136,256]{2,1,0:T(8,128)S(1)}, u32[]{:S(2)}, u32[]{:S(2)}) collective-permute-start(f32[1,136,256]{2,1,0:T(8,128)S(1)} %bitcast.12), channel_id=1, source_target_pairs={{0,8},{4,12},{8,0},{12,4},{16,24},{20,28},{24,16},{28,20},{1,9},{5... | collective-permute-start | bytes 417800 | tf_op jit(solution)/shard_map/ppermute | solution.py:419
  19.3 0.0 copy-done.8
  19.4 0.0 copy-done.1
  19.4 0.0 copy-done.2
  19.4 0.0 copy-done
  19.4 3.4 %shard_map.106 = (f32[16,2,32,128]{3,2,1,0:T(8,128)S(1)}, f32[16,2,64,256]{3,2,1,0:T(8,128)S(1)}) custom-call(f32[32,4096]{1,0:T(8,128)S(1)} %copy-done, f32[16,1,256]{2,1,0:T(1,128)S(1)} %bitcast.16, f32[16,1,256]{2,1,0:T(1,128)S(1)} %bitcast.18), custom_call_target="tpu_custom_call" | custom-call | flops 1000000 | bytes 1000 | tf_op jit(solution)/shard_map/pallas_call | solution.py:403
  22.9 0.0 collective-permute-done.1
  22.9 1.6 %collective-permute-start.8 = (f32[2,136,256]{2,1,0:T(8,128)S(1)}, f32[2,136,256]{2,1,0:T(8,128)S(1)}, u32[]{:S(2)}, u32[]{:S(2)}) collective-permute-start(f32[2,136,256]{2,1,0:T(8,128)S(1)} %pad_maximum_fusion.2), channel_id=1, source_target_pairs={{0,16},{4,20},{8,24},{12,28},{16,0},{20,4},{24,8},{28,12},{1,17},{... | collective-permute-start | bytes 835592 | tf_op jit(solution)/shard_map/ppermute | solution.py:419
  24.5 0.0 copy-start.3
  24.5 0.0 collective-permute-done.3.refs_1_
  24.6 3.4 %collective-permute-done.2.refs_2_ = f32[32,2048]{1,0:T(8,128)S(1)} collective-permute-done((f32[32,2048]{1,0:T(8,128)S(1)}, f32[32,2048]{1,0:T(8,128)S(1)}, u32[]{:S(2)}, u32[]{:S(2)}) %collective-permute-start.2) | collective-permute-done | bytes 262176 | tf_op jit(solution)/shard_map/ppermute | solution.py:554
  27.9 4.8 %shard_map.107 = f32[128,256]{1,0:T(8,128)S(1)} custom-call(f32[64,2048]{1,0:T(8,128)S(1)} %pad_maximum_fusion.refs_0_, f32[32,2048]{1,0:T(8,128)S(1)} %collective-permute-done.3.refs_1_, f32[32,2048]{1,0:T(8,128)S(1)} %collective-permute-done.2.refs_2_, s32[2048,128]{1,0:T(8,128)S(1)} %broadcast_in_dim.4.refs_3_.refs_4_, ...), custom_call_target="tpu_custom_call" | custom-call | flops 4000000000 | bytes 4000000 | tf_op jit(solution)/shard_map/pallas_call | solution.py:403
  32.7 2.5 %collective-permute-start.6 = (f32[128,256]{1,0:T(8,128)S(1)}, f32[128,256]{1,0:T(8,128)S(1)}, u32[]{:S(2)}, u32[]{:S(2)}) collective-permute-start(f32[128,256]{1,0:T(8,128)S(1)} %shard_map.107), channel_id=1, source_target_pairs={{0,24},{4,28},{8,16},{12,20},{16,8},{20,12},{24,0},{28,4},{1,25},{... | collective-permute-start | bytes 393224 | tf_op jit(solution)/shard_map/ppermute | solution.py:419
  35.2 0.5 collective-permute-start.5
  35.7 0.5 collective-permute-start.4
  36.3 0.0 copy-done.3
  36.3 0.0 copy-start.5
  36.3 0.0 copy-start.6
  36.3 0.0 copy-start.7
  36.3 5.5 %shard_map.108.seed_ref = f32[16,128,256]{2,1,0:T(8,128)S(1)} custom-call(f32[64,2048]{1,0:T(8,128)S(1)} %pad_maximum_fusion.refs_0_, f32[32,2048]{1,0:T(8,128)S(1)} %collective-permute-done.3.refs_1_, f32[32,2048]{1,0:T(8,128)S(1)} %collective-permute-done.2.refs_2_, s32[1,2048]{1,0:T(1,128)S(1)} %bitcast.19, s32[2048,128]{1,0:T(8,128)S(1)} %broadcast_in_dim.4.refs_3_.refs_4_), custom_call_target="tpu_custom_call" | custom-call | flops 3000000000 | bytes 3000000 | tf_op jit(solution)/shard_map/pallas_call | solution.py:403
  41.8 0.0 collective-permute-done.8
  41.8 0.1 collective-permute-start.9
  41.9 0.0 collective-permute-done.6
  41.9 0.0 collective-permute-done.5
  41.9 0.0 collective-permute-done.4
  41.9 0.5 collective-permute-start.7
  42.5 2.1 %collective-permute-done.7.a_mate_ref = f32[4,128,256]{2,1,0:T(8,128)S(1)} collective-permute-done((f32[4,128,256]{2,1,0:T(8,128)S(1)}, f32[4,128,256]{2,1,0:T(8,128)S(1)}, u32[]{:S(2)}, u32[]{:S(2)}) %collective-permute-start.7) | collective-permute-done | bytes 524320 | tf_op jit(solution)/shard_map/ppermute | solution.py:419
  44.6 0.0 collective-permute-done.9.c_mate_ref
  44.6 0.0 copy-done.5
  44.6 0.0 copy-done.6
  44.6 0.0 copy-done.7
  44.6 15.8 %shard_map.109 = (f32[32,4096]{1,0:T(8,128)}, f32[2,4096]{1,0:T(2,128)S(1)}) custom-call(s32[16]{0:T(128)S(1)} %copy-done.7, s32[1]{0:T(128)} %bitcast.part_ref, f32[4,128,256]{2,1,0:T(8,128)S(1)} %pad_maximum_fusion.1.a_own_ref, f32[4,128,256]{2,1,0:T(8,128)S(1)} %collective-permute-done.7.a_mate_ref, ...), custom_call_target="tpu_custom_call" | custom-call | flops 10000000000 | bytes 10000000 | tf_op jit(solution)/shard_map/pallas_call | solution.py:403
  60.4 0.0 collective-permute-start.12
  60.4 0.3 collective-permute-start.11
  60.8 4.1 %collective-permute-start.10 = (f32[2,4096]{1,0:T(2,128)S(1)}, f32[2,4096]{1,0:T(2,128)S(1)}, u32[]{:S(2)}, u32[]{:S(2)}) collective-permute-start(f32[2,4096]{1,0:T(2,128)S(1)} %get-tuple-element.41), channel_id=1, source_target_pairs={{0,1},{1,0},{2,3},{3,2},{4,5},{5,4},{6,7},{7,6},{8,9},{9,8},{10,11... | collective-permute-start | bytes 98312 | tf_op jit(solution)/shard_map/ppermute | solution.py:419
  64.8 1.3 %collective-permute-done.12 = f32[2,4096]{1,0:T(2,128)S(1)} collective-permute-done((f32[2,4096]{1,0:T(2,128)S(1)}, f32[2,4096]{1,0:T(2,128)S(1)}, u32[]{:S(2)}, u32[]{:S(2)}) %collective-permute-start.12) | collective-permute-done | bytes 32800 | tf_op jit(solution)/shard_map/ppermute | solution.py:419
  66.1 0.0 collective-permute-done.11
  66.2 0.6 collective-permute-done.10
  66.7 0.6 add_add_fusion
  (5 shorter events, 0.1 us)
Async XLA Ops:
  0.6 11.4 %collective-permute-start = (f32[32,2048]{1,0:T(8,128)}, f32[32,2048]{1,0:T(8,128)S(1)}, u32[]{:S(2)}, u32[]{:S(2)}) collective-permute-start(f32[32,2048]{1,0:T(8,128)} %param.10), channel_id=1, source_target_pairs={{1,0},{2,1},{3,2},{5,4},{6,5},{7,6},{9,8},{10,9},{11,10},{13,12},{... | collective-permute-start | bytes 786440 | tf_op jit(solution)/shard_map/ppermute | solution.py:551
  3.0 16.4 %copy-start.8 = (f32[32,2048]{1,0:T(8,128)S(1)}, f32[32,2048]{1,0:T(8,128)}, u32[]{:S(2)}) copy-start(f32[32,2048]{1,0:T(8,128)} %param.10) | copy-start | bytes 786436
  3.0 16.4 %copy-start.1 = (f32[4096]{0:T(1024)S(1)}, f32[4096]{0:T(1024)}, u32[]{:S(2)}) copy-start(f32[4096]{0:T(1024)} %param.12) | copy-start | bytes 49156
  3.0 16.4 %copy-start.2 = (f32[4096]{0:T(1024)S(1)}, f32[4096]{0:T(1024)}, u32[]{:S(2)}) copy-start(f32[4096]{0:T(1024)} %param.13) | copy-start | bytes 49156
  7.4 12.0 %copy-start = (f32[32,4096]{1,0:T(8,128)S(1)}, f32[32,4096]{1,0:T(8,128)}, u32[]{:S(2)}) copy-start(f32[32,4096]{1,0:T(8,128)} %inflow_ref) | copy-start | bytes 1572868
  12.1 12.5 %collective-permute-start.3 = (f32[32,2048]{1,0:T(8,128)S(1)}, f32[32,2048]{1,0:T(8,128)S(1)}, u32[]{:S(2)}, u32[]{:S(2)}) collective-permute-start(f32[32,2048]{1,0:T(8,128)S(1)} %collective-permute-done), channel_id=1, source_target_pairs={{1,0},{2,1},{5,4},{6,5},{9,8},{10,9},{13,12},{14,13},{17,16},{18,1... | collective-permute-start | bytes 786440 | tf_op jit(solution)/shard_map/ppermute | solution.py:553
  13.4 14.6 %collective-permute-start.2 = (f32[32,2048]{1,0:T(8,128)S(1)}, f32[32,2048]{1,0:T(8,128)S(1)}, u32[]{:S(2)}, u32[]{:S(2)}) collective-permute-start(f32[32,2048]{1,0:T(8,128)S(1)} %collective-permute-done), channel_id=1, source_target_pairs={{2,0},{6,4},{10,8},{14,12},{18,16},{22,20},{26,24},{30,28}} | collective-permute-start | bytes 786440 | tf_op jit(solution)/shard_map/ppermute | solution.py:554
  15.6 0.7 %copy-start.4 = (f32[8,256]{1,0:T(8,128)S(1)}, f32[8,256]{1,0:T(8,128)}, u32[]{:S(2)}) copy-start(f32[8,256]{1,0:T(8,128)} %get-tuple-element.25.ends_ref) | copy-start | bytes 24580
  17.6 5.2 %collective-permute-start.1 = (f32[1,136,256]{2,1,0:T(8,128)S(1)}, f32[1,136,256]{2,1,0:T(8,128)S(1)}, u32[]{:S(2)}, u32[]{:S(2)}) collective-permute-start(f32[1,136,256]{2,1,0:T(8,128)S(1)} %bitcast.12), channel_id=1, source_target_pairs={{0,8},{4,12},{8,0},{12,4},{16,24},{20,28},{24,16},{28,20},{1,9},{5... | collective-permute-start | bytes 417800 | tf_op jit(solution)/shard_map/ppermute | solution.py:419
  22.9 18.9 %collective-permute-start.8 = (f32[2,136,256]{2,1,0:T(8,128)S(1)}, f32[2,136,256]{2,1,0:T(8,128)S(1)}, u32[]{:S(2)}, u32[]{:S(2)}) collective-permute-start(f32[2,136,256]{2,1,0:T(8,128)S(1)} %pad_maximum_fusion.2), channel_id=1, source_target_pairs={{0,16},{4,20},{8,24},{12,28},{16,0},{20,4},{24,8},{28,12},{1,17},{... | collective-permute-start | bytes 835592 | tf_op jit(solution)/shard_map/ppermute | solution.py:419
  24.5 11.7 %copy-start.3 = (s32[2048]{0:T(1024)S(1)}, s32[2048]{0:T(1024)}, u32[]{:S(2)}) copy-start(s32[2048]{0:T(1024)} %param.11) | copy-start | bytes 24580
  32.7 9.2 %collective-permute-start.6 = (f32[128,256]{1,0:T(8,128)S(1)}, f32[128,256]{1,0:T(8,128)S(1)}, u32[]{:S(2)}, u32[]{:S(2)}) collective-permute-start(f32[128,256]{1,0:T(8,128)S(1)} %shard_map.107), channel_id=1, source_target_pairs={{0,24},{4,28},{8,16},{12,20},{16,8},{20,12},{24,0},{28,4},{1,25},{... | collective-permute-start | bytes 393224 | tf_op jit(solution)/shard_map/ppermute | solution.py:419
  35.2 6.7 %collective-permute-start.5 = (f32[128,256]{1,0:T(8,128)S(1)}, f32[128,256]{1,0:T(8,128)S(1)}, u32[]{:S(2)}, u32[]{:S(2)}) collective-permute-start(f32[128,256]{1,0:T(8,128)S(1)} %shard_map.107), channel_id=1, source_target_pairs={{0,16},{4,20},{8,24},{12,28},{16,0},{20,4},{24,8},{28,12},{1,17},{... | collective-permute-start | bytes 393224 | tf_op jit(solution)/shard_map/ppermute | solution.py:419
  35.7 6.2 %collective-permute-start.4 = (f32[128,256]{1,0:T(8,128)S(1)}, f32[128,256]{1,0:T(8,128)S(1)}, u32[]{:S(2)}, u32[]{:S(2)}) collective-permute-start(f32[128,256]{1,0:T(8,128)S(1)} %shard_map.107), channel_id=1, source_target_pairs={{0,8},{4,12},{8,0},{12,4},{16,24},{20,28},{24,16},{28,20},{1,9},{5... | collective-permute-start | bytes 393224 | tf_op jit(solution)/shard_map/ppermute | solution.py:419
  36.3 8.3 %copy-start.5 = (s32[4096]{0:T(1024)S(1)}, s32[4096]{0:T(1024)}, u32[]{:S(2)}) copy-start(s32[4096]{0:T(1024)} %param.15) | copy-start | bytes 49156
  36.3 8.3 %copy-start.6 = (s32[4096]{0:T(1024)S(1)}, s32[4096]{0:T(1024)}, u32[]{:S(2)}) copy-start(s32[4096]{0:T(1024)} %param.16) | copy-start | bytes 49156
  36.3 8.3 %copy-start.7 = (s32[16]{0:T(128)S(1)}, s32[16]{0:T(128)}, u32[]{:S(2)}) copy-start(s32[16]{0:T(128)} %level_ref.3) | copy-start | bytes 196
  41.8 2.8 %collective-permute-start.9 = (f32[4,136,256]{2,1,0:T(8,128)S(1)}, f32[4,136,256]{2,1,0:T(8,128)S(1)}, u32[]{:S(2)}, u32[]{:S(2)}) collective-permute-start(f32[4,136,256]{2,1,0:T(8,128)S(1)} %constant_dynamic-update-slice_fusion.c_own_ref), channel_id=1, source_target_pairs={{0,4},{4,0},{8,12},{12,8},{16,20},{20,16},{24,28},{28,24},{1,5},{5... | collective-permute-start | bytes 1671176 | tf_op jit(solution)/shard_map/ppermute | solution.py:419
  41.9 2.6 %collective-permute-start.7 = (f32[4,128,256]{2,1,0:T(8,128)S(1)}, f32[4,128,256]{2,1,0:T(8,128)S(1)}, u32[]{:S(2)}, u32[]{:S(2)}) collective-permute-start(f32[4,128,256]{2,1,0:T(8,128)S(1)} %pad_maximum_fusion.1.a_own_ref), channel_id=1, source_target_pairs={{0,4},{4,0},{8,12},{12,8},{16,20},{20,16},{24,28},{28,24},{1,5},{5... | collective-permute-start | bytes 1572872 | tf_op jit(solution)/shard_map/ppermute | solution.py:419
  60.4 5.7 %collective-permute-start.12 = (f32[2,4096]{1,0:T(2,128)S(1)}, f32[2,4096]{1,0:T(2,128)S(1)}, u32[]{:S(2)}, u32[]{:S(2)}) collective-permute-start(f32[2,4096]{1,0:T(2,128)S(1)} %get-tuple-element.41), channel_id=1, source_target_pairs={{0,3},{1,2},{2,1},{3,0},{4,7},{5,6},{6,5},{7,4},{8,11},{9,10},{10,... | collective-permute-start | bytes 98312 | tf_op jit(solution)/shard_map/ppermute | solution.py:419
  60.4 5.7 %collective-permute-start.11 = (f32[2,4096]{1,0:T(2,128)S(1)}, f32[2,4096]{1,0:T(2,128)S(1)}, u32[]{:S(2)}, u32[]{:S(2)}) collective-permute-start(f32[2,4096]{1,0:T(2,128)S(1)} %get-tuple-element.41), channel_id=1, source_target_pairs={{0,2},{1,3},{2,0},{3,1},{4,6},{5,7},{6,4},{7,5},{8,10},{9,11},{10,... | collective-permute-start | bytes 98312 | tf_op jit(solution)/shard_map/ppermute | solution.py:419
  60.8 5.9 %collective-permute-start.10 = (f32[2,4096]{1,0:T(2,128)S(1)}, f32[2,4096]{1,0:T(2,128)S(1)}, u32[]{:S(2)}, u32[]{:S(2)}) collective-permute-start(f32[2,4096]{1,0:T(2,128)S(1)} %get-tuple-element.41), channel_id=1, source_target_pairs={{0,1},{1,0},{2,3},{3,2},{4,5},{5,4},{6,7},{7,6},{8,9},{9,8},{10,11... | collective-permute-start | bytes 98312 | tf_op jit(solution)/shard_map/ppermute | solution.py:419

commit v4 on v3

--- a/solution.py
+++ b/solution.py
@@ -217,7 +217,11 @@
 
 def gauge_hits(gauge_ref, targets):
     return jnp.concatenate(
-        [one_hot(gauge_ref[...] == targets[:, c * LANES : (c + 1) * LANES]) for c in range(2)], axis=1
+        [
+            one_hot(gauge_ref[...] == targets[:, start : start + LANES])
+            for start in range(0, targets.shape[1], LANES)
+        ],
+        axis=1,
     )
 
 
@@ -232,13 +236,19 @@
     days = out_ref.shape[0]
     gather_terms(pieces, terms_ref)
 
-    @pl.loop(0, SENDS)
-    def _(height):
-        nodes = [weight_ref[height, chunk, KROWS - 1 : KROWS, :] for chunk in range(2)]
+    def fill(places):
+        nodes = [weight_ref[height, chunk, KROWS - 1 : KROWS, :] for height, chunk in places]
         nodes = jnp.round(jnp.concatenate(nodes, axis=1)).astype(jnp.int32)
         seeds = folded(product(terms_ref[...], gauge_hits(gauge_ref, nodes)))
-        for chunk in range(2):
-            seed_ref[height, chunk] = seeds[:, chunk * LANES : (chunk + 1) * LANES]
+        for number, (height, chunk) in enumerate(places):
+            seed_ref[height, chunk] = seeds[:, number * LANES : (number + 1) * LANES]
+
+    @pl.loop(0, 4)
+    def _(height):
+        fill([(height, 0), (height, 1)])
+
+    fill([(4, 1), (5, 1)])
+    fill([(6, 1)])
 
     for chunk in range(2):
         buf_ref[chunk] = jnp.zeros(buf_ref.shape[1:], F32)

time: 67.9 us -> 66.9 us (0.985)
  Pallas kernels: 35.2 us -> 34.2 us
    pallas_call x6, Pallas kernels: 35.2 us -> 34.2 us  [call(): pl.pallas_call(kernel, out_shape=out_shape, in_specs=[smem] * len(in_smem...]
  transfers between devices with their start and end apart: 13 -> 13, of which waited for: 5 -> 5; matrix products, arithmetic and copies ran while one was open for 3% -> 3% of each run, Pallas kernels for 29% -> 28%
where the time goes in v4:
time: 66.9 us; the launch traced here: 66.4 us
  Pallas kernels  34.2 us (51%)
  starting transfers between devices  15.7 us (23%)
  waiting for transfers between devices  12.1 us (18%)
  local copies, waits for them, and re-layouts  2.75 us (4%)
  between operations  0.87 us (1%)
  other arithmetic  0.74 us (1%)
    pallas_call x6, Pallas kernels, call(): pl.pallas_call(kernel, out_shape=out_shape, in_specs=[smem] * len(in_smem...  34.2 us
    ppermute x10, starting transfers between devices, exchange(): lax.ppermute(values, axis, [(i, i ^ by) for i in range(lax.axis_size(axis...  11.9 us
    ppermute x1, waiting for transfers between devices, fast_shards(): following = lax.ppermute(cotangent, 'tm', back(1, 1))  4.72 us
    ppermute x10, waiting for transfers between devices, exchange(): lax.ppermute(values, axis, [(i, i ^ by) for i in range(lax.axis_size(axis...  4.02 us
    ppermute x1, waiting for transfers between devices, fast_shards(): third = lax.ppermute(following, 'tm', back(2, 3))  3.36 us
  transfers between devices with their start and end apart: 13, of which 5 were waited for; matrix products, arithmetic and copies ran while one was open for 3% of the time, Pallas kernels for 28%

profile of v4, /device:TPU:0, one launch (start us, length us, event | category | flops | bytes accessed | tf_op | source)
XLA Modules:
  0.0 66.4 jit_solution(2737900393295350114)
XLA Ops:
  0.6 1.3 %collective-permute-start = (f32[32,2048]{1,0:T(8,128)}, f32[32,2048]{1,0:T(8,128)S(1)}, u32[]{:S(2)}, u32[]{:S(2)}) collective-permute-start(f32[32,2048]{1,0:T(8,128)} %param.10), channel_id=1, source_target_pairs={{1,0},{2,1},{3,2},{5,4},{6,5},{7,6},{9,8},{10,9},{11,10},{13,12},{... | collective-permute-start | bytes 786440 | tf_op jit(solution)/shard_map/ppermute | solution.py:561
  1.9 1.0 %broadcast_in_dim.4.refs_3_.refs_4_ = s32[2048,128]{1,0:T(8,128)S(1)} broadcast(s32[2048]{0:T(1024)} %param.11), dimensions={0} | broadcast | bytes 1056768 | tf_op jit(solution)/shard_map/broadcast_in_dim | solution.py:439
  3.0 0.0 copy-start.8
  3.0 0.0 copy-start.1
  3.0 0.0 copy-start.2
  3.0 4.4 %shard_map.104 = (f32[7,2,32,128]{3,2,1,0:T(8,128)}, f32[8,256]{1,0:T(8,128)}) custom-call(s32[16]{0:T(128)} %level_ref.3, s32[1]{0:T(128)} %bitcast.part_ref, s32[16,1,256]{2,1,0:T(1,128)} %bitcast.20, s32[16,1,256]{2,1,0:T(1,128)} %bitcast.22, f32[16,1,256]{2,1,0:T(1,128)} %bitcast.15, f32[16,1,256]{2,1,0:T(1,128)} %bitcast.17, s32[7,1,32]{2,1,0:T(1,128)} %bitcast.27), custom_call_target="tpu_custom_call" | custom-call | flops 8999999488 | bytes 9000000 | tf_op jit(solution)/shard_map/pallas_call | solution.py:413
  7.4 0.0 copy-start
  7.4 4.7 %collective-permute-done = f32[32,2048]{1,0:T(8,128)S(1)} collective-permute-done((f32[32,2048]{1,0:T(8,128)}, f32[32,2048]{1,0:T(8,128)S(1)}, u32[]{:S(2)}, u32[]{:S(2)}) %collective-permute-start) | collective-permute-done | bytes 262176 | tf_op jit(solution)/shard_map/ppermute | solution.py:561
  12.1 1.3 %collective-permute-start.3 = (f32[32,2048]{1,0:T(8,128)S(1)}, f32[32,2048]{1,0:T(8,128)S(1)}, u32[]{:S(2)}, u32[]{:S(2)}) collective-permute-start(f32[32,2048]{1,0:T(8,128)S(1)} %collective-permute-done), channel_id=1, source_target_pairs={{1,0},{2,1},{5,4},{6,5},{9,8},{10,9},{13,12},{14,13},{17,16},{18,1... | collective-permute-start | bytes 786440 | tf_op jit(solution)/shard_map/ppermute | solution.py:563
  13.4 1.3 %collective-permute-start.2 = (f32[32,2048]{1,0:T(8,128)S(1)}, f32[32,2048]{1,0:T(8,128)S(1)}, u32[]{:S(2)}, u32[]{:S(2)}) collective-permute-start(f32[32,2048]{1,0:T(8,128)S(1)} %collective-permute-done), channel_id=1, source_target_pairs={{2,0},{6,4},{10,8},{14,12},{18,16},{22,20},{26,24},{30,28}} | collective-permute-start | bytes 786440 | tf_op jit(solution)/shard_map/ppermute | solution.py:564
  14.7 1.0 %pad.4.weight_ref.refs_4_ = f32[8,2,32,128]{3,2,1,0:T(8,128)S(1)} pad(f32[7,2,32,128]{3,2,1,0:T(8,128)} %get-tuple-element.26, f32[]{:T(128)} %constant.8.clone.1), padding=0_1x0_0x0_0x0_0 | pad | bytes 491524 | tf_op jit(solution)/shard_map/jit(_pad)/pad | solution.py:566
  15.6 0.0 copy-start.4
  15.6 0.7 %copy-done.4 = f32[8,256]{1,0:T(8,128)S(1)} copy-done((f32[8,256]{1,0:T(8,128)S(1)}, f32[8,256]{1,0:T(8,128)}, u32[]{:S(2)}) %copy-start.4) | copy-done | bytes 8216
  16.3 1.3 %shard_map.105 = f32[136,256]{1,0:T(8,128)S(1)} custom-call(f32[8,256]{1,0:T(8,128)S(1)} %copy-done.4, f32[8,2,32,128]{3,2,1,0:T(8,128)S(1)} %pad.4.weight_ref.refs_4_), custom_call_target="tpu_custom_call" | custom-call | flops 1000000 | bytes 1000 | tf_op jit(solution)/shard_map/pallas_call | solution.py:413
  17.6 1.7 %collective-permute-start.1 = (f32[1,136,256]{2,1,0:T(8,128)S(1)}, f32[1,136,256]{2,1,0:T(8,128)S(1)}, u32[]{:S(2)}, u32[]{:S(2)}) collective-permute-start(f32[1,136,256]{2,1,0:T(8,128)S(1)} %bitcast.12), channel_id=1, source_target_pairs={{0,8},{4,12},{8,0},{12,4},{16,24},{20,28},{24,16},{28,20},{1,9},{5... | collective-permute-start | bytes 417800 | tf_op jit(solution)/shard_map/ppermute | solution.py:429
  19.3 0.0 copy-done.8
  19.4 0.0 copy-done.1
  19.4 0.0 copy-done.2
  19.4 0.0 copy-done
  19.4 3.4 %shard_map.106 = (f32[16,2,32,128]{3,2,1,0:T(8,128)S(1)}, f32[16,2,64,256]{3,2,1,0:T(8,128)S(1)}) custom-call(f32[32,4096]{1,0:T(8,128)S(1)} %copy-done, f32[16,1,256]{2,1,0:T(1,128)S(1)} %bitcast.16, f32[16,1,256]{2,1,0:T(1,128)S(1)} %bitcast.18), custom_call_target="tpu_custom_call" | custom-call | flops 1000000 | bytes 1000 | tf_op jit(solution)/shard_map/pallas_call | solution.py:413
  22.9 0.0 collective-permute-done.1
  22.9 1.6 %collective-permute-start.8 = (f32[2,136,256]{2,1,0:T(8,128)S(1)}, f32[2,136,256]{2,1,0:T(8,128)S(1)}, u32[]{:S(2)}, u32[]{:S(2)}) collective-permute-start(f32[2,136,256]{2,1,0:T(8,128)S(1)} %pad_maximum_fusion.2), channel_id=1, source_target_pairs={{0,16},{4,20},{8,24},{12,28},{16,0},{20,4},{24,8},{28,12},{1,17},{... | collective-permute-start | bytes 835592 | tf_op jit(solution)/shard_map/ppermute | solution.py:429
  24.5 0.0 copy-start.3
  24.5 0.0 collective-permute-done.3.refs_1_
  24.6 3.4 %collective-permute-done.2.refs_2_ = f32[32,2048]{1,0:T(8,128)S(1)} collective-permute-done((f32[32,2048]{1,0:T(8,128)S(1)}, f32[32,2048]{1,0:T(8,128)S(1)}, u32[]{:S(2)}, u32[]{:S(2)}) %collective-permute-start.2) | collective-permute-done | bytes 262176 | tf_op jit(solution)/shard_map/ppermute | solution.py:564
  27.9 4.2 %shard_map.107 = f32[128,256]{1,0:T(8,128)S(1)} custom-call(f32[64,2048]{1,0:T(8,128)S(1)} %pad_maximum_fusion.refs_0_, f32[32,2048]{1,0:T(8,128)S(1)} %collective-permute-done.3.refs_1_, f32[32,2048]{1,0:T(8,128)S(1)} %collective-permute-done.2.refs_2_, s32[2048,128]{1,0:T(8,128)S(1)} %broadcast_in_dim.4.refs_3_.refs_4_, ...), custom_call_target="tpu_custom_call" | custom-call | flops 4000000000 | bytes 4000000 | tf_op jit(solution)/shard_map/pallas_call | solution.py:413
  32.1 2.5 %collective-permute-start.6 = (f32[128,256]{1,0:T(8,128)S(1)}, f32[128,256]{1,0:T(8,128)S(1)}, u32[]{:S(2)}, u32[]{:S(2)}) collective-permute-start(f32[128,256]{1,0:T(8,128)S(1)} %shard_map.107), channel_id=1, source_target_pairs={{0,24},{4,28},{8,16},{12,20},{16,8},{20,12},{24,0},{28,4},{1,25},{... | collective-permute-start | bytes 393224 | tf_op jit(solution)/shard_map/ppermute | solution.py:429
  34.6 0.5 collective-permute-start.5
  35.1 0.5 collective-permute-start.4
  35.6 0.0 copy-done.3
  35.6 0.0 copy-start.5
  35.6 0.0 copy-start.6
  35.6 0.0 copy-start.7
  35.6 5.5 %shard_map.108.seed_ref = f32[16,128,256]{2,1,0:T(8,128)S(1)} custom-call(f32[64,2048]{1,0:T(8,128)S(1)} %pad_maximum_fusion.refs_0_, f32[32,2048]{1,0:T(8,128)S(1)} %collective-permute-done.3.refs_1_, f32[32,2048]{1,0:T(8,128)S(1)} %collective-permute-done.2.refs_2_, s32[1,2048]{1,0:T(1,128)S(1)} %bitcast.19, s32[2048,128]{1,0:T(8,128)S(1)} %broadcast_in_dim.4.refs_3_.refs_4_), custom_call_target="tpu_custom_call" | custom-call | flops 3000000000 | bytes 3000000 | tf_op jit(solution)/shard_map/pallas_call | solution.py:413
  41.1 0.0 collective-permute-done.8
  41.2 0.1 collective-permute-start.9
  41.2 0.0 collective-permute-done.6
  41.2 0.0 collective-permute-done.5
  41.3 0.0 collective-permute-done.4
  41.3 0.5 collective-permute-start.7
  41.9 2.1 %collective-permute-done.7.a_mate_ref = f32[4,128,256]{2,1,0:T(8,128)S(1)} collective-permute-done((f32[4,128,256]{2,1,0:T(8,128)S(1)}, f32[4,128,256]{2,1,0:T(8,128)S(1)}, u32[]{:S(2)}, u32[]{:S(2)}) %collective-permute-start.7) | collective-permute-done | bytes 524320 | tf_op jit(solution)/shard_map/ppermute | solution.py:429
  43.9 0.0 collective-permute-done.9.c_mate_ref
  43.9 0.0 copy-done.5
  43.9 0.0 copy-done.6
  43.9 0.0 copy-done.7
  43.9 15.5 %shard_map.109 = (f32[32,4096]{1,0:T(8,128)}, f32[2,4096]{1,0:T(2,128)S(1)}) custom-call(s32[16]{0:T(128)S(1)} %copy-done.7, s32[1]{0:T(128)} %bitcast.part_ref, f32[4,128,256]{2,1,0:T(8,128)S(1)} %pad_maximum_fusion.1.a_own_ref, f32[4,128,256]{2,1,0:T(8,128)S(1)} %collective-permute-done.7.a_mate_ref, ...), custom_call_target="tpu_custom_call" | custom-call | flops 10000000000 | bytes 10000000 | tf_op jit(solution)/shard_map/pallas_call | solution.py:413
  59.5 0.0 collective-permute-start.12
  59.5 0.3 collective-permute-start.11
  59.8 4.0 %collective-permute-start.10 = (f32[2,4096]{1,0:T(2,128)S(1)}, f32[2,4096]{1,0:T(2,128)S(1)}, u32[]{:S(2)}, u32[]{:S(2)}) collective-permute-start(f32[2,4096]{1,0:T(2,128)S(1)} %get-tuple-element.41), channel_id=1, source_target_pairs={{0,1},{1,0},{2,3},{3,2},{4,5},{5,4},{6,7},{7,6},{8,9},{9,8},{10,11... | collective-permute-start | bytes 98312 | tf_op jit(solution)/shard_map/ppermute | solution.py:429
  63.9 1.6 %collective-permute-done.12 = f32[2,4096]{1,0:T(2,128)S(1)} collective-permute-done((f32[2,4096]{1,0:T(2,128)S(1)}, f32[2,4096]{1,0:T(2,128)S(1)}, u32[]{:S(2)}, u32[]{:S(2)}) %collective-permute-start.12) | collective-permute-done | bytes 32800 | tf_op jit(solution)/shard_map/ppermute | solution.py:429
  65.5 0.0 collective-permute-done.11
  65.5 0.3 collective-permute-done.10
  65.8 0.6 add_add_fusion
  (5 shorter events, 0.1 us)
Async XLA Ops:
  0.6 11.4 %collective-permute-start = (f32[32,2048]{1,0:T(8,128)}, f32[32,2048]{1,0:T(8,128)S(1)}, u32[]{:S(2)}, u32[]{:S(2)}) collective-permute-start(f32[32,2048]{1,0:T(8,128)} %param.10), channel_id=1, source_target_pairs={{1,0},{2,1},{3,2},{5,4},{6,5},{7,6},{9,8},{10,9},{11,10},{13,12},{... | collective-permute-start | bytes 786440 | tf_op jit(solution)/shard_map/ppermute | solution.py:561
  3.0 16.4 %copy-start.8 = (f32[32,2048]{1,0:T(8,128)S(1)}, f32[32,2048]{1,0:T(8,128)}, u32[]{:S(2)}) copy-start(f32[32,2048]{1,0:T(8,128)} %param.10) | copy-start | bytes 786436
  3.0 16.4 %copy-start.1 = (f32[4096]{0:T(1024)S(1)}, f32[4096]{0:T(1024)}, u32[]{:S(2)}) copy-start(f32[4096]{0:T(1024)} %param.12) | copy-start | bytes 49156
  3.0 16.4 %copy-start.2 = (f32[4096]{0:T(1024)S(1)}, f32[4096]{0:T(1024)}, u32[]{:S(2)}) copy-start(f32[4096]{0:T(1024)} %param.13) | copy-start | bytes 49156
  7.4 12.1 %copy-start = (f32[32,4096]{1,0:T(8,128)S(1)}, f32[32,4096]{1,0:T(8,128)}, u32[]{:S(2)}) copy-start(f32[32,4096]{1,0:T(8,128)} %inflow_ref) | copy-start | bytes 1572868
  12.1 12.5 %collective-permute-start.3 = (f32[32,2048]{1,0:T(8,128)S(1)}, f32[32,2048]{1,0:T(8,128)S(1)}, u32[]{:S(2)}, u32[]{:S(2)}) collective-permute-start(f32[32,2048]{1,0:T(8,128)S(1)} %collective-permute-done), channel_id=1, source_target_pairs={{1,0},{2,1},{5,4},{6,5},{9,8},{10,9},{13,12},{14,13},{17,16},{18,1... | collective-permute-start | bytes 786440 | tf_op jit(solution)/shard_map/ppermute | solution.py:563
  13.4 14.6 %collective-permute-start.2 = (f32[32,2048]{1,0:T(8,128)S(1)}, f32[32,2048]{1,0:T(8,128)S(1)}, u32[]{:S(2)}, u32[]{:S(2)}) collective-permute-start(f32[32,2048]{1,0:T(8,128)S(1)} %collective-permute-done), channel_id=1, source_target_pairs={{2,0},{6,4},{10,8},{14,12},{18,16},{22,20},{26,24},{30,28}} | collective-permute-start | bytes 786440 | tf_op jit(solution)/shard_map/ppermute | solution.py:564
  15.6 0.7 %copy-start.4 = (f32[8,256]{1,0:T(8,128)S(1)}, f32[8,256]{1,0:T(8,128)}, u32[]{:S(2)}) copy-start(f32[8,256]{1,0:T(8,128)} %get-tuple-element.25.ends_ref) | copy-start | bytes 24580
  17.6 5.2 %collective-permute-start.1 = (f32[1,136,256]{2,1,0:T(8,128)S(1)}, f32[1,136,256]{2,1,0:T(8,128)S(1)}, u32[]{:S(2)}, u32[]{:S(2)}) collective-permute-start(f32[1,136,256]{2,1,0:T(8,128)S(1)} %bitcast.12), channel_id=1, source_target_pairs={{0,8},{4,12},{8,0},{12,4},{16,24},{20,28},{24,16},{28,20},{1,9},{5... | collective-permute-start | bytes 417800 | tf_op jit(solution)/shard_map/ppermute | solution.py:429
  22.9 18.2 %collective-permute-start.8 = (f32[2,136,256]{2,1,0:T(8,128)S(1)}, f32[2,136,256]{2,1,0:T(8,128)S(1)}, u32[]{:S(2)}, u32[]{:S(2)}) collective-permute-start(f32[2,136,256]{2,1,0:T(8,128)S(1)} %pad_maximum_fusion.2), channel_id=1, source_target_pairs={{0,16},{4,20},{8,24},{12,28},{16,0},{20,4},{24,8},{28,12},{1,17},{... | collective-permute-start | bytes 835592 | tf_op jit(solution)/shard_map/ppermute | solution.py:429
  24.5 11.1 %copy-start.3 = (s32[2048]{0:T(1024)S(1)}, s32[2048]{0:T(1024)}, u32[]{:S(2)}) copy-start(s32[2048]{0:T(1024)} %param.11) | copy-start | bytes 24580
  32.1 9.2 %collective-permute-start.6 = (f32[128,256]{1,0:T(8,128)S(1)}, f32[128,256]{1,0:T(8,128)S(1)}, u32[]{:S(2)}, u32[]{:S(2)}) collective-permute-start(f32[128,256]{1,0:T(8,128)S(1)} %shard_map.107), channel_id=1, source_target_pairs={{0,24},{4,28},{8,16},{12,20},{16,8},{20,12},{24,0},{28,4},{1,25},{... | collective-permute-start | bytes 393224 | tf_op jit(solution)/shard_map/ppermute | solution.py:429
  34.6 6.7 %collective-permute-start.5 = (f32[128,256]{1,0:T(8,128)S(1)}, f32[128,256]{1,0:T(8,128)S(1)}, u32[]{:S(2)}, u32[]{:S(2)}) collective-permute-start(f32[128,256]{1,0:T(8,128)S(1)} %shard_map.107), channel_id=1, source_target_pairs={{0,16},{4,20},{8,24},{12,28},{16,0},{20,4},{24,8},{28,12},{1,17},{... | collective-permute-start | bytes 393224 | tf_op jit(solution)/shard_map/ppermute | solution.py:429
  35.1 6.2 %collective-permute-start.4 = (f32[128,256]{1,0:T(8,128)S(1)}, f32[128,256]{1,0:T(8,128)S(1)}, u32[]{:S(2)}, u32[]{:S(2)}) collective-permute-start(f32[128,256]{1,0:T(8,128)S(1)} %shard_map.107), channel_id=1, source_target_pairs={{0,8},{4,12},{8,0},{12,4},{16,24},{20,28},{24,16},{28,20},{1,9},{5... | collective-permute-start | bytes 393224 | tf_op jit(solution)/shard_map/ppermute | solution.py:429
  35.6 8.3 %copy-start.5 = (s32[4096]{0:T(1024)S(1)}, s32[4096]{0:T(1024)}, u32[]{:S(2)}) copy-start(s32[4096]{0:T(1024)} %param.15) | copy-start | bytes 49156
  35.6 8.3 %copy-start.6 = (s32[4096]{0:T(1024)S(1)}, s32[4096]{0:T(1024)}, u32[]{:S(2)}) copy-start(s32[4096]{0:T(1024)} %param.16) | copy-start | bytes 49156
  35.6 8.3 %copy-start.7 = (s32[16]{0:T(128)S(1)}, s32[16]{0:T(128)}, u32[]{:S(2)}) copy-start(s32[16]{0:T(128)} %level_ref.3) | copy-start | bytes 196
  41.2 2.8 %collective-permute-start.9 = (f32[4,136,256]{2,1,0:T(8,128)S(1)}, f32[4,136,256]{2,1,0:T(8,128)S(1)}, u32[]{:S(2)}, u32[]{:S(2)}) collective-permute-start(f32[4,136,256]{2,1,0:T(8,128)S(1)} %constant_dynamic-update-slice_fusion.c_own_ref), channel_id=1, source_target_pairs={{0,4},{4,0},{8,12},{12,8},{16,20},{20,16},{24,28},{28,24},{1,5},{5... | collective-permute-start | bytes 1671176 | tf_op jit(solution)/shard_map/ppermute | solution.py:429
  41.3 2.6 %collective-permute-start.7 = (f32[4,128,256]{2,1,0:T(8,128)S(1)}, f32[4,128,256]{2,1,0:T(8,128)S(1)}, u32[]{:S(2)}, u32[]{:S(2)}) collective-permute-start(f32[4,128,256]{2,1,0:T(8,128)S(1)} %pad_maximum_fusion.1.a_own_ref), channel_id=1, source_target_pairs={{0,4},{4,0},{8,12},{12,8},{16,20},{20,16},{24,28},{28,24},{1,5},{5... | collective-permute-start | bytes 1572872 | tf_op jit(solution)/shard_map/ppermute | solution.py:429
  59.5 6.0 %collective-permute-start.12 = (f32[2,4096]{1,0:T(2,128)S(1)}, f32[2,4096]{1,0:T(2,128)S(1)}, u32[]{:S(2)}, u32[]{:S(2)}) collective-permute-start(f32[2,4096]{1,0:T(2,128)S(1)} %get-tuple-element.41), channel_id=1, source_target_pairs={{0,3},{1,2},{2,1},{3,0},{4,7},{5,6},{6,5},{7,4},{8,11},{9,10},{10,... | collective-permute-start | bytes 98312 | tf_op jit(solution)/shard_map/ppermute | solution.py:429
  59.5 6.0 %collective-permute-start.11 = (f32[2,4096]{1,0:T(2,128)S(1)}, f32[2,4096]{1,0:T(2,128)S(1)}, u32[]{:S(2)}, u32[]{:S(2)}) collective-permute-start(f32[2,4096]{1,0:T(2,128)S(1)} %get-tuple-element.41), channel_id=1, source_target_pairs={{0,2},{1,3},{2,0},{3,1},{4,6},{5,7},{6,4},{7,5},{8,10},{9,11},{10,... | collective-permute-start | bytes 98312 | tf_op jit(solution)/shard_map/ppermute | solution.py:429
  59.8 6.0 %collective-permute-start.10 = (f32[2,4096]{1,0:T(2,128)S(1)}, f32[2,4096]{1,0:T(2,128)S(1)}, u32[]{:S(2)}, u32[]{:S(2)}) collective-permute-start(f32[2,4096]{1,0:T(2,128)S(1)} %get-tuple-element.41), channel_id=1, source_target_pairs={{0,1},{1,0},{2,3},{3,2},{4,5},{5,4},{6,7},{7,6},{8,9},{9,8},{10,11... | collective-permute-start | bytes 98312 | tf_op jit(solution)/shard_map/ppermute | solution.py:429
